TPU v7x, 32 devices: a whole 2x2x4 slice. The times are simulated.
32 devices in a mesh: dp: 8 (over y, x, core), tensor: 4 (over z).
Axes of the slice: x: 2, y: 2, z: 4, core: 2. Of those that a mesh axis runs over, the one named last changes fastest.
Arguments:
- tokens_in: bfloat16 [12288, 1088], P(('dp', 'tensor')), may hold values from -6 to 6
- ln1_gain: bfloat16 [1088], replicated, may hold values from 0.5 to 1.5
- ln1_bias: bfloat16 [1088], replicated, may hold values from -3 to 3
- w_qkv: bfloat16 [3, 1088, 1088], P(None, 'tensor'), may hold values from -0.1875 to 0.1875
- b_qv: bfloat16 [2, 1088], replicated, may hold values from -4 to 4
- w_out: bfloat16 [1088, 1088], P('tensor'), may hold values from -0.75 to 0.75
- b_out: bfloat16 [1088], replicated, may hold values from -3 to 3
- ln2_gain: bfloat16 [1088], replicated, may hold values from 0.5 to 1.5
- ln2_bias: bfloat16 [1088], replicated, may hold values from -3 to 3
- w_up: bfloat16 [1088, 4352], P(None, 'tensor'), may hold values from -0.1875 to 0.1875
- b_up: bfloat16 [4352], P('tensor'), may hold values from -4 to 4
- w_down: bfloat16 [4352, 1088], P('tensor'), may hold values from -0.09375 to 0.09375
- b_down: bfloat16 [1088], replicated, may hold values from -3 to 3
- seq_lengths: int32 [6], replicated, may hold values from 1 to 4096, 12288 in all
- cotangent: bfloat16 [12288, 1088], P(('dp', 'tensor')), may hold values from -6 to 6
Outputs:
- block_out: bfloat16 [12288, 1088], P(('dp', 'tensor'))
- grad_input: float32 [12288, 1088], P(('dp', 'tensor'))
- grad_ln1_gain: float32 [1088], replicated
- grad_ln1_bias: float32 [1088], replicated
- grad_qkv: float32 [3, 1088, 1088], P(None, 'tensor', 'dp')
- grad_qv_bias: float32 [2, 1088], replicated
- grad_out: float32 [1088, 1088], P('tensor', 'dp')
- grad_out_bias: float32 [1088], replicated
- grad_ln2_gain: float32 [1088], replicated
- grad_ln2_bias: float32 [1088], replicated
- grad_up: float32 [1088, 4352], P('dp', 'tensor')
- grad_up_bias: float32 [4352], P('tensor')
- grad_down: float32 [4352, 1088], P('tensor', 'dp')
- grad_down_bias: float32 [1088], replicated
Inputs may be any that keep to these rules, and one draw needn't show every extreme that they name: `seq_lengths`: the sequences lie one after another in token order; the lengths sum to 12288 and the longest is exactly 4096.
All inputs are finite; a program needn't handle non-finite values.
Results may differ from a plain program's by a relative error of at most 0.02.
Values may be sent and summed in bfloat16 or wider, within the bound.
No kernel may reach another device: no remote copies, remote signals or barrier semaphores. Data moves between devices by JAX's collectives and lax.ppermute only.
A program may use at most 192 MiB of HBM per device.

v0:
```python
import jax
import jax.numpy as jnp
from jax import lax
from jax.sharding import PartitionSpec as P

HEADS = 17
HEAD_DIM = 64
REACH = 11


norm_eps = 1e-05
score_scale = 0.125
masked_score = -1e30


def shifted(value, axis, steps):
    count = lax.axis_size(axis)
    first, last = (max(0, -steps), min(count, count - steps))
    return lax.ppermute(value, axis, [(source, source + steps) for source in range(first, last)])


def segment_of(positions, seq_ends):
    return jnp.sum((positions[:, None] >= seq_ends[None, :]).astype(jnp.int32), axis=1)


def widen(token_rows):
    return lax.all_gather(token_rows, "tensor", axis=0, tiled=True)


def narrow(partial_sum):
    return lax.psum_scatter(
        partial_sum.astype(jnp.bfloat16), "tensor", scatter_dimension=0, tiled=True
    ).astype(jnp.float32)


def to_tokens(feature_rows):
    return lax.all_to_all(feature_rows, "tensor", split_axis=0, concat_axis=2, tiled=True)


def norm_forward(values, gain_vec, bias_vec):
    mean_row = jnp.mean(values, axis=1, keepdims=True)
    centered = values - mean_row
    variance = jnp.mean(centered * centered, axis=1, keepdims=True)
    inv_std = lax.rsqrt(variance + norm_eps)
    normed = centered * inv_std
    return (normed, inv_std, normed * gain_vec + bias_vec)


def norm_backward(grad_normed, normed, inv_std, gain_vec):
    scaled = grad_normed * gain_vec
    plain_mean = jnp.mean(scaled, axis=1, keepdims=True)
    cross_mean = jnp.mean(scaled * normed, axis=1, keepdims=True)
    grad_values = inv_std * (scaled - plain_mean - normed * cross_mean)
    return (grad_values, jnp.sum(grad_normed * normed, axis=0), jnp.sum(grad_normed, axis=0))


def head_view(flat_rows):
    return flat_rows.reshape(flat_rows.shape[0], HEADS, HEAD_DIM)


def block_scores(queries, key_heads):
    return (
        jnp.einsum("qhd,khd->hqk", queries, key_heads, preferred_element_type=jnp.float32)
        * score_scale
    )


def key_layout(offset, flat_index, row_count, query_seg, seq_ends):
    key_pos = (flat_index - offset) * row_count + jnp.arange(row_count, dtype=jnp.int32)
    key_seg = segment_of(key_pos, seq_ends)
    is_live = (offset == 0) | (flat_index >= offset) & (key_seg[row_count - 1] == query_seg[0])
    return (key_pos, key_seg, is_live)


def allowed_pairs(query_pos, query_seg, key_pos, key_seg):
    return (
        (query_seg[:, None] == key_seg[None, :])
        & (key_pos[None, :] <= query_pos[:, None])
        & (key_pos[None, :] >= 0)
    )[None]


def attention_forward(qkv_rows, flat_index, seq_ends):
    row_count = qkv_rows.shape[0]
    query_pos = flat_index * row_count + jnp.arange(row_count, dtype=jnp.int32)
    query_seg = segment_of(query_pos, seq_ends)
    queries = head_view(qkv_rows[:, 0])
    local_pairs = qkv_rows[:, 1:]

    def carry_keys(offset, carried):
        moving, stored = carried
        moving = shifted(moving, ("dp", "tensor"), 1)
        return (moving, lax.dynamic_update_index_in_dim(stored, moving, offset, 0))

    stored = jnp.zeros((REACH + 1,) + local_pairs.shape, local_pairs.dtype).at[0].set(local_pairs)
    stored = lax.fori_loop(1, REACH + 1, carry_keys, (local_pairs, stored))[1]
    heads_shape = (HEADS, row_count)

    def stats_step(offset, carried):
        key_pos, key_seg, is_live = key_layout(offset, flat_index, row_count, query_seg, seq_ends)

        def update(running):
            running_max, running_sum = running
            allowed = allowed_pairs(query_pos, query_seg, key_pos, key_seg)
            scores = jnp.where(
                allowed, block_scores(queries, head_view(stored[offset, :, 0])), masked_score
            )
            new_max = jnp.maximum(running_max, jnp.max(scores, axis=2))
            new_sum = running_sum * jnp.exp(running_max - new_max) + jnp.sum(
                jnp.exp(scores - new_max[:, :, None]), axis=2
            )
            return (new_max, new_sum)

        return lax.cond(is_live, update, lambda running: running, carried)

    start_max = jnp.full(heads_shape, masked_score, jnp.float32)
    final_max, final_sum = lax.fori_loop(
        0, REACH + 1, stats_step, (start_max, jnp.zeros(heads_shape, jnp.float32))
    )
    log_total = final_max + jnp.log(final_sum)

    def value_step(offset, summed):
        key_pos, key_seg, is_live = key_layout(offset, flat_index, row_count, query_seg, seq_ends)

        def add_values(current):
            allowed = allowed_pairs(query_pos, query_seg, key_pos, key_seg)
            weights = jnp.where(
                allowed,
                jnp.exp(
                    block_scores(queries, head_view(stored[offset, :, 0])) - log_total[:, :, None]
                ),
                0.0,
            )
            return current + jnp.einsum(
                "hqk,khd->qhd",
                weights.astype(jnp.bfloat16),
                head_view(stored[offset, :, 1]),
                preferred_element_type=jnp.float32,
            )

        return lax.cond(is_live, add_values, lambda current: current, summed)

    attended = lax.fori_loop(
        0, REACH + 1, value_step, jnp.zeros((row_count, HEADS, HEAD_DIM), jnp.float32)
    )
    return (attended.reshape(row_count, HEADS * HEAD_DIM), log_total, stored)


def attention_backward(grad_attended, attended, log_total, qkv_rows, stored, flat_index, seq_ends):
    row_count = qkv_rows.shape[0]
    query_pos = flat_index * row_count + jnp.arange(row_count, dtype=jnp.int32)
    query_seg = segment_of(query_pos, seq_ends)
    queries = head_view(qkv_rows[:, 0])
    grad_heads = head_view(grad_attended)
    row_inner = jnp.sum(grad_heads.astype(jnp.float32) * head_view(attended), axis=2).T
    zero_query = jnp.zeros((row_count, HEADS * HEAD_DIM), jnp.float32)
    zero_pairs = jnp.zeros((row_count, 2, HEADS * HEAD_DIM), jnp.float32)

    def block_grads(offset):
        key_pos, key_seg, is_live = key_layout(offset, flat_index, row_count, query_seg, seq_ends)
        key_heads = head_view(stored[offset, :, 0])
        value_heads = head_view(stored[offset, :, 1])
        allowed = allowed_pairs(query_pos, query_seg, key_pos, key_seg)
        weights = jnp.where(
            allowed, jnp.exp(block_scores(queries, key_heads) - log_total[:, :, None]), 0.0
        )
        grad_weights = jnp.einsum(
            "qhd,khd->hqk", grad_heads, value_heads, preferred_element_type=jnp.float32
        )
        grad_scores = (weights * (grad_weights - row_inner[:, :, None])).astype(jnp.bfloat16)
        grad_query = (
            jnp.einsum("hqk,khd->qhd", grad_scores, key_heads, preferred_element_type=jnp.float32)
            * score_scale
        )
        grad_key = (
            jnp.einsum("hqk,qhd->khd", grad_scores, queries, preferred_element_type=jnp.float32)
            * score_scale
        )
        grad_value = jnp.einsum(
            "hqk,qhd->khd",
            weights.astype(jnp.bfloat16),
            grad_heads,
            preferred_element_type=jnp.float32,
        )
        pair_grads = jnp.stack(
            (grad_key.reshape(row_count, -1), grad_value.reshape(row_count, -1)), axis=1
        )
        return (grad_query.reshape(row_count, -1), pair_grads)

    def far_step(counter, carried):
        grad_query, moving = carried
        offset = REACH - counter
        is_live = key_layout(offset, flat_index, row_count, query_seg, seq_ends)[2]
        add_query, add_pairs = lax.cond(
            is_live, block_grads, lambda unused: (zero_query, zero_pairs), offset
        )
        moving = shifted((moving + add_pairs).astype(jnp.bfloat16), ("dp", "tensor"), -1).astype(
            jnp.float32
        )
        return (grad_query + add_query, moving)

    grad_query, returned = lax.fori_loop(0, REACH, far_step, (zero_query, zero_pairs))
    own_query, own_pairs = block_grads(0)
    grad_pairs = returned + own_pairs
    return jnp.concatenate(((grad_query + own_query)[:, None], grad_pairs), axis=1).astype(
        jnp.bfloat16
    )


def local(
    tokens_in,
    ln1_gain,
    ln1_bias,
    w_qkv,
    b_qv,
    w_out,
    b_out,
    ln2_gain,
    ln2_bias,
    w_up,
    b_up,
    w_down,
    b_down,
    seq_lengths,
    cotangent,
):
    tensor_size = lax.axis_size("tensor")
    tensor_index = lax.axis_index("tensor")
    flat_index = lax.axis_index("dp") * tensor_size + tensor_index
    slab = w_qkv.shape[1]
    unit_slab = w_up.shape[1]
    seq_ends = jnp.cumsum(seq_lengths)
    gain_one = ln1_gain.astype(jnp.float32)
    shift_one = ln1_bias.astype(jnp.float32)
    gain_two = ln2_gain.astype(jnp.float32)
    shift_two = ln2_bias.astype(jnp.float32)
    out_bias = b_out.astype(jnp.float32)
    stream = tokens_in.astype(jnp.float32)
    normed_one, inv_one, pre_one = norm_forward(stream, gain_one, shift_one)
    wide_one = widen(pre_one.astype(jnp.bfloat16))
    bias_full = jnp.stack((b_qv[0], jnp.zeros_like(b_qv[0]), b_qv[1])).astype(jnp.float32)
    qkv_bias = lax.dynamic_slice_in_dim(bias_full, tensor_index * slab, slab, 1)
    projected = (
        jnp.einsum("td,ced->tce", wide_one, w_qkv, preferred_element_type=jnp.float32)
        + qkv_bias[None]
    )
    qkv_rows = to_tokens(projected.astype(jnp.bfloat16))
    attended, log_total, stored = attention_forward(qkv_rows, flat_index, seq_ends)
    attended_low = attended.astype(jnp.bfloat16)
    attended_cols = lax.all_to_all(
        attended_low[:, None], "tensor", split_axis=2, concat_axis=0, tiled=True
    )[:, 0]
    branch = narrow(jnp.dot(attended_cols, w_out, preferred_element_type=jnp.float32))
    stream_one = stream + branch + out_bias
    normed_two, inv_two, pre_two = norm_forward(stream_one, gain_two, shift_two)
    wide_two = widen(pre_two.astype(jnp.bfloat16))
    hidden_pre = jnp.dot(wide_two, w_up, preferred_element_type=jnp.float32) + b_up.astype(
        jnp.float32
    )
    gelu_out, gelu_pull = jax.vjp(
        lambda hidden_in: jax.nn.gelu(hidden_in, approximate=True), hidden_pre
    )
    activated = gelu_out.astype(jnp.bfloat16)
    down_sum = narrow(jnp.dot(activated, w_down, preferred_element_type=jnp.float32))
    block_out = (stream_one + down_sum + b_down.astype(jnp.float32)).astype(jnp.bfloat16)
    contract_rows = (((0,), (0,)), ((), ()))
    contract_cols = (((1,), (1,)), ((), ()))
    grad_two = cotangent.astype(jnp.float32)
    grad_down_bias = jnp.sum(grad_two, axis=0)
    wide_grad = widen(cotangent)
    grad_act = lax.dot_general(wide_grad, w_down, contract_cols, preferred_element_type=jnp.float32)
    grad_down = lax.dot_general(
        activated, wide_grad, contract_rows, preferred_element_type=jnp.float32
    )
    grad_hidden = gelu_pull(grad_act)[0].astype(jnp.bfloat16)
    grad_up_part = jnp.sum(grad_hidden.astype(jnp.float32), axis=0)
    grad_up = lax.dot_general(
        wide_two, grad_hidden, contract_rows, preferred_element_type=jnp.float32
    )
    grad_normed_two = narrow(
        lax.dot_general(grad_hidden, w_up, contract_cols, preferred_element_type=jnp.float32)
    )
    grad_res_two, grad_gain_two, grad_shift_two = norm_backward(
        grad_normed_two, normed_two, inv_two, gain_two
    )
    grad_stream_one = grad_two + grad_res_two
    grad_branch = grad_stream_one.astype(jnp.bfloat16)
    grad_out_bias = jnp.sum(grad_branch.astype(jnp.float32), axis=0)
    wide_branch = lax.all_gather(grad_branch, "tensor", axis=0, tiled=True)
    grad_cols = lax.dot_general(
        wide_branch, w_out, contract_cols, preferred_element_type=jnp.float32
    )
    grad_attended = to_tokens(grad_cols.astype(jnp.bfloat16)[:, None])[:, 0]
    grad_out = lax.dot_general(
        attended_cols, wide_branch, contract_rows, preferred_element_type=jnp.float32
    )
    grad_qkv_rows = attention_backward(
        grad_attended, attended, log_total, qkv_rows, stored, flat_index, seq_ends
    )
    grad_qv_bias = jnp.stack(
        (
            jnp.sum(grad_qkv_rows[:, 0].astype(jnp.float32), axis=0),
            jnp.sum(grad_qkv_rows[:, 2].astype(jnp.float32), axis=0),
        )
    )
    grad_projected = lax.all_to_all(
        grad_qkv_rows, "tensor", split_axis=2, concat_axis=0, tiled=True
    )
    grad_qkv = jnp.einsum(
        "tce,td->ced", grad_projected, wide_one, preferred_element_type=jnp.float32
    )
    grad_normed_one = narrow(
        jnp.einsum("tce,ced->td", grad_projected, w_qkv, preferred_element_type=jnp.float32)
    )
    grad_res_one, grad_gain_one, grad_shift_one = norm_backward(
        grad_normed_one, normed_one, inv_one, gain_one
    )
    grad_input = grad_stream_one + grad_res_one
    grad_qkv, grad_out, grad_up, grad_down = (
        lax.psum_scatter(
            grad_qkv.astype(jnp.bfloat16), "dp", scatter_dimension=2, tiled=True
        ).astype(jnp.float32),
        lax.psum_scatter(
            grad_out.astype(jnp.bfloat16), "dp", scatter_dimension=1, tiled=True
        ).astype(jnp.float32),
        lax.psum_scatter(
            grad_up.astype(jnp.bfloat16), "dp", scatter_dimension=0, tiled=True
        ).astype(jnp.float32),
        lax.psum_scatter(
            grad_down.astype(jnp.bfloat16), "dp", scatter_dimension=1, tiled=True
        ).astype(jnp.float32),
    )
    up_full = lax.dynamic_update_slice_in_dim(
        jnp.zeros((unit_slab * tensor_size,), jnp.float32),
        grad_up_part,
        tensor_index * unit_slab,
        0,
    )
    small = lax.psum(
        (
            grad_gain_one,
            grad_shift_one,
            grad_qv_bias,
            grad_out_bias,
            grad_gain_two,
            grad_shift_two,
            up_full,
            grad_down_bias,
        ),
        ("dp", "tensor"),
    )
    grad_up_bias = lax.dynamic_slice_in_dim(small[6], tensor_index * unit_slab, unit_slab, 0)
    return (
        block_out,
        grad_input,
        small[0],
        small[1],
        grad_qkv,
        small[2],
        grad_out,
        small[3],
        small[4],
        small[5],
        grad_up,
        grad_up_bias,
        grad_down,
        small[7],
    )


def solution(mesh):
    in_specs = (
        P(("dp", "tensor"), None),
        P(),
        P(),
        P(None, "tensor", None),
        P(),
        P("tensor", None),
        P(),
        P(),
        P(),
        P(None, "tensor"),
        P("tensor"),
        P("tensor", None),
        P(),
        P(),
        P(("dp", "tensor"), None),
    )
    out_specs = (
        P(("dp", "tensor"), None),
        P(("dp", "tensor"), None),
        P(),
        P(),
        P(None, "tensor", "dp"),
        P(),
        P("tensor", "dp"),
        P(),
        P(),
        P(),
        P("dp", "tensor"),
        P("tensor"),
        P("tensor", "dp"),
        P(),
    )
    return jax.shard_map(local, mesh=mesh, in_specs=in_specs, out_specs=out_specs, check_vma=False)
```

profile of v0, /device:TPU:0, one launch (start us, length us, event | category | flops | bytes accessed | tf_op | source)
XLA Modules:
  0.0 2366.9 jit_solution(14839702922099974165)
XLA Ops:
  14.2 69.3 %all-gather.5.cloned.1.call-done = bf16[1536,1088]{0,1:T(8,128)(2,1)} async-done(((bf16[384,1088]{0,1:T(8,128)(2,1)}), bf16[1536,1088]{0,1:T(8,128)(2,1)}) %all-gather.5.cloned.1.call-update) | async-done | bytes 3342352 | tf_op jit(solution)/shard_map/all_gather | solution.py:27
  83.5 7.4 add_convert_fusion
  90.9 7.6 copy.104
  104.3 104.1 %all-to-all-done = bf16[1536,3,272]{2,1,0:T(4,128)(2,1)} async-done(((bf16[1536,3,272]{2,1,0:T(4,128)(2,1)}), bf16[1536,3,272]{2,1,0:T(4,128)(2,1)}, u32[]{:S(2)}, u32[]{:S(2)}) %all-to-all-start) | async-done | bytes 2506784 | tf_op jit(solution)/shard_map/all_to_all | solution.py:37
  208.3 7.7 copy.106
  220.2 7.2 scatter.4
  227.4 499.6 %while.65 = (s32[]{:T(128)}, bf16[384,2,1088]{0,2,1:T(8,128)(2,1)}, bf16[12,384,2,1088]{1,3,2,0:T(8,128)(2,1)}, s32[]{:T(128)}, s32[]{:T(128)}, /*index=5*/s32[]{:T(128)}) while((s32[]{:T(128)}, bf16[384,2,1088]{0,2,1:T(8,128)(2,1)}, bf16[12,384,2,1088]{1,3,2,0:T(8,128)(2,1)}, s32[]{:T(128)}, s32[]{:T(128)}, /*index=5*/s32[]{:T(128)}) %tuple.191), condition=%wide.region_5.6_spmd, body=%wide.region_4.5_spmd.sunk | while | flops 5 | bytes 13369491 | solution.py:96
  229.9 35.0 %collective-permute-done = bf16[384,2,1088]{0,2,1:T(8,128)(2,1)} collective-permute-done((bf16[384,2,1088]{0,2,1:T(8,128)(2,1)}, bf16[384,2,1088]{0,2,1:T(8,128)(2,1)}, u32[]{:S(2)}, u32[]{:S(2)}) %collective-permute-start) | collective-permute-done | bytes 1671200 | tf_op jit(solution)/shard_map/while/body/eval_jaxpr/ppermute | solution.py:19
  276.1 35.5 %collective-permute-done = bf16[384,2,1088]{0,2,1:T(8,128)(2,1)} collective-permute-done((bf16[384,2,1088]{0,2,1:T(8,128)(2,1)}, bf16[384,2,1088]{0,2,1:T(8,128)(2,1)}, u32[]{:S(2)}, u32[]{:S(2)}) %collective-permute-start) | collective-permute-done | bytes 1671200 | tf_op jit(solution)/shard_map/while/body/eval_jaxpr/ppermute | solution.py:19
  322.8 34.7 %collective-permute-done = bf16[384,2,1088]{0,2,1:T(8,128)(2,1)} collective-permute-done((bf16[384,2,1088]{0,2,1:T(8,128)(2,1)}, bf16[384,2,1088]{0,2,1:T(8,128)(2,1)}, u32[]{:S(2)}, u32[]{:S(2)}) %collective-permute-start) | collective-permute-done | bytes 1671200 | tf_op jit(solution)/shard_map/while/body/eval_jaxpr/ppermute | solution.py:19
  368.7 33.8 %collective-permute-done = bf16[384,2,1088]{0,2,1:T(8,128)(2,1)} collective-permute-done((bf16[384,2,1088]{0,2,1:T(8,128)(2,1)}, bf16[384,2,1088]{0,2,1:T(8,128)(2,1)}, u32[]{:S(2)}, u32[]{:S(2)}) %collective-permute-start) | collective-permute-done | bytes 1671200 | tf_op jit(solution)/shard_map/while/body/eval_jaxpr/ppermute | solution.py:19
  413.7 33.2 %collective-permute-done = bf16[384,2,1088]{0,2,1:T(8,128)(2,1)} collective-permute-done((bf16[384,2,1088]{0,2,1:T(8,128)(2,1)}, bf16[384,2,1088]{0,2,1:T(8,128)(2,1)}, u32[]{:S(2)}, u32[]{:S(2)}) %collective-permute-start) | collective-permute-done | bytes 1671200 | tf_op jit(solution)/shard_map/while/body/eval_jaxpr/ppermute | solution.py:19
  458.2 35.4 %collective-permute-done = bf16[384,2,1088]{0,2,1:T(8,128)(2,1)} collective-permute-done((bf16[384,2,1088]{0,2,1:T(8,128)(2,1)}, bf16[384,2,1088]{0,2,1:T(8,128)(2,1)}, u32[]{:S(2)}, u32[]{:S(2)}) %collective-permute-start) | collective-permute-done | bytes 1671200 | tf_op jit(solution)/shard_map/while/body/eval_jaxpr/ppermute | solution.py:19
  504.7 34.6 %collective-permute-done = bf16[384,2,1088]{0,2,1:T(8,128)(2,1)} collective-permute-done((bf16[384,2,1088]{0,2,1:T(8,128)(2,1)}, bf16[384,2,1088]{0,2,1:T(8,128)(2,1)}, u32[]{:S(2)}, u32[]{:S(2)}) %collective-permute-start) | collective-permute-done | bytes 1671200 | tf_op jit(solution)/shard_map/while/body/eval_jaxpr/ppermute | solution.py:19
  550.5 34.1 %collective-permute-done = bf16[384,2,1088]{0,2,1:T(8,128)(2,1)} collective-permute-done((bf16[384,2,1088]{0,2,1:T(8,128)(2,1)}, bf16[384,2,1088]{0,2,1:T(8,128)(2,1)}, u32[]{:S(2)}, u32[]{:S(2)}) %collective-permute-start) | collective-permute-done | bytes 1671200 | tf_op jit(solution)/shard_map/while/body/eval_jaxpr/ppermute | solution.py:19
  595.7 33.2 %collective-permute-done = bf16[384,2,1088]{0,2,1:T(8,128)(2,1)} collective-permute-done((bf16[384,2,1088]{0,2,1:T(8,128)(2,1)}, bf16[384,2,1088]{0,2,1:T(8,128)(2,1)}, u32[]{:S(2)}, u32[]{:S(2)}) %collective-permute-start) | collective-permute-done | bytes 1671200 | tf_op jit(solution)/shard_map/while/body/eval_jaxpr/ppermute | solution.py:19
  640.1 35.5 %collective-permute-done = bf16[384,2,1088]{0,2,1:T(8,128)(2,1)} collective-permute-done((bf16[384,2,1088]{0,2,1:T(8,128)(2,1)}, bf16[384,2,1088]{0,2,1:T(8,128)(2,1)}, u32[]{:S(2)}, u32[]{:S(2)}) %collective-permute-start) | collective-permute-done | bytes 1671200 | tf_op jit(solution)/shard_map/while/body/eval_jaxpr/ppermute | solution.py:19
  686.7 34.7 %collective-permute-done = bf16[384,2,1088]{0,2,1:T(8,128)(2,1)} collective-permute-done((bf16[384,2,1088]{0,2,1:T(8,128)(2,1)}, bf16[384,2,1088]{0,2,1:T(8,128)(2,1)}, u32[]{:S(2)}, u32[]{:S(2)}) %collective-permute-start) | collective-permute-done | bytes 1671200 | tf_op jit(solution)/shard_map/while/body/eval_jaxpr/ppermute | solution.py:19
  727.0 36.0 %while.66 = (s32[]{:T(128)}, f32[17,384]{1,0:T(8,128)S(1)}, f32[17,384]{1,0:T(8,128)S(1)}, s32[]{:T(128)}, s32[6]{0:T(128)S(1)}, /*index=5*/s32[384]{0:T(512)S(1...) while((s32[]{:T(128)}, f32[17,384]{1,0:T(8,128)S(1)}, ...), condition=%wide.region_12.13_spmd.clone, body=%wide.region_6.12_spmd.clone.sunk | while | flops 339022464 | bytes 24197780 | solution.py:117
  764.4 39.7 %while.67 = (s32[]{:T(128)}, f32[384,17,64]{0,2,1:T(8,128)}, s32[]{:T(128)}, s32[6]{0:T(128)S(1)}, s32[384]{0:T(512)S(1)}, /*index=5*/bf16[12,384,2,1088]{1,3,2,...) while((s32[]{:T(128)}, f32[384,17,64]{0,2,1:T(8,128)}, ...), condition=%wide.region_17.18_spmd.clone, body=%wide.region_13.17_spmd.clone.sunk | while | flops 652771200 | bytes 9532021 | solution.py:143
  766.9 9.0 conditional.10
  770.0 6.0 bitcast_add_fusion
  805.7 9.5 copy.139
  815.6 9.1 reduce.4
  826.7 46.4 %all_to_all.66 = bf16[4,2,52224]{2,1,0:T(2,128)(2,1)} all-to-all(bf16[4,2,52224]{2,1,0:T(2,128)(2,1)} %reshape.519), channel_id=1, replica_groups=mesh['dp'=8,'tensor'=4] {'tensor'}, dimensions={0} | all-to-all | bytes 1671168 | tf_op jit(solution)/shard_map/all_to_all | solution.py:250
  890.1 133.9 %reduce-scatter.23.cloned.1.call-done = bf16[384,1088]{1,0:T(8,128)(2,1)} async-done(((bf16[1536,1088]{1,0:T(8,128)(2,1)}), bf16[384,1088]{1,0:T(8,128)(2,1)}) %reduce-scatter.23.cloned.1.call-update) | async-done | bytes 835600
  1031.5 61.0 %all-gather.9.cloned.1.call-done = bf16[1536,1088]{0,1:T(8,128)(2,1)} async-done(((bf16[384,1088]{0,1:T(8,128)(2,1)}), bf16[1536,1088]{0,1:T(8,128)(2,1)}) %all-gather.9.cloned.1.call-update) | async-done | bytes 3342352 | tf_op jit(solution)/shard_map/all_gather | solution.py:27
  1092.5 9.9 fusion.79
  1102.5 56.9 %all-gather.7.cloned.1.call-done = bf16[1536,1088]{0,1:T(8,128)(2,1)} async-done(((bf16[384,1088]{0,1:T(8,128)(2,1)}), bf16[1536,1088]{0,1:T(8,128)(2,1)}) %all-gather.7.cloned.1.call-update) | async-done | bytes 3342352 | tf_op jit(solution)/shard_map/all_gather | solution.py:27
  1159.4 14.6 convert_reduce_fusion.4
  1175.6 6.0 convolution_convert_fusion
  1187.3 65.2 %reduce-scatter.27.cloned.1.call-done = bf16[384,1088]{1,0:T(8,128)(2,1)} async-done(((bf16[1536,1088]{1,0:T(8,128)(2,1)}), bf16[384,1088]{1,0:T(8,128)(2,1)}) %reduce-scatter.27.cloned.1.call-update) | async-done | bytes 835600
  1260.4 9.9 convolution_convert_fusion.3
  1270.4 9.0 convolution_convert_fusion.4
  1282.2 45.0 %all-gather.11.cloned.1.call-done = bf16[1536,1088]{0,1:T(8,128)(2,1)} async-done(((bf16[384,1088]{0,1:T(8,128)(2,1)}), bf16[1536,1088]{0,1:T(8,128)(2,1)}) %all-gather.11.cloned.1.call-update) | async-done | bytes 3342352 | tf_op jit(solution)/shard_map/all_gather | solution.py:289
  1346.1 9.3 convolution_convert_fusion.1
  1355.4 6.0 copy.125
  1365.3 6.6 copy.110
  1375.9 5.9 fusion.34
  1381.9 6.9 multiply_convert_fusion
  1392.8 6.0 copy.113
  1398.8 6.0 copy.112
  1404.8 563.0 %while.68 = (s32[]{:T(128)}, f32[384,1088]{0,1:T(8,128)}, f32[384,2,1088]{0,2,1:T(8,128)}, s32[]{:T(128)}, s32[6]{0:T(128)S(1)}, /*index=5*/s32[384]{0:T(512)S(1...) while((s32[]{:T(128)}, f32[384,1088]{0,1:T(8,128)}, ...), condition=%wide.region_31.32_spmd.clone, body=%wide.region_26.0_spmd.clone.sunk | while | flops 1635842688 | bytes 101647712 | solution.py:202
  1414.7 79.5 %collective-permute-done.1 = bf16[384,2,1088]{0,2,1:T(8,128)(2,1)S(1)} collective-permute-done((bf16[384,2,1088]{0,2,1:T(8,128)(2,1)}, bf16[384,2,1088]{0,2,1:T(8,128)(2,1)S(1)}, u32[]{:S(2)}, u32[]{:S(2)}) %collective-permute-start.1) | collective-permute-done | bytes 1671200 | tf_op jit(solution)/shard_map/while/body/eval_jaxpr/ppermute | solution.py:19
  1508.3 34.7 %collective-permute-done.1 = bf16[384,2,1088]{0,2,1:T(8,128)(2,1)S(1)} collective-permute-done((bf16[384,2,1088]{0,2,1:T(8,128)(2,1)}, bf16[384,2,1088]{0,2,1:T(8,128)(2,1)S(1)}, u32[]{:S(2)}, u32[]{:S(2)}) %collective-permute-start.1) | collective-permute-done | bytes 1671200 | tf_op jit(solution)/shard_map/while/body/eval_jaxpr/ppermute | solution.py:19
  1557.1 31.7 %collective-permute-done.1 = bf16[384,2,1088]{0,2,1:T(8,128)(2,1)S(1)} collective-permute-done((bf16[384,2,1088]{0,2,1:T(8,128)(2,1)}, bf16[384,2,1088]{0,2,1:T(8,128)(2,1)S(1)}, u32[]{:S(2)}, u32[]{:S(2)}) %collective-permute-start.1) | collective-permute-done | bytes 1671200 | tf_op jit(solution)/shard_map/while/body/eval_jaxpr/ppermute | solution.py:19
  1602.9 32.2 %collective-permute-done.1 = bf16[384,2,1088]{0,2,1:T(8,128)(2,1)S(1)} collective-permute-done((bf16[384,2,1088]{0,2,1:T(8,128)(2,1)}, bf16[384,2,1088]{0,2,1:T(8,128)(2,1)S(1)}, u32[]{:S(2)}, u32[]{:S(2)}) %collective-permute-start.1) | collective-permute-done | bytes 1671200 | tf_op jit(solution)/shard_map/while/body/eval_jaxpr/ppermute | solution.py:19
  1649.2 42.9 %collective-permute-done.1 = bf16[384,2,1088]{0,2,1:T(8,128)(2,1)S(1)} collective-permute-done((bf16[384,2,1088]{0,2,1:T(8,128)(2,1)}, bf16[384,2,1088]{0,2,1:T(8,128)(2,1)S(1)}, u32[]{:S(2)}, u32[]{:S(2)}) %collective-permute-start.1) | collective-permute-done | bytes 1671200 | tf_op jit(solution)/shard_map/while/body/eval_jaxpr/ppermute | solution.py:19
  1706.2 36.3 %collective-permute-done.1 = bf16[384,2,1088]{0,2,1:T(8,128)(2,1)S(1)} collective-permute-done((bf16[384,2,1088]{0,2,1:T(8,128)(2,1)}, bf16[384,2,1088]{0,2,1:T(8,128)(2,1)S(1)}, u32[]{:S(2)}, u32[]{:S(2)}) %collective-permute-start.1) | collective-permute-done | bytes 1671200 | tf_op jit(solution)/shard_map/while/body/eval_jaxpr/ppermute | solution.py:19
  1756.6 35.5 %collective-permute-done.1 = bf16[384,2,1088]{0,2,1:T(8,128)(2,1)S(1)} collective-permute-done((bf16[384,2,1088]{0,2,1:T(8,128)(2,1)}, bf16[384,2,1088]{0,2,1:T(8,128)(2,1)S(1)}, u32[]{:S(2)}, u32[]{:S(2)}) %collective-permute-start.1) | collective-permute-done | bytes 1671200 | tf_op jit(solution)/shard_map/while/body/eval_jaxpr/ppermute | solution.py:19
  1806.2 34.6 %collective-permute-done.1 = bf16[384,2,1088]{0,2,1:T(8,128)(2,1)S(1)} collective-permute-done((bf16[384,2,1088]{0,2,1:T(8,128)(2,1)}, bf16[384,2,1088]{0,2,1:T(8,128)(2,1)S(1)}, u32[]{:S(2)}, u32[]{:S(2)}) %collective-permute-start.1) | collective-permute-done | bytes 1671200 | tf_op jit(solution)/shard_map/while/body/eval_jaxpr/ppermute | solution.py:19
  1854.9 24.2 %collective-permute-done.1 = bf16[384,2,1088]{0,2,1:T(8,128)(2,1)S(1)} collective-permute-done((bf16[384,2,1088]{0,2,1:T(8,128)(2,1)}, bf16[384,2,1088]{0,2,1:T(8,128)(2,1)S(1)}, u32[]{:S(2)}, u32[]{:S(2)}) %collective-permute-start.1) | collective-permute-done | bytes 1671200 | tf_op jit(solution)/shard_map/while/body/eval_jaxpr/ppermute | solution.py:19
  1893.2 19.0 collective-permute-done.1
  1926.2 39.6 %collective-permute-done.1 = bf16[384,2,1088]{0,2,1:T(8,128)(2,1)S(1)} collective-permute-done((bf16[384,2,1088]{0,2,1:T(8,128)(2,1)}, bf16[384,2,1088]{0,2,1:T(8,128)(2,1)S(1)}, u32[]{:S(2)}, u32[]{:S(2)}) %collective-permute-start.1) | collective-permute-done | bytes 1671200 | tf_op jit(solution)/shard_map/while/body/eval_jaxpr/ppermute | solution.py:19
  1970.1 16.0 copy.115
  1986.1 9.9 fusion.37
  2001.7 33.0 %all-to-all-start.3 = ((bf16[384,3,1088]{0,1,2:T(4,128)(2,1)}), bf16[384,3,1088]{0,1,2:T(4,128)(2,1)S(1)}, u32[]{:S(2)}, u32[]{:S(2)}) async-start(bf16[384,3,1088]{0,1,2:T(4,128)(2,1)} %pad_maximum_fusion.1), calls=%async_computation.3 | async-start | bytes 6684672 | tf_op jit(solution)/shard_map/all_to_all | solution.py:306
  2039.8 61.2 %all-to-all-done.3 = bf16[384,3,1088]{0,1,2:T(4,128)(2,1)S(1)} async-done(((bf16[384,3,1088]{0,1,2:T(4,128)(2,1)}), bf16[384,3,1088]{0,1,2:T(4,128)(2,1)S(1)}, u32[]{:S(2)}, u32[]{:S(2)}) %all-to-all-start.3) | async-done | bytes 2506784 | tf_op jit(solution)/shard_map/all_to_all | solution.py:306
  2109.0 9.6 convolution_convert_fusion.5
  2118.9 6.0 fusion.26
  2138.6 8.3 fusion.64
  2147.2 90.8 %all-reduce.8.cloned.1.call-done = bf16[3,272,1088]{1,2,0:T(8,128)(2,1)} async-done(((bf16[3,272,1088]{1,2,0:T(8,128)(2,1)}), bf16[3,272,1088]{1,2,0:T(8,128)(2,1)}) %all-reduce.8.cloned.1.call-update) | async-done | bytes 1775632
  2239.8 66.4 %reduce-scatter.29.cloned.1.call-done = bf16[384,1088]{1,0:T(8,128)(2,1)} async-done(((bf16[1536,1088]{1,0:T(8,128)(2,1)}), bf16[384,1088]{1,0:T(8,128)(2,1)}) %reduce-scatter.29.cloned.1.call-update) | async-done | bytes 835600
  2316.1 43.0 %all-reduce.5 = (f32[1088]{0:T(1024)}, f32[1088]{0:T(1024)}, f32[2,1088]{1,0:T(2,128)}, f32[1088]{0:T(1024)}, f32[1088]{0:T(1024)}, /*index=5*/f32[1088]{0:T(1024)}, f32[4352]{0:T(1024)S(1)}, f32[1088]{0:T(1024)}) all-reduce(f32[1088]{0:T(1024)S(1)} %get-tuple-element.914, ...), channel_id=1, replica_groups=mesh['dp'=8,'tensor'=4] {'dp','tensor'}, use_global_device_ids=true, to_apply=%region_36.37 | all-reduce | flops 13056 | bytes 104448 | tf_op jit(solution)/shard_map/psum | solution.py:339
  (598 shorter events, 460.1 us)
Async XLA Ops:
  7.2 1152.2 %copy-start = (bf16[1088,1088]{1,0:T(8,128)(2,1)S(1)}, bf16[1088,1088]{1,0:T(8,128)(2,1)}, u32[]{:S(2)}) copy-start(bf16[1088,1088]{1,0:T(8,128)(2,1)} %param.40) | copy-start | bytes 7102468
  7.2 76.3 %all-gather.5.cloned.1.call-start = ((), (), s32[]{:S(2)}) async-start(), calls=%async_computation.11 | async-start | bytes 4177920 | tf_op jit(solution)/shard_map/all_gather | solution.py:27
  8.7 82.2 %copy-start.32 = (f32[384]{0:T(512)}, f32[384]{0:T(512)S(1)}, u32[]{:S(2)}) copy-start(f32[384]{0:T(512)S(1)} %broadcast_multiply_fusion.5) | copy-start | bytes 4612
  10.2 80.7 %copy-start.38 = (f32[384]{0:T(512)}, f32[384]{0:T(512)S(1)}, u32[]{:S(2)}) copy-start(f32[384]{0:T(512)S(1)} %add_rsqrt_fusion.1) | copy-start | bytes 4612
  10.9 80.0 %copy-start.28 = (f32[1088]{0:T(1024)}, f32[1088]{0:T(1024)S(1)}, u32[]{:S(2)}) copy-start(f32[1088]{0:T(1024)S(1)} %convert_element_type.214) | copy-start | bytes 13060
  98.5 109.8 %all-to-all-start = ((bf16[1536,3,272]{2,1,0:T(4,128)(2,1)}), bf16[1536,3,272]{2,1,0:T(4,128)(2,1)}, u32[]{:S(2)}, u32[]{:S(2)}) async-start(bf16[1536,3,272]{2,1,0:T(4,128)(2,1)} %copy.104), calls=%async_computation | async-start | bytes 9437184 | tf_op jit(solution)/shard_map/all_to_all | solution.py:37
  103.6 920.3 %reduce-scatter.23.cloned.1.call-start = ((), (), s32[]{:S(2)}) async-start(), calls=%async_computation.15 | async-start | bytes 4423680
  104.2 111.9 %copy-start.43 = (s32[384]{0:T(512)}, s32[384]{0:T(512)S(1)}, u32[]{:S(2)}) copy-start(s32[384]{0:T(512)S(1)} %iota_add_fusion.4) | copy-start | bytes 4612
  227.4 37.5 %collective-permute-start = (bf16[384,2,1088]{0,2,1:T(8,128)(2,1)}, bf16[384,2,1088]{0,2,1:T(8,128)(2,1)}, u32[]{:S(2)}, u32[]{:S(2)}) collective-permute-start(bf16[384,2,1088]{0,2,1:T(8,128)(2,1)} %get-tuple-element.1247), channel_id=1, source_target_pairs={{0,1},{1,2},{2,3},{3,4},{4,5},{5,6},{6,7},{7,8},{8,9},{9,10},{10,1... | collective-permute-start | bytes 5013512 | tf_op jit(solution)/shard_map/while/body/eval_jaxpr/ppermute | solution.py:19
  270.5 41.1 %collective-permute-start = (bf16[384,2,1088]{0,2,1:T(8,128)(2,1)}, bf16[384,2,1088]{0,2,1:T(8,128)(2,1)}, u32[]{:S(2)}, u32[]{:S(2)}) collective-permute-start(bf16[384,2,1088]{0,2,1:T(8,128)(2,1)} %get-tuple-element.1247), channel_id=1, source_target_pairs={{0,1},{1,2},{2,3},{3,4},{4,5},{5,6},{6,7},{7,8},{8,9},{9,10},{10,1... | collective-permute-start | bytes 5013512 | tf_op jit(solution)/shard_map/while/body/eval_jaxpr/ppermute | solution.py:19
  317.2 40.3 %collective-permute-start = (bf16[384,2,1088]{0,2,1:T(8,128)(2,1)}, bf16[384,2,1088]{0,2,1:T(8,128)(2,1)}, u32[]{:S(2)}, u32[]{:S(2)}) collective-permute-start(bf16[384,2,1088]{0,2,1:T(8,128)(2,1)} %get-tuple-element.1247), channel_id=1, source_target_pairs={{0,1},{1,2},{2,3},{3,4},{4,5},{5,6},{6,7},{7,8},{8,9},{9,10},{10,1... | collective-permute-start | bytes 5013512 | tf_op jit(solution)/shard_map/while/body/eval_jaxpr/ppermute | solution.py:19
  363.1 39.4 %collective-permute-start = (bf16[384,2,1088]{0,2,1:T(8,128)(2,1)}, bf16[384,2,1088]{0,2,1:T(8,128)(2,1)}, u32[]{:S(2)}, u32[]{:S(2)}) collective-permute-start(bf16[384,2,1088]{0,2,1:T(8,128)(2,1)} %get-tuple-element.1247), channel_id=1, source_target_pairs={{0,1},{1,2},{2,3},{3,4},{4,5},{5,6},{6,7},{7,8},{8,9},{9,10},{10,1... | collective-permute-start | bytes 5013512 | tf_op jit(solution)/shard_map/while/body/eval_jaxpr/ppermute | solution.py:19
  408.2 38.8 %collective-permute-start = (bf16[384,2,1088]{0,2,1:T(8,128)(2,1)}, bf16[384,2,1088]{0,2,1:T(8,128)(2,1)}, u32[]{:S(2)}, u32[]{:S(2)}) collective-permute-start(bf16[384,2,1088]{0,2,1:T(8,128)(2,1)} %get-tuple-element.1247), channel_id=1, source_target_pairs={{0,1},{1,2},{2,3},{3,4},{4,5},{5,6},{6,7},{7,8},{8,9},{9,10},{10,1... | collective-permute-start | bytes 5013512 | tf_op jit(solution)/shard_map/while/body/eval_jaxpr/ppermute | solution.py:19
  452.6 40.9 %collective-permute-start = (bf16[384,2,1088]{0,2,1:T(8,128)(2,1)}, bf16[384,2,1088]{0,2,1:T(8,128)(2,1)}, u32[]{:S(2)}, u32[]{:S(2)}) collective-permute-start(bf16[384,2,1088]{0,2,1:T(8,128)(2,1)} %get-tuple-element.1247), channel_id=1, source_target_pairs={{0,1},{1,2},{2,3},{3,4},{4,5},{5,6},{6,7},{7,8},{8,9},{9,10},{10,1... | collective-permute-start | bytes 5013512 | tf_op jit(solution)/shard_map/while/body/eval_jaxpr/ppermute | solution.py:19
  499.1 40.1 %collective-permute-start = (bf16[384,2,1088]{0,2,1:T(8,128)(2,1)}, bf16[384,2,1088]{0,2,1:T(8,128)(2,1)}, u32[]{:S(2)}, u32[]{:S(2)}) collective-permute-start(bf16[384,2,1088]{0,2,1:T(8,128)(2,1)} %get-tuple-element.1247), channel_id=1, source_target_pairs={{0,1},{1,2},{2,3},{3,4},{4,5},{5,6},{6,7},{7,8},{8,9},{9,10},{10,1... | collective-permute-start | bytes 5013512 | tf_op jit(solution)/shard_map/while/body/eval_jaxpr/ppermute | solution.py:19
  544.9 39.7 %collective-permute-start = (bf16[384,2,1088]{0,2,1:T(8,128)(2,1)}, bf16[384,2,1088]{0,2,1:T(8,128)(2,1)}, u32[]{:S(2)}, u32[]{:S(2)}) collective-permute-start(bf16[384,2,1088]{0,2,1:T(8,128)(2,1)} %get-tuple-element.1247), channel_id=1, source_target_pairs={{0,1},{1,2},{2,3},{3,4},{4,5},{5,6},{6,7},{7,8},{8,9},{9,10},{10,1... | collective-permute-start | bytes 5013512 | tf_op jit(solution)/shard_map/while/body/eval_jaxpr/ppermute | solution.py:19
  590.2 38.8 %collective-permute-start = (bf16[384,2,1088]{0,2,1:T(8,128)(2,1)}, bf16[384,2,1088]{0,2,1:T(8,128)(2,1)}, u32[]{:S(2)}, u32[]{:S(2)}) collective-permute-start(bf16[384,2,1088]{0,2,1:T(8,128)(2,1)} %get-tuple-element.1247), channel_id=1, source_target_pairs={{0,1},{1,2},{2,3},{3,4},{4,5},{5,6},{6,7},{7,8},{8,9},{9,10},{10,1... | collective-permute-start | bytes 5013512 | tf_op jit(solution)/shard_map/while/body/eval_jaxpr/ppermute | solution.py:19
  634.5 41.1 %collective-permute-start = (bf16[384,2,1088]{0,2,1:T(8,128)(2,1)}, bf16[384,2,1088]{0,2,1:T(8,128)(2,1)}, u32[]{:S(2)}, u32[]{:S(2)}) collective-permute-start(bf16[384,2,1088]{0,2,1:T(8,128)(2,1)} %get-tuple-element.1247), channel_id=1, source_target_pairs={{0,1},{1,2},{2,3},{3,4},{4,5},{5,6},{6,7},{7,8},{8,9},{9,10},{10,1... | collective-permute-start | bytes 5013512 | tf_op jit(solution)/shard_map/while/body/eval_jaxpr/ppermute | solution.py:19
  681.1 40.3 %collective-permute-start = (bf16[384,2,1088]{0,2,1:T(8,128)(2,1)}, bf16[384,2,1088]{0,2,1:T(8,128)(2,1)}, u32[]{:S(2)}, u32[]{:S(2)}) collective-permute-start(bf16[384,2,1088]{0,2,1:T(8,128)(2,1)} %get-tuple-element.1247), channel_id=1, source_target_pairs={{0,1},{1,2},{2,3},{3,4},{4,5},{5,6},{6,7},{7,8},{8,9},{9,10},{10,1... | collective-permute-start | bytes 5013512 | tf_op jit(solution)/shard_map/while/body/eval_jaxpr/ppermute | solution.py:19
  889.2 203.3 %all-gather.9.cloned.1.call-start = ((), (), s32[]{:S(2)}) async-start(), calls=%async_computation.13 | async-start | bytes 4177920 | tf_op jit(solution)/shard_map/all_gather | solution.py:27
  890.0 269.4 %all-gather.7.cloned.1.call-start = ((), (), s32[]{:S(2)}) async-start(), calls=%async_computation.12 | async-start | bytes 4177920 | tf_op jit(solution)/shard_map/all_gather | solution.py:27
  890.0 366.5 %copy-start.24 = (f32[1088]{0:T(1024)}, f32[1088]{0:T(1024)S(1)}, u32[]{:S(2)}) copy-start(f32[1088]{0:T(1024)S(1)} %convert_element_type.223) | copy-start | bytes 13060
  890.1 366.4 %copy-start.26 = (f32[1088]{0:T(1024)}, f32[1088]{0:T(1024)S(1)}, u32[]{:S(2)}) copy-start(f32[1088]{0:T(1024)S(1)} %convert_element_type.224) | copy-start | bytes 13060
  1028.0 228.5 %copy-start.30 = (f32[384]{0:T(512)}, f32[384]{0:T(512)S(1)}, u32[]{:S(2)}) copy-start(f32[384]{0:T(512)S(1)} %broadcast_multiply_fusion.4) | copy-start | bytes 4612
  1029.8 226.7 %copy-start.34 = (f32[384]{0:T(512)}, f32[384]{0:T(512)S(1)}, u32[]{:S(2)}) copy-start(f32[384]{0:T(512)S(1)} %add_rsqrt_fusion) | copy-start | bytes 4612
  1031.3 221.2 %reduce-scatter.27.cloned.1.call-start = ((), (), s32[]{:S(2)}) async-start(), calls=%async_computation.17 | async-start | bytes 4423680
  1187.2 67.6 %copy-start.6 = (bf16[384,1088]{0,1:T(8,128)(2,1)S(1)}, bf16[384,1088]{0,1:T(8,128)(2,1)}, u32[]{:S(2)}) copy-start(bf16[384,1088]{0,1:T(8,128)(2,1)} %param.31) | copy-start | bytes 2506756
  1187.2 67.6 %copy-start.9 = (bf16[384,1088]{0,1:T(8,128)(2,1)S(1)}, bf16[384,1088]{0,1:T(8,128)(2,1)}, u32[]{:S(2)}) copy-start(bf16[384,1088]{0,1:T(8,128)(2,1)} %copy.124) | copy-start | bytes 2506756
  1187.2 140.0 %all-gather.11.cloned.1.call-start = ((), (), s32[]{:S(2)}) async-start(), calls=%async_computation.14 | async-start | bytes 4177920 | tf_op jit(solution)/shard_map/all_gather | solution.py:289
  1260.1 870.8 %reduce-scatter.35.cloned.1.call-start = ((), (), s32[]{:S(2)}) async-start(), calls=%async_computation.22 | async-start | bytes 2820096
  1270.4 862.4 %reduce-scatter.33.cloned.1.call-start = ((), (), s32[]{:S(2)}) async-start(), calls=%async_computation.21 | async-start | bytes 2820096
  1279.5 47.8 %copy-start.58 = (bf16[272,1088]{1,0:T(8,128)(2,1)S(1)}, bf16[272,1088]{1,0:T(8,128)(2,1)}, u32[]{:S(2)}) copy-start(bf16[272,1088]{1,0:T(8,128)(2,1)} %param.36) | copy-start | bytes 1775620
  1337.0 24.9 %all-to-all-start.2 = ((bf16[4,2,52224]{2,1,0:T(2,128)(2,1)}), bf16[4,2,52224]{2,1,0:T(2,128)(2,1)S(1)}, u32[]{:S(2)}, u32[]{:S(2)}) async-start(bf16[4,2,52224]{2,1,0:T(2,128)(2,1)} %reshape.521), calls=%async_computation.2 | async-start | bytes 1671168 | tf_op jit(solution)/shard_map/all_to_all | solution.py:37
  1340.5 794.2 %reduce-scatter.25.cloned.1.call-start = ((), (), s32[]{:S(2)}) async-start(), calls=%async_computation.16 | async-start | bytes 4423680
  1410.5 83.7 %collective-permute-start.1 = (bf16[384,2,1088]{0,2,1:T(8,128)(2,1)}, bf16[384,2,1088]{0,2,1:T(8,128)(2,1)S(1)}, u32[]{:S(2)}, u32[]{:S(2)}) collective-permute-start(bf16[384,2,1088]{0,2,1:T(8,128)(2,1)} %fusion.124), channel_id=1, source_target_pairs={{1,0},{2,1},{3,2},{4,3},{5,4},{6,5},{7,6},{8,7},{9,8},{10,9},{11,1... | collective-permute-start | bytes 5013512 | tf_op jit(solution)/shard_map/while/body/eval_jaxpr/ppermute | solution.py:19
  1414.7 81.5 %copy-start.3 = (bf16[384,17,64]{0,2,1:T(8,128)(2,1)S(1)}, bf16[384,17,64]{0,2,1:T(8,128)(2,1)}, u32[]{:S(2)}) copy-start(bf16[384,17,64]{0,2,1:T(8,128)(2,1)} %copy-done.2) | copy-start | bytes 2506756 | tf_op jit(solution)/shard_map/while
  1503.8 39.3 %collective-permute-start.1 = (bf16[384,2,1088]{0,2,1:T(8,128)(2,1)}, bf16[384,2,1088]{0,2,1:T(8,128)(2,1)S(1)}, u32[]{:S(2)}, u32[]{:S(2)}) collective-permute-start(bf16[384,2,1088]{0,2,1:T(8,128)(2,1)} %fusion.124), channel_id=1, source_target_pairs={{1,0},{2,1},{3,2},{4,3},{5,4},{6,5},{7,6},{8,7},{9,8},{10,9},{11,1... | collective-permute-start | bytes 5013512 | tf_op jit(solution)/shard_map/while/body/eval_jaxpr/ppermute | solution.py:19
  1552.5 36.3 %collective-permute-start.1 = (bf16[384,2,1088]{0,2,1:T(8,128)(2,1)}, bf16[384,2,1088]{0,2,1:T(8,128)(2,1)S(1)}, u32[]{:S(2)}, u32[]{:S(2)}) collective-permute-start(bf16[384,2,1088]{0,2,1:T(8,128)(2,1)} %fusion.124), channel_id=1, source_target_pairs={{1,0},{2,1},{3,2},{4,3},{5,4},{6,5},{7,6},{8,7},{9,8},{10,9},{11,1... | collective-permute-start | bytes 5013512 | tf_op jit(solution)/shard_map/while/body/eval_jaxpr/ppermute | solution.py:19
  1598.3 36.8 %collective-permute-start.1 = (bf16[384,2,1088]{0,2,1:T(8,128)(2,1)}, bf16[384,2,1088]{0,2,1:T(8,128)(2,1)S(1)}, u32[]{:S(2)}, u32[]{:S(2)}) collective-permute-start(bf16[384,2,1088]{0,2,1:T(8,128)(2,1)} %fusion.124), channel_id=1, source_target_pairs={{1,0},{2,1},{3,2},{4,3},{5,4},{6,5},{7,6},{8,7},{9,8},{10,9},{11,1... | collective-permute-start | bytes 5013512 | tf_op jit(solution)/shard_map/while/body/eval_jaxpr/ppermute | solution.py:19
  1644.7 47.5 %collective-permute-start.1 = (bf16[384,2,1088]{0,2,1:T(8,128)(2,1)}, bf16[384,2,1088]{0,2,1:T(8,128)(2,1)S(1)}, u32[]{:S(2)}, u32[]{:S(2)}) collective-permute-start(bf16[384,2,1088]{0,2,1:T(8,128)(2,1)} %fusion.124), channel_id=1, source_target_pairs={{1,0},{2,1},{3,2},{4,3},{5,4},{6,5},{7,6},{8,7},{9,8},{10,9},{11,1... | collective-permute-start | bytes 5013512 | tf_op jit(solution)/shard_map/while/body/eval_jaxpr/ppermute | solution.py:19
  1649.2 44.9 %copy-start.3 = (bf16[384,17,64]{0,2,1:T(8,128)(2,1)S(1)}, bf16[384,17,64]{0,2,1:T(8,128)(2,1)}, u32[]{:S(2)}) copy-start(bf16[384,17,64]{0,2,1:T(8,128)(2,1)} %copy-done.2) | copy-start | bytes 2506756 | tf_op jit(solution)/shard_map/while
  1701.6 40.9 %collective-permute-start.1 = (bf16[384,2,1088]{0,2,1:T(8,128)(2,1)}, bf16[384,2,1088]{0,2,1:T(8,128)(2,1)S(1)}, u32[]{:S(2)}, u32[]{:S(2)}) collective-permute-start(bf16[384,2,1088]{0,2,1:T(8,128)(2,1)} %fusion.124), channel_id=1, source_target_pairs={{1,0},{2,1},{3,2},{4,3},{5,4},{6,5},{7,6},{8,7},{9,8},{10,9},{11,1... | collective-permute-start | bytes 5013512 | tf_op jit(solution)/shard_map/while/body/eval_jaxpr/ppermute | solution.py:19
  1706.2 38.3 %copy-start.3 = (bf16[384,17,64]{0,2,1:T(8,128)(2,1)S(1)}, bf16[384,17,64]{0,2,1:T(8,128)(2,1)}, u32[]{:S(2)}) copy-start(bf16[384,17,64]{0,2,1:T(8,128)(2,1)} %copy-done.2) | copy-start | bytes 2506756 | tf_op jit(solution)/shard_map/while
  1752.0 40.1 %collective-permute-start.1 = (bf16[384,2,1088]{0,2,1:T(8,128)(2,1)}, bf16[384,2,1088]{0,2,1:T(8,128)(2,1)S(1)}, u32[]{:S(2)}, u32[]{:S(2)}) collective-permute-start(bf16[384,2,1088]{0,2,1:T(8,128)(2,1)} %fusion.124), channel_id=1, source_target_pairs={{1,0},{2,1},{3,2},{4,3},{5,4},{6,5},{7,6},{8,7},{9,8},{10,9},{11,1... | collective-permute-start | bytes 5013512 | tf_op jit(solution)/shard_map/while/body/eval_jaxpr/ppermute | solution.py:19
  1801.6 39.2 %collective-permute-start.1 = (bf16[384,2,1088]{0,2,1:T(8,128)(2,1)}, bf16[384,2,1088]{0,2,1:T(8,128)(2,1)S(1)}, u32[]{:S(2)}, u32[]{:S(2)}) collective-permute-start(bf16[384,2,1088]{0,2,1:T(8,128)(2,1)} %fusion.124), channel_id=1, source_target_pairs={{1,0},{2,1},{3,2},{4,3},{5,4},{6,5},{7,6},{8,7},{9,8},{10,9},{11,1... | collective-permute-start | bytes 5013512 | tf_op jit(solution)/shard_map/while/body/eval_jaxpr/ppermute | solution.py:19
  1850.3 28.8 %collective-permute-start.1 = (bf16[384,2,1088]{0,2,1:T(8,128)(2,1)}, bf16[384,2,1088]{0,2,1:T(8,128)(2,1)S(1)}, u32[]{:S(2)}, u32[]{:S(2)}) collective-permute-start(bf16[384,2,1088]{0,2,1:T(8,128)(2,1)} %fusion.124), channel_id=1, source_target_pairs={{1,0},{2,1},{3,2},{4,3},{5,4},{6,5},{7,6},{8,7},{9,8},{10,9},{11,1... | collective-permute-start | bytes 5013512 | tf_op jit(solution)/shard_map/while/body/eval_jaxpr/ppermute | solution.py:19
  1888.6 23.6 collective-permute-start.1
  1921.6 44.2 %collective-permute-start.1 = (bf16[384,2,1088]{0,2,1:T(8,128)(2,1)}, bf16[384,2,1088]{0,2,1:T(8,128)(2,1)S(1)}, u32[]{:S(2)}, u32[]{:S(2)}) collective-permute-start(bf16[384,2,1088]{0,2,1:T(8,128)(2,1)} %fusion.124), channel_id=1, source_target_pairs={{1,0},{2,1},{3,2},{4,3},{5,4},{6,5},{7,6},{8,7},{9,8},{10,9},{11,1... | collective-permute-start | bytes 5013512 | tf_op jit(solution)/shard_map/while/body/eval_jaxpr/ppermute | solution.py:19
  1926.2 41.6 %copy-start.3 = (bf16[384,17,64]{0,2,1:T(8,128)(2,1)S(1)}, bf16[384,17,64]{0,2,1:T(8,128)(2,1)}, u32[]{:S(2)}) copy-start(bf16[384,17,64]{0,2,1:T(8,128)(2,1)} %copy-done.2) | copy-start | bytes 2506756 | tf_op jit(solution)/shard_map/while
  2001.7 99.3 %all-to-all-start.3 = ((bf16[384,3,1088]{0,1,2:T(4,128)(2,1)}), bf16[384,3,1088]{0,1,2:T(4,128)(2,1)S(1)}, u32[]{:S(2)}, u32[]{:S(2)}) async-start(bf16[384,3,1088]{0,1,2:T(4,128)(2,1)} %pad_maximum_fusion.1), calls=%async_computation.3 | async-start | bytes 6684672 | tf_op jit(solution)/shard_map/all_to_all | solution.py:306
  2034.7 102.3 %reduce-scatter.31.cloned.1.call-start = ((), (), s32[]{:S(2)}) async-start(), calls=%async_computation.20 | async-start | bytes 940032
  2039.8 198.2 %all-reduce.8.cloned.1.call-start = ((), (), s32[]{:S(2)}) async-start(), calls=%async_computation.19 | async-start | bytes 5013504
  2118.6 187.6 %reduce-scatter.29.cloned.1.call-start = ((), (), s32[]{:S(2)}) async-start(), calls=%async_computation.18 | async-start | bytes 4423680
  2134.7 174.8 %copy-start.7 = (bf16[384,1088]{0,1:T(8,128)(2,1)S(1)}, bf16[384,1088]{0,1:T(8,128)(2,1)}, u32[]{:S(2)}) copy-start(bf16[384,1088]{0,1:T(8,128)(2,1)} %param.31) | copy-start | bytes 2506756
  2134.7 174.8 %copy-start.29 = (f32[1088]{0:T(1024)S(1)}, f32[1088]{0:T(1024)}, u32[]{:S(2)}) copy-start(f32[1088]{0:T(1024)} %copy-done.28) | copy-start | bytes 13060
  2134.7 174.8 %copy-start.33 = (f32[384]{0:T(512)S(1)}, f32[384]{0:T(512)}, u32[]{:S(2)}) copy-start(f32[384]{0:T(512)} %copy-done.32) | copy-start | bytes 4612
  2134.7 174.8 %copy-start.39 = (f32[384]{0:T(512)S(1)}, f32[384]{0:T(512)}, u32[]{:S(2)}) copy-start(f32[384]{0:T(512)} %copy-done.38) | copy-start | bytes 4612
  2138.6 171.8 %copy-start.25 = (f32[1088]{0:T(1024)S(1)}, f32[1088]{0:T(1024)}, u32[]{:S(2)}) copy-start(f32[1088]{0:T(1024)} %copy-done.24) | copy-start | bytes 13060
  2138.6 171.8 %copy-start.27 = (f32[1088]{0:T(1024)S(1)}, f32[1088]{0:T(1024)}, u32[]{:S(2)}) copy-start(f32[1088]{0:T(1024)} %copy-done.26) | copy-start | bytes 13060
  2138.6 171.8 %copy-start.31 = (f32[384]{0:T(512)S(1)}, f32[384]{0:T(512)}, u32[]{:S(2)}) copy-start(f32[384]{0:T(512)} %copy-done.30) | copy-start | bytes 4612
  2138.6 171.8 %copy-start.35 = (f32[384]{0:T(512)S(1)}, f32[384]{0:T(512)}, u32[]{:S(2)}) copy-start(f32[384]{0:T(512)} %copy-done.34) | copy-start | bytes 4612
  2138.6 171.8 %copy-start.46 = (f32[384]{0:T(512)S(1)}, f32[384]{0:T(512)}, u32[]{:S(2)}) copy-start(f32[384]{0:T(512)} %copy-done.45) | copy-start | bytes 4612
  2138.6 171.8 %copy-start.48 = (f32[384]{0:T(512)S(1)}, f32[384]{0:T(512)}, u32[]{:S(2)}) copy-start(f32[384]{0:T(512)} %copy-done.47) | copy-start | bytes 4612
  2310.3 49.4 %copy-start.1 = (bf16[1088,1088]{1,0:T(8,128)(2,1)S(1)}, bf16[1088,1088]{1,0:T(8,128)(2,1)}, u32[]{:S(2)}) copy-start(bf16[1088,1088]{1,0:T(8,128)(2,1)} %param.40) | copy-start | bytes 7102468
  (54 other events, 505.1 us)
Sparse Core Ops, SparseCore 0:
  14.1 69.3 all-gather.4
  889.3 134.5 reduce-scatter.22
  1025.6 66.9 all-gather.8
  1094.0 65.3 all-gather.6
  1187.3 65.0 reduce-scatter.26
  1260.3 66.9 all-gather.10
  1330.7 41.7 reduce-scatter.34
  1376.0 43.0 reduce-scatter.32
  1421.3 91.1 reduce-scatter.24
  2039.9 84.9 reduce-scatter.30
  2128.2 109.7 all-reduce.7
  2240.2 65.9 reduce-scatter.28
where the time goes:
time: 2400 us; the launch traced here: 2370 us
  waiting for transfers between devices  1540 us (64%)
  local copies, waits for them, and re-layouts  261 us (11%)
  other arithmetic  169 us (7%)
  matrix products  123 us (5%)
  starting transfers between devices  116 us (5%)
  blocking collectives  89.4 us (4%)
  loops' own time  47.1 us (2%)
    ppermute x22, waiting for transfers between devices, shifted(): lax.ppermute(value, axis, [(source, source + steps) for source in range(f...  790 us
    unnamed x20, waiting for transfers between devices  357 us
    all_gather x3, waiting for transfers between devices, widen(): return lax.all_gather(token_rows, 'tensor', axis=0, tiled=True)  187 us
    all_to_all x2, waiting for transfers between devices, to_tokens(): lax.all_to_all(feature_rows, 'tensor', split_axis=0, concat_axis=2, tiled...  105 us
    ppermute x22, starting transfers between devices, shifted(): lax.ppermute(value, axis, [(source, source + steps) for source in range(f...  72.3 us
    all_to_all x1, waiting for transfers between devices, local(): lax.all_to_all(grad_qkv_rows, 'tensor', split_axis=2, concat_axis=0, tile...  61.2 us
    unnamed x135, local copies, waits for them, and re-layouts  52.2 us
  transfers between devices with their start and end apart: 37, of which 33 were waited for; matrix products, arithmetic and copies ran while one was open for 13% of the time, Pallas kernels for 0%

commit v1 on v0

v1 whole, which is shorter than its diff:
```python
import functools

import jax
import jax.numpy as jnp
from jax import lax
from jax.experimental import pallas as pl
from jax.experimental.pallas import tpu as pltpu
from jax.sharding import PartitionSpec as P

HEADS = 17
HEAD_DIM = 64
REACH = 11

norm_eps = 1e-05
score_scale = 0.125
masked_score = -1e30
everywhere = ("dp", "tensor")


def line(count, steps):
    first, last = (max(0, -steps), min(count, count - steps))
    return [(source, source + steps) for source in range(first, last)]


def gather_tensor(rows, axis):
    count = lax.axis_size("tensor")
    index = lax.axis_index("tensor")
    up, down = [rows], [rows]
    for _ in range(count - 1):
        up.append(lax.ppermute(up[-1], "tensor", line(count, 1)))
        down.append(lax.ppermute(down[-1], "tensor", line(count, -1)))
    shape = rows.shape[:axis] + (count,) + rows.shape[axis:]
    gathered = lax.dynamic_update_index_in_dim(jnp.zeros(shape, rows.dtype), rows, index, axis)
    for steps in range(1, count):
        block = jnp.where(index >= steps, up[steps], down[count - steps])
        gathered = lax.dynamic_update_index_in_dim(
            gathered, block, lax.rem(index - steps + count, count), axis
        )
    return gathered


def scatter_tensor(partial_sum):
    arrived = lax.all_to_all(
        partial_sum.astype(jnp.bfloat16), "tensor", split_axis=0, concat_axis=0, tiled=True
    )
    return jnp.sum(arrived.astype(jnp.float32), axis=0)


def scatter_dp(partial_sum, axis):
    return lax.psum_scatter(
        partial_sum.astype(jnp.bfloat16), "dp", scatter_dimension=axis, tiled=True
    ).astype(jnp.float32)


def norm_forward(values, gain_vec, bias_vec):
    mean_row = jnp.mean(values, axis=1, keepdims=True)
    centered = values - mean_row
    variance = jnp.mean(centered * centered, axis=1, keepdims=True)
    inv_std = lax.rsqrt(variance + norm_eps)
    normed = centered * inv_std
    return (normed, inv_std, normed * gain_vec + bias_vec)


def norm_backward(grad_normed, normed, inv_std, gain_vec):
    scaled = grad_normed * gain_vec
    plain_mean = jnp.mean(scaled, axis=1, keepdims=True)
    cross_mean = jnp.mean(scaled * normed, axis=1, keepdims=True)
    grad_values = inv_std * (scaled - plain_mean - normed * cross_mean)
    return (grad_values, jnp.sum(grad_normed * normed, axis=0), jnp.sum(grad_normed, axis=0))


def tile_of(width):
    return 384 if width % 384 == 0 else width


def attention_plan(query_pos, key_base, key_offsets, seq_ends):
    width = query_pos.shape[1]
    key_width = key_offsets.shape[0]
    tile, key_tile = tile_of(width), tile_of(key_width)
    starts = jnp.max(
        jnp.where(seq_ends[None, None, :] <= query_pos[:, :, None], seq_ends[None, None, :], 0),
        axis=2,
    )
    rows = jnp.stack((query_pos, starts), axis=1)
    tiles = query_pos.reshape(-1, tile)
    first, last = tiles[:, 0], tiles[:, tile - 1]
    last_start = starts.reshape(-1, tile)[:, tile - 1]
    offset_tiles = key_offsets.reshape(-1, key_tile)
    key_min = (key_base[:, None] + offset_tiles[None, :, 0]).reshape(-1)
    key_max = (key_base[:, None] + offset_tiles[None, :, key_tile - 1]).reshape(-1)
    key_end = jnp.min(
        jnp.where(seq_ends[None, :] > key_max[:, None], seq_ends[None, :], seq_ends[-1]), axis=1
    )
    low = jnp.sum((last[None, :] < key_min[:, None]).astype(jnp.int32), axis=1)
    high = jnp.sum((first[None, :] < key_end[:, None]).astype(jnp.int32), axis=1)
    bases = jnp.repeat(key_base, key_width // key_tile)
    plan = jnp.concatenate((low, high, bases, key_min, key_max, first, last_start))
    return (plan.astype(jnp.int32), rows.astype(jnp.int32), key_offsets[:, None].astype(jnp.int32))


def key_allowed(column_ref, rows_ref, step, per_key, key_tile, base, group, lanes):
    offset = pl.multiple_of(lax.rem(step, per_key) * key_tile, key_tile)
    key_pos = column_ref[pl.ds(offset, key_tile), :] + base
    query_pos = rows_ref[group, 0:1, lanes]
    query_start = rows_ref[group, 1:2, lanes]
    return (key_pos <= query_pos) & (key_pos >= query_start)


def forward_kernel(
    dims, plan_ref, query_ref, pair_ref, rows_ref, column_ref, out_ref, total_ref, acc, top, tot
):
    blocks, groups, per_query, per_key, tile, key_tile = dims
    count = groups * per_query
    step = pl.program_id(0)

    @pl.when(step == 0)
    def _():
        acc[...] = jnp.zeros_like(acc)
        tot[...] = jnp.zeros_like(tot)
        top[...] = jnp.full(top.shape, masked_score, jnp.float32)

    keys = jnp.transpose(pair_ref[0, :HEAD_DIM, :].astype(jnp.float32)).astype(jnp.bfloat16)
    values_t = pair_ref[0, HEAD_DIM:, :]
    base, key_min, key_max = (plan_ref[kind * blocks + step] for kind in (2, 3, 4))

    def one_tile(index, _):
        group = lax.div(index, per_query)
        lanes = pl.ds(pl.multiple_of(lax.rem(index, per_query) * tile, tile), tile)
        queries_t = query_ref[group, :HEAD_DIM, lanes] * jnp.bfloat16(score_scale)
        inside = (key_max <= plan_ref[5 * blocks + index]) & (
            key_min >= plan_ref[5 * blocks + count + index]
        )

        def update(masked):
            scores = jnp.dot(keys, queries_t, preferred_element_type=jnp.float32)
            if masked:
                allowed = key_allowed(
                    column_ref, rows_ref, step, per_key, key_tile, base, group, lanes
                )
                scores = jnp.where(allowed, scores, masked_score)
            old_top = top[index]
            new_top = jnp.maximum(old_top, jnp.max(scores, axis=0, keepdims=True))
            weights = jnp.exp(scores - new_top)
            shrink = jnp.exp(old_top - new_top)
            top[index] = new_top
            tot[index] = tot[index] * shrink + jnp.sum(weights, axis=0, keepdims=True)
            acc[index] = acc[index] * shrink + jnp.dot(
                values_t, weights.astype(jnp.bfloat16), preferred_element_type=jnp.float32
            )

        pl.when(inside)(lambda: update(False))
        pl.when(jnp.logical_not(inside))(lambda: update(True))
        return 0

    lax.fori_loop(plan_ref[step], plan_ref[blocks + step], one_tile, 0)

    @pl.when(step == blocks - 1)
    def _():
        def finish(index, _):
            group = lax.div(index, per_query)
            lanes = pl.ds(pl.multiple_of(lax.rem(index, per_query) * tile, tile), tile)
            out_ref[group, :, lanes] = acc[index] / tot[index]
            total_ref[index] = top[index] + jnp.log(tot[index])
            return 0

        lax.fori_loop(0, count, finish, 0)


def backward_kernel(
    dims,
    plan_ref,
    query_ref,
    pair_ref,
    rows_ref,
    column_ref,
    grad_ref,
    out_ref,
    total_ref,
    query_grad_ref,
    pair_grad_ref,
    acc,
    inner,
    query_rows,
    grad_rows,
    key_acc,
    value_acc,
):
    blocks, groups, per_query, per_key, tile, key_tile = dims
    count = groups * per_query
    step = pl.program_id(0)

    @pl.when(step == 0)
    def _():
        acc[...] = jnp.zeros_like(acc)

        def prepare(index, _):
            group = lax.div(index, per_query)
            lanes = pl.ds(pl.multiple_of(lax.rem(index, per_query) * tile, tile), tile)
            grads = grad_ref[group, :, lanes].astype(jnp.float32)
            inner[index] = jnp.sum(grads * out_ref[group, :, lanes], axis=0, keepdims=True)
            grad_rows[index] = jnp.transpose(grads).astype(jnp.bfloat16)
            scaled = query_ref[group, :HEAD_DIM, lanes].astype(jnp.float32) * score_scale
            query_rows[index] = jnp.transpose(scaled).astype(jnp.bfloat16)
            return 0

        lax.fori_loop(0, count, prepare, 0)

    keys_t = pair_ref[0, :HEAD_DIM, :]
    keys = jnp.transpose(keys_t.astype(jnp.float32)).astype(jnp.bfloat16)
    values = jnp.transpose(pair_ref[0, HEAD_DIM:, :].astype(jnp.float32)).astype(jnp.bfloat16)
    base, key_min, key_max = (plan_ref[kind * blocks + step] for kind in (2, 3, 4))
    key_acc[...] = jnp.zeros_like(key_acc)
    value_acc[...] = jnp.zeros_like(value_acc)

    def one_tile(index, _):
        group = lax.div(index, per_query)
        lanes = pl.ds(pl.multiple_of(lax.rem(index, per_query) * tile, tile), tile)
        queries_t = query_ref[group, :HEAD_DIM, lanes] * jnp.bfloat16(score_scale)
        grads_t = grad_ref[group, :, lanes]
        inside = (key_max <= plan_ref[5 * blocks + index]) & (
            key_min >= plan_ref[5 * blocks + count + index]
        )

        def update(masked):
            scores = jnp.dot(keys, queries_t, preferred_element_type=jnp.float32)
            weights = jnp.exp(scores - total_ref[index])
            if masked:
                allowed = key_allowed(
                    column_ref, rows_ref, step, per_key, key_tile, base, group, lanes
                )
                weights = jnp.where(allowed, weights, 0.0)
            grad_weights = jnp.dot(values, grads_t, preferred_element_type=jnp.float32)
            grad_scores = (weights * (grad_weights - inner[index])).astype(jnp.bfloat16)
            value_acc[...] += jnp.dot(
                weights.astype(jnp.bfloat16), grad_rows[index], preferred_element_type=jnp.float32
            )
            key_acc[...] += jnp.dot(
                grad_scores, query_rows[index], preferred_element_type=jnp.float32
            )
            acc[index] += jnp.dot(keys_t, grad_scores, preferred_element_type=jnp.float32)

        pl.when(inside)(lambda: update(False))
        pl.when(jnp.logical_not(inside))(lambda: update(True))
        return 0

    lax.fori_loop(plan_ref[step], plan_ref[blocks + step], one_tile, 0)
    pair_grad_ref[0, :HEAD_DIM, :] = jnp.transpose(key_acc[...]).astype(jnp.bfloat16)
    pair_grad_ref[0, HEAD_DIM:, :] = jnp.transpose(value_acc[...]).astype(jnp.bfloat16)

    @pl.when(step == blocks - 1)
    def _():
        def finish(index, _):
            group = lax.div(index, per_query)
            lanes = pl.ds(pl.multiple_of(lax.rem(index, per_query) * tile, tile), tile)
            query_grad_ref[group, :, lanes] = (acc[index] * score_scale).astype(jnp.bfloat16)
            return 0

        lax.fori_loop(0, count, finish, 0)


def attention_call(kernel, queries, pairs, plan, more, outs, scratch, flops):
    numbers, rows, column = plan
    groups, _, width = queries.shape
    key_groups, _, key_width = pairs.shape
    tile, key_tile = tile_of(width), tile_of(key_width)
    per_query, per_key = width // tile, key_width // key_tile
    blocks = key_groups * per_key
    count = groups * per_query

    def whole(array):
        return pl.BlockSpec(array.shape, lambda step, plan_ref: (0,) * array.ndim)

    pair_spec = pl.BlockSpec(
        (1, 2 * HEAD_DIM, key_tile),
        lambda step, plan_ref: (lax.div(step, per_key), 0, lax.rem(step, per_key)),
    )
    out_shapes, out_specs = [], []
    for kind in outs:
        if kind == "pairs":
            out_shapes.append(jax.ShapeDtypeStruct(pairs.shape, jnp.bfloat16))
            out_specs.append(pair_spec)
        else:
            shape = (count, 1, tile) if kind == "total" else (groups, HEAD_DIM, width)
            dtype = jnp.bfloat16 if kind == "grads" else jnp.float32
            out_shapes.append(jax.ShapeDtypeStruct(shape, dtype))
            out_specs.append(whole(out_shapes[-1]))
    sizes = {
        "acc": pltpu.VMEM((count, HEAD_DIM, tile), jnp.float32),
        "row": pltpu.VMEM((count, 1, tile), jnp.float32),
        "rows": pltpu.VMEM((count, tile, HEAD_DIM), jnp.bfloat16),
        "keys": pltpu.VMEM((key_tile, HEAD_DIM), jnp.float32),
    }
    pairs_near = groups * width * min(key_groups * key_width, 2304)
    return pl.pallas_call(
        functools.partial(kernel, (blocks, groups, per_query, per_key, tile, key_tile)),
        out_shape=out_shapes,
        grid_spec=pltpu.PrefetchScalarGridSpec(
            num_scalar_prefetch=1,
            grid=(blocks,),
            in_specs=[whole(queries), pair_spec, whole(rows), whole(column)]
            + [whole(array) for array in more],
            out_specs=out_specs,
            scratch_shapes=[sizes[name] for name in scratch],
        ),
        compiler_params=pltpu.CompilerParams(
            dimension_semantics=("arbitrary",), vmem_limit_bytes=56 * 2**20
        ),
        cost_estimate=pl.CostEstimate(
            flops=flops * pairs_near * HEAD_DIM,
            bytes_accessed=4 * queries.size + 4 * pairs.size,
            transcendentals=pairs_near,
        ),
    )(numbers, queries, pairs, rows, column, *more)


def attend(queries, pairs, plan):
    return attention_call(
        forward_kernel, queries, pairs, plan, (), ("out", "total"), ("acc", "row", "row"), 16
    )


def attend_back(queries, pairs, plan, grads, out, total):
    return attention_call(
        backward_kernel,
        queries,
        pairs,
        plan,
        (grads, out, total),
        ("grads", "pairs"),
        ("acc", "row", "rows", "rows", "keys", "keys"),
        40,
    )


def aligned_weights(stacked, tensor_size, tensor_index, head_rows):
    slab = stacked.shape[1]
    extra = slab - head_rows
    most = (tensor_size - 1) * extra
    before = lax.ppermute(stacked[:, slab - most :], "tensor", line(tensor_size, 1))
    joined = jnp.concatenate((before, stacked), axis=1)
    own = lax.dynamic_slice_in_dim(joined, most - extra * tensor_index, head_rows, 1)
    final = stacked[:, slab - HEAD_DIM :]
    last = jnp.where(tensor_index == tensor_size - 1, final, jnp.zeros_like(final))
    for target in range(tensor_size - 1):
        last = last + lax.ppermute(final, "tensor", [(tensor_size - 1, target)])
    return own, last


def slab_rows(own, last, slab, tensor_size, tensor_index):
    extra = slab - own.shape[1]
    most = (tensor_size - 1) * extra
    after = lax.ppermute(own[:, :most], "tensor", line(tensor_size, -1))
    after = jnp.pad(after, ((0, 0), (0, HEAD_DIM - most), (0, 0)))
    after = jnp.where(tensor_index == tensor_size - 1, last, after)
    joined = jnp.concatenate((own, after), axis=1)
    return lax.dynamic_slice_in_dim(joined, extra * tensor_index, slab, 1)


def local(
    tokens_in,
    ln1_gain,
    ln1_bias,
    w_qkv,
    b_qv,
    w_out,
    b_out,
    ln2_gain,
    ln2_bias,
    w_up,
    b_up,
    w_down,
    b_down,
    seq_lengths,
    cotangent,
):
    tensor_size = lax.axis_size("tensor")
    tensor_index = lax.axis_index("tensor")
    dp_size = lax.axis_size("dp")
    dp_index = lax.axis_index("dp")
    flat_index = dp_index * tensor_size + tensor_index
    rows, width = tokens_in.shape
    slab = w_qkv.shape[1]
    unit_slab = w_up.shape[1]
    slots = (HEADS - 1) // tensor_size
    members = dp_size // slots
    member = lax.rem(dp_index, members)
    part = rows // members
    lanes = tensor_size * part
    head_rows = slots * HEAD_DIM
    low = jnp.bfloat16
    seq_ends = jnp.cumsum(seq_lengths)
    gain_one = ln1_gain.astype(jnp.float32)
    shift_one = ln1_bias.astype(jnp.float32)
    gain_two = ln2_gain.astype(jnp.float32)
    shift_two = ln2_bias.astype(jnp.float32)

    stream = tokens_in.astype(jnp.float32)
    normed_one, inv_one, pre_one = norm_forward(stream, gain_one, shift_one)
    pre_one = pre_one.astype(low)
    wide_one = gather_tensor(pre_one.reshape(members, part, width), 1)
    wide_one = wide_one.reshape(members, lanes, width)
    stacked = jnp.concatenate((w_qkv, w_out[None]), axis=0)
    own_w, last_w = aligned_weights(stacked, tensor_size, tensor_index, head_rows)
    head_w = own_w.reshape(4, slots, HEAD_DIM, width).transpose(1, 0, 2, 3)
    qkv_w = head_w[:, :3].reshape(slots, 3 * HEAD_DIM, width)
    out_w = head_w[:, 3]
    last_qkv_w = last_w[:3].reshape(3 * HEAD_DIM, width)
    last_out_w = last_w[3]
    bias_full = jnp.stack((b_qv[0], jnp.zeros_like(b_qv[0]), b_qv[1])).astype(jnp.float32)
    own_bias = lax.dynamic_slice_in_dim(bias_full, tensor_index * head_rows, head_rows, 1)
    own_bias = own_bias.reshape(3, slots, HEAD_DIM).transpose(1, 0, 2).reshape(slots, -1)
    last_bias = bias_full[:, width - HEAD_DIM :].reshape(-1)

    offsets = jnp.arange(tensor_size, dtype=jnp.int32)[:, None] * rows
    offsets = (offsets + jnp.arange(part, dtype=jnp.int32)[None]).reshape(-1)
    dp_starts = jnp.arange(dp_size, dtype=jnp.int32) * (tensor_size * rows)
    query_pos = dp_starts[:, None] + offsets[None] + member * part
    halves = jnp.arange(members, dtype=jnp.int32)
    if members == 2:
        halves = lax.rem(member + halves, 2)
    key_base = (halves[:, None] * part + dp_starts[None]).reshape(-1)
    plan = attention_plan(query_pos, key_base, offsets, seq_ends)
    row_range = jnp.arange(rows, dtype=jnp.int32)
    reach = min(REACH + 1, dp_size * tensor_size)
    window = jnp.clip(flat_index - REACH, 0, dp_size * tensor_size - reach)
    last_base = (window + jnp.arange(reach, dtype=jnp.int32)) * rows
    last_plan = attention_plan(
        (flat_index * rows + row_range)[None], last_base, row_range, seq_ends
    )

    qkv = jnp.einsum("cfd,gtd->cgft", qkv_w, wide_one, preferred_element_type=jnp.float32)
    qkv = (qkv + own_bias[:, None, :, None]).astype(low).reshape(dp_size, 3 * HEAD_DIM, lanes)
    qkv = lax.all_to_all(qkv, "dp", split_axis=0, concat_axis=0, tiled=True)
    last_qkv = jnp.einsum("fd,td->ft", last_qkv_w, pre_one, preferred_element_type=jnp.float32)
    last_qkv = (last_qkv + last_bias[:, None]).astype(low)[None]
    last_pairs = lax.all_gather(last_qkv[:, HEAD_DIM:], everywhere, axis=0, tiled=True)
    last_pairs = lax.dynamic_slice_in_dim(last_pairs, window, reach, 0)

    swap = [(i, i ^ 1) for i in range(dp_size)]
    sharing = [list(range(i, i + members)) for i in range(0, dp_size, members)]
    own_pairs = qkv[:, HEAD_DIM:]
    if members == 2:
        pairs = jnp.concatenate((own_pairs, lax.ppermute(own_pairs, "dp", swap)), axis=0)
    else:
        pairs = lax.all_gather(own_pairs, "dp", axis_index_groups=sharing, axis=0, tiled=True)
    mixed, total = attend(qkv, pairs, plan)
    last_mixed, last_total = attend(last_qkv, last_pairs, last_plan)
    attended = lax.all_to_all(mixed.astype(low), "dp", split_axis=0, concat_axis=0, tiled=True)
    attended = attended.reshape(slots, members, HEAD_DIM, lanes)
    last_attended = last_mixed[0].astype(low)

    contract_first = (((0,), (0,)), ((), ()))
    contract_cols = (((1,), (1,)), ((), ()))
    branch = jnp.einsum("cgft,cfd->gtd", attended, out_w, preferred_element_type=jnp.float32)
    branch = branch.astype(low).reshape(members, tensor_size, part, width).transpose(1, 0, 2, 3)
    branch = scatter_tensor(branch.reshape(tensor_size, rows, width))
    last_branch = lax.dot_general(
        last_attended, last_out_w, contract_first, preferred_element_type=jnp.float32
    )
    stream_one = stream + (branch + last_branch) + b_out.astype(jnp.float32)
    normed_two, inv_two, pre_two = norm_forward(stream_one, gain_two, shift_two)
    wide_two = gather_tensor(pre_two.astype(low), 0).reshape(tensor_size * rows, width)
    hidden_pre = jnp.dot(wide_two, w_up, preferred_element_type=jnp.float32) + b_up.astype(
        jnp.float32
    )
    gelu_out, gelu_pull = jax.vjp(
        lambda hidden_in: jax.nn.gelu(hidden_in, approximate=True), hidden_pre
    )
    activated = gelu_out.astype(low)
    down_sum = jnp.dot(activated, w_down, preferred_element_type=jnp.float32)
    down_sum = scatter_tensor(down_sum.reshape(tensor_size, rows, width))
    block_out = (stream_one + down_sum + b_down.astype(jnp.float32)).astype(low)

    grad_two = cotangent.astype(jnp.float32)
    grad_down_bias = jnp.sum(grad_two, axis=0)
    wide_grad = gather_tensor(cotangent, 0).reshape(tensor_size * rows, width)
    grad_act = lax.dot_general(wide_grad, w_down, contract_cols, preferred_element_type=jnp.float32)
    grad_down = lax.dot_general(
        activated, wide_grad, contract_first, preferred_element_type=jnp.float32
    )
    grad_hidden = gelu_pull(grad_act)[0].astype(low)
    grad_up_part = jnp.sum(grad_hidden.astype(jnp.float32), axis=0)
    grad_up = lax.dot_general(
        wide_two, grad_hidden, contract_first, preferred_element_type=jnp.float32
    )
    grad_normed_two = lax.dot_general(
        grad_hidden, w_up, contract_cols, preferred_element_type=jnp.float32
    )
    grad_normed_two = scatter_tensor(grad_normed_two.reshape(tensor_size, rows, width))
    grad_res_two, grad_gain_two, grad_shift_two = norm_backward(
        grad_normed_two, normed_two, inv_two, gain_two
    )
    grad_stream_one = grad_two + grad_res_two
    grad_branch = grad_stream_one.astype(low)
    grad_out_bias = jnp.sum(grad_branch.astype(jnp.float32), axis=0)
    wide_branch = gather_tensor(grad_branch.reshape(members, part, width), 1)
    wide_branch = wide_branch.reshape(members, lanes, width)
    last_grads = lax.dot_general(
        last_out_w, grad_branch, contract_cols, preferred_element_type=jnp.float32
    )
    last_grads = last_grads.astype(low)[None]
    grads = jnp.einsum("cfd,gtd->cgft", out_w, wide_branch, preferred_element_type=jnp.float32)
    grads = grads.astype(low).reshape(dp_size, HEAD_DIM, lanes)
    grads = lax.all_to_all(grads, "dp", split_axis=0, concat_axis=0, tiled=True)
    last_query_grad, last_pair_grad = attend_back(
        last_qkv, last_pairs, last_plan, last_grads, last_mixed, last_total
    )
    last_pair_grad = lax.dynamic_update_slice_in_dim(
        jnp.zeros((dp_size * tensor_size, 2 * HEAD_DIM, rows), low), last_pair_grad, window, 0
    )
    last_pair_grad = lax.psum_scatter(last_pair_grad, everywhere, scatter_dimension=0, tiled=True)
    query_grad, pair_grad = attend_back(qkv, pairs, plan, grads, mixed, total)
    pair_grad = pair_grad.reshape(members, dp_size, 2 * HEAD_DIM, lanes)
    if members == 2:
        other_grad = lax.ppermute(pair_grad[1], "dp", swap)
        pair_sum = pair_grad[0].astype(jnp.float32) + other_grad.astype(jnp.float32)
    else:
        pair_grad = lax.all_to_all(
            pair_grad, "dp", 0, 0, axis_index_groups=sharing, tiled=True
        )
        pair_sum = jnp.sum(pair_grad.astype(jnp.float32), axis=0)
    qkv_grad = jnp.concatenate((query_grad, pair_sum.astype(low)), axis=1)
    qkv_grad = lax.all_to_all(qkv_grad, "dp", split_axis=0, concat_axis=0, tiled=True)
    qkv_grad = qkv_grad.reshape(slots, members, 3 * HEAD_DIM, lanes)
    last_qkv_grad = jnp.concatenate((last_query_grad[0], last_pair_grad[0]), axis=0)

    grad_normed_one = jnp.einsum(
        "cgft,cfd->gtd", qkv_grad, qkv_w, preferred_element_type=jnp.float32
    )
    grad_normed_one = grad_normed_one.astype(low).reshape(members, tensor_size, part, width)
    grad_normed_one = scatter_tensor(
        grad_normed_one.transpose(1, 0, 2, 3).reshape(tensor_size, rows, width)
    )
    last_normed_one = lax.dot_general(
        last_qkv_grad, last_qkv_w, contract_first, preferred_element_type=jnp.float32
    )
    grad_normed_one = grad_normed_one + last_normed_one
    grad_res_one, grad_gain_one, grad_shift_one = norm_backward(
        grad_normed_one, normed_one, inv_one, gain_one
    )
    grad_input = grad_stream_one + grad_res_one

    own_qkv_grad = jnp.einsum(
        "cgft,gtd->cfd", qkv_grad, wide_one, preferred_element_type=jnp.float32
    )
    own_qkv_grad = own_qkv_grad.reshape(slots, 3, HEAD_DIM, width).transpose(1, 0, 2, 3)
    own_qkv_grad = own_qkv_grad.reshape(3, head_rows, width).astype(low)
    own_out_grad = jnp.einsum(
        "cgft,gtd->cfd", attended, wide_branch, preferred_element_type=jnp.float32
    )
    own_out_grad = own_out_grad.reshape(1, head_rows, width).astype(low)
    last_qkv_part = jnp.dot(last_qkv_grad, pre_one, preferred_element_type=jnp.float32)
    last_out_part = jnp.dot(last_attended, grad_branch, preferred_element_type=jnp.float32)
    last_parts = jnp.concatenate((last_qkv_part, last_out_part), axis=0).astype(low)
    last_parts = lax.psum(last_parts, "tensor").reshape(4, HEAD_DIM, width)
    grad_qkv = slab_rows(own_qkv_grad, last_parts[:3], slab, tensor_size, tensor_index)
    grad_out = slab_rows(own_out_grad, last_parts[3:], slab, tensor_size, tensor_index)[0]

    qkv_sums = jnp.sum(qkv_grad.astype(jnp.float32), axis=(1, 3)).reshape(slots, 3, HEAD_DIM)
    qkv_sums = qkv_sums.transpose(1, 0, 2).reshape(3, head_rows)
    last_sums = jnp.sum(last_qkv_grad.astype(jnp.float32), axis=1).reshape(3, HEAD_DIM)
    sums_full = jnp.zeros((3, width), jnp.float32).at[:, width - HEAD_DIM :].set(last_sums)
    sums_full = lax.dynamic_update_slice_in_dim(
        sums_full, qkv_sums, tensor_index * head_rows, 1
    )
    grad_qv_bias = jnp.stack((sums_full[0], sums_full[2]))
    up_full = lax.dynamic_update_slice_in_dim(
        jnp.zeros((unit_slab * tensor_size,), jnp.float32),
        grad_up_part,
        tensor_index * unit_slab,
        0,
    )
    early = lax.psum(
        (grad_out_bias, grad_gain_two, grad_shift_two, up_full, grad_down_bias), everywhere
    )
    late = lax.psum((grad_gain_one, grad_shift_one, grad_qv_bias), everywhere)
    grad_up_bias = lax.dynamic_slice_in_dim(early[3], tensor_index * unit_slab, unit_slab, 0)
    return (
        block_out,
        grad_input,
        late[0],
        late[1],
        scatter_dp(grad_qkv, 2),
        late[2],
        scatter_dp(grad_out, 1),
        early[0],
        early[1],
        early[2],
        scatter_dp(grad_up, 0),
        grad_up_bias,
        scatter_dp(grad_down, 1),
        early[4],
    )


def solution(mesh):
    in_specs = (
        P(("dp", "tensor"), None),
        P(),
        P(),
        P(None, "tensor", None),
        P(),
        P("tensor", None),
        P(),
        P(),
        P(),
        P(None, "tensor"),
        P("tensor"),
        P("tensor", None),
        P(),
        P(),
        P(("dp", "tensor"), None),
    )
    out_specs = (
        P(("dp", "tensor"), None),
        P(("dp", "tensor"), None),
        P(),
        P(),
        P(None, "tensor", "dp"),
        P(),
        P("tensor", "dp"),
        P(),
        P(),
        P(),
        P("dp", "tensor"),
        P("tensor"),
        P("tensor", "dp"),
        P(),
    )
    return jax.shard_map(local, mesh=mesh, in_specs=in_specs, out_specs=out_specs, check_vma=False)
```

time: 2400 us -> 1150 us (0.48)
  waiting for transfers between devices: 1540 us -> 423 us
  local copies, waits for them, and re-layouts: 261 us -> 108 us
  Pallas kernels: 0 us -> 143 us
  other arithmetic: 169 us -> 77.4 us
  loops' own time: 47.1 us -> 0 us
  blocking collectives: 89.4 us -> 131 us
  matrix products: 123 us -> 83.8 us
  starting transfers between devices: 116 us -> 145 us
    ppermute x22 -> x32, waiting for transfers between devices: 790 us -> 186 us  [the longest x12 158 us: gather_tensor(): down.append(lax.ppermute(down[-1], 'tensor', line(count, -1)))]
    unnamed x20 -> x9, waiting for transfers between devices: 357 us -> 57.3 us
    all_gather x4 -> x1, waiting for transfers between devices: 232 us -> 0.01 us  [local(): lax.all_gather(last_qkv[:, HEAD_DIM:], everywhere, axis=0, tiled=True)]
    pallas_call x0 -> x4, Pallas kernels: none -> 143 us  [attention_call(): pl.pallas_call(functools.partial(kernel, (blocks, groups, per_query, per_...]
    all_to_all x3 -> x6, waiting for transfers between devices: 166 us -> 80.6 us  [the longest x3 30.4 us: scatter_tensor(): lax.all_to_all(partial_sum.astype(jnp.bfloat16), 'tensor', split_axis=0,...]
    convert_element_type x31 -> x12, other arithmetic: 71 us -> 14.5 us  [the longest x4 5.97 us: scatter_dp(): return lax.psum_scatter(partial_sum.astype(jnp.bfloat16), 'dp', scatter_d...]
    reduce_scatter x0 -> x1, waiting for transfers between devices: none -> 55.5 us  [local(): lax.psum_scatter(last_pair_grad, everywhere, scatter_dimension=0, tiled=T...]
    another operation x39 -> x0, loops' own time: 47.1 us -> none  [the longest x1 16.2 us: attention_forward(): lax.fori_loop(0, REACH + 1, stats_step, (start_max, jnp.zeros(heads_shape...]
  transfers between devices with their start and end apart: 37 -> 44, of which waited for: 33 -> 22; matrix products, arithmetic and copies ran while one was open for 13% -> 18% of each run, Pallas kernels for 0% -> 13%
where the time goes in v1:
time: 1150 us; the launch traced here: 1130 us
  waiting for transfers between devices  423 us (37%)
  starting transfers between devices  145 us (13%)
  Pallas kernels  143 us (12%)
  blocking collectives  131 us (11%)
  local copies, waits for them, and re-layouts  108 us (9%)
  matrix products  83.8 us (7%)
  other arithmetic  77.4 us (7%)
  between operations  16.3 us (1%)
    ppermute x12, waiting for transfers between devices, gather_tensor(): down.append(lax.ppermute(down[-1], 'tensor', line(count, -1)))  158 us
    pallas_call x4, Pallas kernels, attention_call(): pl.pallas_call(functools.partial(kernel, (blocks, groups, per_query, per_...  143 us
    ppermute x12, starting transfers between devices, gather_tensor(): up.append(lax.ppermute(up[-1], 'tensor', line(count, 1)))  76.9 us
    all_to_all x1, blocking collectives, scatter_tensor(): lax.all_to_all(partial_sum.astype(jnp.bfloat16), 'tensor', split_axis=0,...  73 us
    unnamed x9, waiting for transfers between devices  57.3 us
    reduce_scatter x1, waiting for transfers between devices, local(): lax.psum_scatter(last_pair_grad, everywhere, scatter_dimension=0, tiled=T...  55.5 us
    psum x1, waiting for transfers between devices, local(): last_parts = lax.psum(last_parts, 'tensor').reshape(4, HEAD_DIM, width)  42.9 us
    psum x1, blocking collectives, local(): late = lax.psum((grad_gain_one, grad_shift_one, grad_qv_bias), everywhere)  41.8 us
  transfers between devices with their start and end apart: 44, of which 22 were waited for; matrix products, arithmetic and copies ran while one was open for 18% of the time, Pallas kernels for 13%

profile of v1, /device:TPU:0, one launch (start us, length us, event | category | flops | bytes accessed | tf_op | source)
XLA Modules:
  0.0 1126.5 jit_solution(11791171429266853016)
XLA Ops:
  16.4 6.5 collective-permute-start
  22.9 17.0 %collective-permute-done.1 = bf16[2,192,1088]{2,1,0:T(8,128)(2,1)S(1)} collective-permute-done((bf16[2,192,1088]{2,1,0:T(8,128)(2,1)}, bf16[2,192,1088]{2,1,0:T(8,128)(2,1)S(1)}, u32[]{:S(2)}, u32[]{:S(2)}) %collective-permute-start.1) | collective-permute-done | bytes 835616 | tf_op jit(solution)/shard_map/ppermute | solution.py:31
  43.9 5.3 collective-permute-start.6
  49.4 3.8 collective-permute-start.4
  53.2 10.5 collective-permute-done.2
  69.1 7.3 collective-permute-done.4
  76.3 4.4 collective-permute-start.5
  80.8 5.0 collective-permute-done.3
  88.6 9.6 collective-permute-done.5
  98.5 3.5 fusion.15
  103.6 4.4 all-to-all-start
  116.4 21.0 %all-to-all-done.query_ref = bf16[8,192,768]{2,1,0:T(8,128)(2,1)} async-done(((bf16[8,192,768]{2,1,0:T(8,128)(2,1)}), bf16[8,192,768]{2,1,0:T(8,128)(2,1)}, u32[]{:S(2)}, u32[]{:S(2)}) %all-to-all-start) | async-done | bytes 2359328 | tf_op jit(solution)/shard_map/all_to_all | solution.py:433
  147.7 3.9 pad_maximum_fusion.pair_ref
  151.6 57.2 %shard_map.254 = (f32[8,64,768]{2,1,0:T(8,128)}, f32[16,1,384]{2,1,0:T(1,128)}) custom-call(s32[192]{0:T(256)} %concatenate.33.plan_ref, bf16[8,192,768]{2,1,0:T(8,128)(2,1)} %all-to-all-done.query_ref, bf16[16,128,768]{2,1,0:T(8,128)(2,1)} %pad_maximum_fusion.pair_ref, s32[8,2,768]{2,1,0:T(2,128)} %pad_add_fusion.rows_ref, s32[768,1]{1,0:T(8,128)} %add.649.column_ref), custom_call_target="tpu_custom_call" | custom-call | flops 14495514624 | bytes 11010048 | tf_op jit(solution)/shard_map/pallas_call | solution.py:294
  210.3 16.0 %all_to_all.40 = bf16[8,64,768]{2,1,0:T(8,128)(2,1)S(1)} all-to-all(bf16[8,64,768]{2,1,0:T(8,128)(2,1)S(1)} %convert_element_type.193), channel_id=1, replica_groups=mesh['dp'=8,'tensor'=4] {'dp'}, dimensions={0} | all-to-all | bytes 1572864 | tf_op jit(solution)/shard_map/all_to_all | solution.py:448
  227.2 4.0 bitcast_convert_fusion.1
  231.2 5.6 copy.336
  236.7 4.2 copy.337
  240.9 5.7 copy.338
  246.6 13.8 %all-to-all-start.2 = ((bf16[4,384,1088]{1,2,0:T(8,128)(2,1)}), bf16[4,384,1088]{1,2,0:T(8,128)(2,1)}, u32[]{:S(2)}, u32[]{:S(2)}) async-start(bf16[4,384,1088]{1,2,0:T(8,128)(2,1)} %copy.338), calls=%async_computation.2 | async-start | bytes 6684672 | tf_op jit(solution)/shard_map/all_to_all | solution.py:43
  261.8 7.1 collective-permute-start.17
  269.6 66.1 %collective-permute-done.18 = bf16[384,1088]{0,1:T(8,128)(2,1)} collective-permute-done((bf16[384,1088]{0,1:T(8,128)(2,1)S(1)}, bf16[384,1088]{0,1:T(8,128)(2,1)}, u32[]{:S(2)}, u32[]{:S(2)}) %collective-permute-start.18) | collective-permute-done | bytes 835616 | tf_op jit(solution)/shard_map/ppermute | solution.py:31
  337.0 21.1 %collective-permute-start.21 = (bf16[384,1088]{0,1:T(8,128)(2,1)}, bf16[384,1088]{0,1:T(8,128)(2,1)}, u32[]{:S(2)}, u32[]{:S(2)}) collective-permute-start(bf16[384,1088]{0,1:T(8,128)(2,1)} %collective-permute-done.17), channel_id=1, source_target_pairs={{0,1},{1,2},{2,3},{4,5},{5,6},{6,7},{8,9},{9,10},{10,11},{12,13},{... | collective-permute-start | bytes 2506760 | tf_op jit(solution)/shard_map/ppermute | solution.py:30
  368.5 4.9 collective-permute-done.19
  374.6 5.5 collective-permute-start.22
  383.2 8.3 shard_map.255
  398.1 4.2 collective-permute-start.11
  409.5 8.3 collective-permute-done.11
  417.8 5.3 collective-permute-start.15
  437.7 5.3 collective-permute-start.16
  448.8 3.9 collective-permute-done.13
  462.5 8.8 collective-permute-done.14
  480.1 6.8 convolution_add_fusion
  486.9 10.5 convert_reduce_fusion.2
  497.4 4.8 convolution_convert_fusion
  502.5 73.0 %all_to_all.41 = bf16[4,384,1088]{1,2,0:T(8,128)(2,1)S(1)} all-to-all(bf16[4,384,1088]{1,2,0:T(8,128)(2,1)S(1)} %bitcast.211), channel_id=1, replica_groups=mesh['dp'=8,'tensor'=4] {'tensor'}, dimensions={0} | all-to-all | bytes 6684672 | tf_op jit(solution)/shard_map/all_to_all | solution.py:43
  583.5 4.6 collective-permute-start.23
  588.1 15.1 %collective-permute-done.24 = bf16[2,192,1088]{2,1,0:T(8,128)(2,1)S(1)} collective-permute-done((bf16[2,192,1088]{2,1,0:T(8,128)(2,1)}, bf16[2,192,1088]{2,1,0:T(8,128)(2,1)S(1)}, u32[]{:S(2)}, u32[]{:S(2)}) %collective-permute-start.24) | collective-permute-done | bytes 835616 | tf_op jit(solution)/shard_map/ppermute | solution.py:31
  604.6 4.6 collective-permute-start.27
  609.2 14.0 %collective-permute-done.25 = bf16[2,192,1088]{2,1,0:T(8,128)(2,1)S(1)} collective-permute-done((bf16[2,192,1088]{2,1,0:T(8,128)(2,1)S(1)}, bf16[2,192,1088]{2,1,0:T(8,128)(2,1)S(1)}, u32[]{:S(2)}, u32[]{:S(2)}) %collective-permute-start.25) | collective-permute-done | bytes 835616 | tf_op jit(solution)/shard_map/ppermute | solution.py:31
  625.1 4.6 collective-permute-start.28
  629.7 12.5 %collective-permute-done.26 = bf16[2,192,1088]{2,1,0:T(8,128)(2,1)S(1)} collective-permute-done((bf16[2,192,1088]{2,1,0:T(8,128)(2,1)S(1)}, bf16[2,192,1088]{2,1,0:T(8,128)(2,1)S(1)}, u32[]{:S(2)}, u32[]{:S(2)}) %collective-permute-start.26) | collective-permute-done | bytes 835616 | tf_op jit(solution)/shard_map/ppermute | solution.py:31
  647.9 5.7 all-to-all-start.5
  653.7 9.4 convolution_convert_fusion.3
  666.3 66.9 %shard_map.256 = (bf16[8,64,768]{2,1,0:T(8,128)(2,1)}, bf16[16,128,768]{2,1,0:T(8,128)(2,1)}) custom-call(s32[192]{0:T(256)} %concatenate.33.plan_ref, bf16[8,192,768]{2,1,0:T(8,128)(2,1)} %all-to-all-done.query_ref, bf16[16,128,768]{2,1,0:T(8,128)(2,1)} %pad_maximum_fusion.pair_ref, s32[8,2,768]{2,1,0:T(2,128)} %pad_add_fusion.rows_ref, ...), custom_call_target="tpu_custom_call" | custom-call | flops 36238786560 | bytes 11010048 | tf_op jit(solution)/shard_map/pallas_call | solution.py:294
  736.0 10.1 convolution_convert_fusion.2
  750.1 4.8 all-to-all-start.6
  754.9 7.9 convolution_convert_fusion.1
  764.9 26.2 %all-to-all-done.6 = bf16[8,192,768]{2,1,0:T(8,128)(2,1)} async-done(((bf16[8,192,768]{2,1,0:T(8,128)(2,1)}), bf16[8,192,768]{2,1,0:T(8,128)(2,1)}, u32[]{:S(2)}, u32[]{:S(2)}) %all-to-all-start.6) | async-done | bytes 2359328 | tf_op jit(solution)/shard_map/all_to_all | solution.py:523
  791.1 4.8 all-to-all-start.3
  798.4 10.1 shard_map.257
  819.9 6.8 bitcast_convert_fusion
  826.7 5.6 copy.360
  832.3 4.1 copy.361
  836.4 5.8 copy.362
  842.2 30.4 %all-to-all-done.3 = bf16[4,384,1088]{1,2,0:T(8,128)(2,1)} async-done(((bf16[4,384,1088]{1,2,0:T(8,128)(2,1)}), bf16[4,384,1088]{1,2,0:T(8,128)(2,1)}, u32[]{:S(2)}, u32[]{:S(2)}) %all-to-all-start.3) | async-done | bytes 3342368 | tf_op jit(solution)/shard_map/all_to_all | solution.py:43
  872.6 5.5 all-to-all-start.7
  879.6 3.5 fusion.12
  885.8 55.5 %reduce-scatter.10.cloned.1.call-done = bf16[1,128,384]{2,1,0:T(8,128)(2,1)} async-done(((bf16[32,128,384]{2,1,0:T(8,128)(2,1)}), bf16[1,128,384]{2,1,0:T(8,128)(2,1)}) %reduce-scatter.10.cloned.1.call-update) | async-done | bytes 98320 | tf_op jit(solution)/shard_map/reduce_scatter | solution.py:511
  943.6 5.9 fusion.10
  952.3 42.9 %all-reduce.12.cloned.1.call-done = bf16[256,1088]{1,0:T(8,128)(2,1)} async-done(((bf16[256,1088]{1,0:T(8,128)(2,1)}), bf16[256,1088]{1,0:T(8,128)(2,1)}) %all-reduce.12.cloned.1.call-update) | async-done | bytes 557072 | tf_op jit(solution)/shard_map/psum | solution.py:555
  1000.7 3.8 convert_reduce_fusion.4
  1007.6 57.2 %all-reduce.14.cloned.1.call-done = (bf16[3,272,1088]{2,1,0:T(8,128)(2,1)}, bf16[272,1088]{1,0:T(8,128)(2,1)}) async-done(((bf16[3,272,1088]{2,1,0:T(8,128)(2,1)}, bf16[272,1088]{1,0:T(8,128)(2,1)}), (bf16[3,272,1088]{2,1,0:T(8,128)(2,1)}, bf16[272,1088]{1,0:T(8,128)(2,1)})) %all-reduce.14.cloned.1.call-update) | async-done | bytes 2367504
  1077.0 41.8 %all-reduce.7 = (f32[1088]{0:T(1024)}, f32[1088]{0:T(1024)}, f32[2,1088]{1,0:T(2,128)}, f32[1088]{0:T(1024)}, f32[1088]{0:T(1024)}, /*index=5*/f32[1088]{0:T(1024)}, f32[4352]{0:T(1024)S(1)}, f32[1088]{0:T(1024)}) all-reduce(f32[1088]{0:T(1024)S(1)} %copy-done.60, ...), channel_id=1, replica_groups=mesh['dp'=8,'tensor'=4] {'dp','tensor'}, use_global_device_ids=true, to_apply=%region_21.22 | all-reduce | flops 13056 | bytes 104448 | tf_op jit(solution)/shard_map/psum | solution.py:576
  (393 shorter events, 187.8 us)
Async XLA Ops:
  7.2 479.7 %copy-start = (bf16[1088,1088]{1,0:T(8,128)(2,1)S(1)}, bf16[1088,1088]{1,0:T(8,128)(2,1)}, u32[]{:S(2)}) copy-start(bf16[1088,1088]{1,0:T(8,128)(2,1)} %param.28) | copy-start | bytes 7102468
  13.1 133.0 %copy-start.10 = (bf16[384,1088]{0,1:T(8,128)(2,1)}, bf16[384,1088]{0,1:T(8,128)(2,1)S(1)}, u32[]{:S(2)}) copy-start(bf16[384,1088]{0,1:T(8,128)(2,1)S(1)} %fusion.24) | copy-start | bytes 2506756
  13.1 36.3 %copy-start.52 = (bf16[2,1088]{1,0:T(2,128)(2,1)S(1)}, bf16[2,1088]{1,0:T(2,128)(2,1)}, u32[]{:S(2)}) copy-start(bf16[2,1088]{1,0:T(2,128)(2,1)} %param.21) | copy-start | bytes 13060
  15.1 24.8 %collective-permute-start.1 = (bf16[2,192,1088]{2,1,0:T(8,128)(2,1)}, bf16[2,192,1088]{2,1,0:T(8,128)(2,1)S(1)}, u32[]{:S(2)}, u32[]{:S(2)}) collective-permute-start(bf16[2,192,1088]{2,1,0:T(8,128)(2,1)} %bitcast.229), channel_id=1, source_target_pairs={{1,0},{2,1},{3,2},{5,4},{6,5},{7,6},{9,8},{10,9},{11,10},{13,12},{... | collective-permute-start | bytes 2506760 | tf_op jit(solution)/shard_map/ppermute | solution.py:31
  16.4 32.9 %collective-permute-start = (bf16[2,192,1088]{2,1,0:T(8,128)(2,1)}, bf16[2,192,1088]{2,1,0:T(8,128)(2,1)}, u32[]{:S(2)}, u32[]{:S(2)}) collective-permute-start(bf16[2,192,1088]{2,1,0:T(8,128)(2,1)} %bitcast.230), channel_id=1, source_target_pairs={{0,1},{1,2},{2,3},{4,5},{5,6},{6,7},{8,9},{9,10},{10,11},{12,13},{... | collective-permute-start | bytes 2506760 | tf_op jit(solution)/shard_map/ppermute | solution.py:30
  40.8 22.8 %collective-permute-start.2 = (bf16[2,192,1088]{2,1,0:T(8,128)(2,1)S(1)}, bf16[2,192,1088]{2,1,0:T(8,128)(2,1)}, u32[]{:S(2)}, u32[]{:S(2)}) collective-permute-start(bf16[2,192,1088]{2,1,0:T(8,128)(2,1)S(1)} %collective-permute-done.1), channel_id=1, source_target_pairs={{1,0},{2,1},{3,2},{5,4},{6,5},{7,6},{9,8},{10,9},{11,10},{13,12},{... | collective-permute-start | bytes 2506760 | tf_op jit(solution)/shard_map/ppermute | solution.py:31
  43.9 22.6 %collective-permute-start.6 = (bf16[4,48,1088]{2,1,0:T(8,128)(2,1)}, bf16[4,48,1088]{2,1,0:T(8,128)(2,1)}, u32[]{:S(2)}, u32[]{:S(2)}) collective-permute-start(bf16[4,48,1088]{2,1,0:T(8,128)(2,1)} %pad_maximum_fusion.4), channel_id=1, source_target_pairs={{0,1},{1,2},{2,3},{4,5},{5,6},{6,7},{8,9},{9,10},{10,11},{12,13},{... | collective-permute-start | bytes 1253384 | tf_op jit(solution)/shard_map/ppermute | solution.py:339
  49.4 27.0 %collective-permute-start.4 = (bf16[2,192,1088]{2,1,0:T(8,128)(2,1)}, bf16[2,192,1088]{2,1,0:T(8,128)(2,1)}, u32[]{:S(2)}, u32[]{:S(2)}) collective-permute-start(bf16[2,192,1088]{2,1,0:T(8,128)(2,1)} %collective-permute-done), channel_id=1, source_target_pairs={{0,1},{1,2},{2,3},{4,5},{5,6},{6,7},{8,9},{9,10},{10,11},{12,13},{... | collective-permute-start | bytes 2506760 | tf_op jit(solution)/shard_map/ppermute | solution.py:30
  63.6 22.1 %collective-permute-start.3 = (bf16[2,192,1088]{2,1,0:T(8,128)(2,1)}, bf16[2,192,1088]{2,1,0:T(8,128)(2,1)}, u32[]{:S(2)}, u32[]{:S(2)}) collective-permute-start(bf16[2,192,1088]{2,1,0:T(8,128)(2,1)} %collective-permute-done.2), channel_id=1, source_target_pairs={{1,0},{2,1},{3,2},{5,4},{6,5},{7,6},{9,8},{10,9},{11,10},{13,12},{... | collective-permute-start | bytes 2506760 | tf_op jit(solution)/shard_map/ppermute | solution.py:31
  69.1 29.4 %copy-start.29 = (bf16[4,3,64,1088]{3,2,1,0:T(8,128)(2,1)}, bf16[4,3,64,1088]{3,2,1,0:T(8,128)(2,1)S(1)}, u32[]{:S(2)}) copy-start(bf16[4,3,64,1088]{3,2,1,0:T(8,128)(2,1)S(1)} %copy.330) | copy-start | bytes 5013508
  69.1 29.1 %copy-start.34 = (bf16[2,192,1088]{2,1,0:T(8,128)(2,1)S(1)}, bf16[2,192,1088]{2,1,0:T(8,128)(2,1)}, u32[]{:S(2)}) copy-start(bf16[2,192,1088]{2,1,0:T(8,128)(2,1)} %copy-done.33) | copy-start | bytes 2506756
  76.3 21.8 %collective-permute-start.5 = (bf16[2,192,1088]{2,1,0:T(8,128)(2,1)}, bf16[2,192,1088]{2,1,0:T(8,128)(2,1)S(1)}, u32[]{:S(2)}, u32[]{:S(2)}) collective-permute-start(bf16[2,192,1088]{2,1,0:T(8,128)(2,1)} %collective-permute-done.4), channel_id=1, source_target_pairs={{0,1},{1,2},{2,3},{4,5},{5,6},{6,7},{8,9},{9,10},{10,11},{12,13},{... | collective-permute-start | bytes 2506760 | tf_op jit(solution)/shard_map/ppermute | solution.py:30
  103.6 33.8 %all-to-all-start = ((bf16[8,192,768]{2,1,0:T(8,128)(2,1)}), bf16[8,192,768]{2,1,0:T(8,128)(2,1)}, u32[]{:S(2)}, u32[]{:S(2)}) async-start(bf16[8,192,768]{2,1,0:T(8,128)(2,1)} %bitcast.218), calls=%async_computation | async-start | bytes 4718592 | tf_op jit(solution)/shard_map/all_to_all | solution.py:433
  108.0 7.3 copy-start.68
  108.0 272.1 %all-gather.2.cloned.1.call-start = ((), (), s32[]{:S(2)}) async-start(), calls=%async_computation.11 | async-start | bytes 3244032 | tf_op jit(solution)/shard_map/all_gather | solution.py:436
  110.0 34.1 %collective-permute-start.10 = (bf16[4,64,1088]{2,1,0:T(8,128)(2,1)}, bf16[4,64,1088]{2,1,0:T(8,128)(2,1)}, u32[]{:S(2)}, u32[]{:S(2)}) collective-permute-start(bf16[4,64,1088]{2,1,0:T(8,128)(2,1)} %pad_maximum_fusion.2), channel_id=1, source_target_pairs={{3,2},{7,6},{11,10},{15,14},{19,18},{23,22},{27,26},{31,30}} | collective-permute-start | bytes 1671176 | tf_op jit(solution)/shard_map/ppermute | solution.py:345
  111.5 32.6 %collective-permute-start.8 = (bf16[4,64,1088]{2,1,0:T(8,128)(2,1)}, bf16[4,64,1088]{2,1,0:T(8,128)(2,1)}, u32[]{:S(2)}, u32[]{:S(2)}) collective-permute-start(bf16[4,64,1088]{2,1,0:T(8,128)(2,1)} %pad_maximum_fusion.2), channel_id=1, source_target_pairs={{3,0},{7,4},{11,8},{15,12},{19,16},{23,20},{27,24},{31,28}} | collective-permute-start | bytes 1671176 | tf_op jit(solution)/shard_map/ppermute | solution.py:345
  112.7 31.3 %collective-permute-start.9 = (bf16[4,64,1088]{2,1,0:T(8,128)(2,1)}, bf16[4,64,1088]{2,1,0:T(8,128)(2,1)}, u32[]{:S(2)}, u32[]{:S(2)}) collective-permute-start(bf16[4,64,1088]{2,1,0:T(8,128)(2,1)} %pad_maximum_fusion.2), channel_id=1, source_target_pairs={{3,1},{7,5},{11,9},{15,13},{19,17},{23,21},{27,25},{31,29}} | collective-permute-start | bytes 1671176 | tf_op jit(solution)/shard_map/ppermute | solution.py:345
  140.1 7.6 collective-permute-start.7
  246.6 13.8 %copy-start.17 = (bf16[384,1088]{0,1:T(8,128)(2,1)S(1)}, bf16[384,1088]{0,1:T(8,128)(2,1)}, u32[]{:S(2)}) copy-start(bf16[384,1088]{0,1:T(8,128)(2,1)} %param.31) | copy-start | bytes 2506756
  246.6 112.7 %copy-start.62 = (bf16[1088]{0:T(1024)(128)(2,1)S(1)}, bf16[1088]{0:T(1024)(128)(2,1)}, u32[]{:S(2)}) copy-start(bf16[1088]{0:T(1024)(128)(2,1)} %param.23) | copy-start | bytes 6532
  246.6 112.7 %copy-start.63 = (bf16[1088]{0:T(1024)(128)(2,1)S(1)}, bf16[1088]{0:T(1024)(128)(2,1)}, u32[]{:S(2)}) copy-start(bf16[1088]{0:T(1024)(128)(2,1)} %param.24) | copy-start | bytes 6532
  246.6 112.7 %copy-start.64 = (bf16[1088]{0:T(1024)(128)(2,1)S(1)}, bf16[1088]{0:T(1024)(128)(2,1)}, u32[]{:S(2)}) copy-start(bf16[1088]{0:T(1024)(128)(2,1)} %param.25) | copy-start | bytes 6532
  246.6 112.7 %copy-start.65 = (bf16[1088]{0:T(1024)(128)(2,1)S(1)}, bf16[1088]{0:T(1024)(128)(2,1)}, u32[]{:S(2)}) copy-start(bf16[1088]{0:T(1024)(128)(2,1)} %param.27) | copy-start | bytes 6532
  246.6 144.9 %all-to-all-start.2 = ((bf16[4,384,1088]{1,2,0:T(8,128)(2,1)}), bf16[4,384,1088]{1,2,0:T(8,128)(2,1)}, u32[]{:S(2)}, u32[]{:S(2)}) async-start(bf16[4,384,1088]{1,2,0:T(8,128)(2,1)} %copy.338), calls=%async_computation.2 | async-start | bytes 6684672 | tf_op jit(solution)/shard_map/all_to_all | solution.py:43
  260.5 75.2 %collective-permute-start.18 = (bf16[384,1088]{0,1:T(8,128)(2,1)S(1)}, bf16[384,1088]{0,1:T(8,128)(2,1)}, u32[]{:S(2)}, u32[]{:S(2)}) collective-permute-start(bf16[384,1088]{0,1:T(8,128)(2,1)S(1)} %copy-done.17), channel_id=1, source_target_pairs={{1,0},{2,1},{3,2},{5,4},{6,5},{7,6},{9,8},{10,9},{11,10},{13,12},{... | collective-permute-start | bytes 2506760 | tf_op jit(solution)/shard_map/ppermute | solution.py:31
  261.8 75.2 %collective-permute-start.17 = (bf16[384,1088]{0,1:T(8,128)(2,1)S(1)}, bf16[384,1088]{0,1:T(8,128)(2,1)}, u32[]{:S(2)}, u32[]{:S(2)}) collective-permute-start(bf16[384,1088]{0,1:T(8,128)(2,1)S(1)} %copy-done.17), channel_id=1, source_target_pairs={{0,1},{1,2},{2,3},{4,5},{5,6},{6,7},{8,9},{9,10},{10,11},{12,13},{... | collective-permute-start | bytes 2506760 | tf_op jit(solution)/shard_map/ppermute | solution.py:30
  335.7 37.6 %collective-permute-start.19 = (bf16[384,1088]{0,1:T(8,128)(2,1)}, bf16[384,1088]{0,1:T(8,128)(2,1)}, u32[]{:S(2)}, u32[]{:S(2)}) collective-permute-start(bf16[384,1088]{0,1:T(8,128)(2,1)} %collective-permute-done.18), channel_id=1, source_target_pairs={{1,0},{2,1},{3,2},{5,4},{6,5},{7,6},{9,8},{10,9},{11,10},{13,12},{... | collective-permute-start | bytes 2506760 | tf_op jit(solution)/shard_map/ppermute | solution.py:31
  337.0 37.6 %collective-permute-start.21 = (bf16[384,1088]{0,1:T(8,128)(2,1)}, bf16[384,1088]{0,1:T(8,128)(2,1)}, u32[]{:S(2)}, u32[]{:S(2)}) collective-permute-start(bf16[384,1088]{0,1:T(8,128)(2,1)} %collective-permute-done.17), channel_id=1, source_target_pairs={{0,1},{1,2},{2,3},{4,5},{5,6},{6,7},{8,9},{9,10},{10,11},{12,13},{... | collective-permute-start | bytes 2506760 | tf_op jit(solution)/shard_map/ppermute | solution.py:30
  361.4 6.0 copy-start.25
  373.3 32.7 %collective-permute-start.20 = (bf16[384,1088]{0,1:T(8,128)(2,1)}, bf16[384,1088]{0,1:T(8,128)(2,1)}, u32[]{:S(2)}, u32[]{:S(2)}) collective-permute-start(bf16[384,1088]{0,1:T(8,128)(2,1)} %collective-permute-done.19), channel_id=1, source_target_pairs={{1,0},{2,1},{3,2},{5,4},{6,5},{7,6},{9,8},{10,9},{11,10},{13,12},{... | collective-permute-start | bytes 2506760 | tf_op jit(solution)/shard_map/ppermute | solution.py:31
  374.6 48.5 %collective-permute-start.22 = (bf16[384,1088]{0,1:T(8,128)(2,1)}, bf16[384,1088]{0,1:T(8,128)(2,1)}, u32[]{:S(2)}, u32[]{:S(2)}) collective-permute-start(bf16[384,1088]{0,1:T(8,128)(2,1)} %collective-permute-done.21), channel_id=1, source_target_pairs={{0,1},{1,2},{2,3},{4,5},{5,6},{6,7},{8,9},{9,10},{10,11},{12,13},{... | collective-permute-start | bytes 2506760 | tf_op jit(solution)/shard_map/ppermute | solution.py:30
  398.1 19.7 %collective-permute-start.11 = (bf16[384,1088]{0,1:T(8,128)(2,1)}, bf16[384,1088]{0,1:T(8,128)(2,1)}, u32[]{:S(2)}, u32[]{:S(2)}) collective-permute-start(bf16[384,1088]{0,1:T(8,128)(2,1)} %add_convert_fusion.3), channel_id=1, source_target_pairs={{0,1},{1,2},{2,3},{4,5},{5,6},{6,7},{8,9},{9,10},{10,11},{12,13},{... | collective-permute-start | bytes 2506760 | tf_op jit(solution)/shard_map/ppermute | solution.py:30
  408.2 24.9 %collective-permute-start.12 = (bf16[384,1088]{0,1:T(8,128)(2,1)}, bf16[384,1088]{0,1:T(8,128)(2,1)}, u32[]{:S(2)}, u32[]{:S(2)}) collective-permute-start(bf16[384,1088]{0,1:T(8,128)(2,1)} %add_convert_fusion.3), channel_id=1, source_target_pairs={{1,0},{2,1},{3,2},{5,4},{6,5},{7,6},{9,8},{10,9},{11,10},{13,12},{... | collective-permute-start | bytes 2506760 | tf_op jit(solution)/shard_map/ppermute | solution.py:31
  417.8 19.9 %collective-permute-start.15 = (bf16[384,1088]{0,1:T(8,128)(2,1)}, bf16[384,1088]{0,1:T(8,128)(2,1)}, u32[]{:S(2)}, u32[]{:S(2)}) collective-permute-start(bf16[384,1088]{0,1:T(8,128)(2,1)} %collective-permute-done.11), channel_id=1, source_target_pairs={{0,1},{1,2},{2,3},{4,5},{5,6},{6,7},{8,9},{9,10},{10,11},{12,13},{... | collective-permute-start | bytes 2506760 | tf_op jit(solution)/shard_map/ppermute | solution.py:30
  429.8 13.2 %copy-start.2 = (f32[384,1088]{0,1:T(8,128)S(1)}, f32[384,1088]{0,1:T(8,128)}, u32[]{:S(2)}) copy-start(f32[384,1088]{0,1:T(8,128)} %copy-done.1) | copy-start | bytes 5013508
  433.1 19.6 %collective-permute-start.13 = (bf16[384,1088]{0,1:T(8,128)(2,1)}, bf16[384,1088]{0,1:T(8,128)(2,1)}, u32[]{:S(2)}, u32[]{:S(2)}) collective-permute-start(bf16[384,1088]{0,1:T(8,128)(2,1)} %collective-permute-done.12), channel_id=1, source_target_pairs={{1,0},{2,1},{3,2},{5,4},{6,5},{7,6},{9,8},{10,9},{11,10},{13,12},{... | collective-permute-start | bytes 2506760 | tf_op jit(solution)/shard_map/ppermute | solution.py:31
  437.7 20.5 %collective-permute-start.16 = (bf16[384,1088]{0,1:T(8,128)(2,1)}, bf16[384,1088]{0,1:T(8,128)(2,1)}, u32[]{:S(2)}, u32[]{:S(2)}) collective-permute-start(bf16[384,1088]{0,1:T(8,128)(2,1)} %collective-permute-done.15), channel_id=1, source_target_pairs={{0,1},{1,2},{2,3},{4,5},{5,6},{6,7},{8,9},{9,10},{10,11},{12,13},{... | collective-permute-start | bytes 2506760 | tf_op jit(solution)/shard_map/ppermute | solution.py:30
  452.7 18.7 %collective-permute-start.14 = (bf16[384,1088]{0,1:T(8,128)(2,1)}, bf16[384,1088]{0,1:T(8,128)(2,1)}, u32[]{:S(2)}, u32[]{:S(2)}) collective-permute-start(bf16[384,1088]{0,1:T(8,128)(2,1)} %collective-permute-done.13), channel_id=1, source_target_pairs={{1,0},{2,1},{3,2},{5,4},{6,5},{7,6},{9,8},{10,9},{11,10},{13,12},{... | collective-permute-start | bytes 2506760 | tf_op jit(solution)/shard_map/ppermute | solution.py:31
  486.8 10.5 copy-start.70
  497.4 4.8 copy-start.71
  582.1 42.8 %copy-start.24 = (bf16[384,1088]{1,0:T(8,128)(2,1)S(1)}, bf16[384,1088]{1,0:T(8,128)(2,1)}, u32[]{:S(2)}) copy-start(bf16[384,1088]{1,0:T(8,128)(2,1)} %copy.351) | copy-start | bytes 2506756
  582.1 21.2 %collective-permute-start.24 = (bf16[2,192,1088]{2,1,0:T(8,128)(2,1)}, bf16[2,192,1088]{2,1,0:T(8,128)(2,1)S(1)}, u32[]{:S(2)}, u32[]{:S(2)}) collective-permute-start(bf16[2,192,1088]{2,1,0:T(8,128)(2,1)} %bitcast.232), channel_id=1, source_target_pairs={{1,0},{2,1},{3,2},{5,4},{6,5},{7,6},{9,8},{10,9},{11,10},{13,12},{... | collective-permute-start | bytes 2506760 | tf_op jit(solution)/shard_map/ppermute | solution.py:31
  583.5 21.0 %collective-permute-start.23 = (bf16[2,192,1088]{2,1,0:T(8,128)(2,1)}, bf16[2,192,1088]{2,1,0:T(8,128)(2,1)S(1)}, u32[]{:S(2)}, u32[]{:S(2)}) collective-permute-start(bf16[2,192,1088]{2,1,0:T(8,128)(2,1)} %bitcast.233), channel_id=1, source_target_pairs={{0,1},{1,2},{2,3},{4,5},{5,6},{6,7},{8,9},{9,10},{10,11},{12,13},{... | collective-permute-start | bytes 2506760 | tf_op jit(solution)/shard_map/ppermute | solution.py:30
  603.3 19.9 %collective-permute-start.25 = (bf16[2,192,1088]{2,1,0:T(8,128)(2,1)S(1)}, bf16[2,192,1088]{2,1,0:T(8,128)(2,1)S(1)}, u32[]{:S(2)}, u32[]{:S(2)}) collective-permute-start(bf16[2,192,1088]{2,1,0:T(8,128)(2,1)S(1)} %collective-permute-done.24), channel_id=1, source_target_pairs={{1,0},{2,1},{3,2},{5,4},{6,5},{7,6},{9,8},{10,9},{11,10},{13,12},{... | collective-permute-start | bytes 2506760 | tf_op jit(solution)/shard_map/ppermute | solution.py:31
  604.6 20.5 %collective-permute-start.27 = (bf16[2,192,1088]{2,1,0:T(8,128)(2,1)S(1)}, bf16[2,192,1088]{2,1,0:T(8,128)(2,1)S(1)}, u32[]{:S(2)}, u32[]{:S(2)}) collective-permute-start(bf16[2,192,1088]{2,1,0:T(8,128)(2,1)S(1)} %collective-permute-done.23), channel_id=1, source_target_pairs={{0,1},{1,2},{2,3},{4,5},{5,6},{6,7},{8,9},{9,10},{10,11},{12,13},{... | collective-permute-start | bytes 2506760 | tf_op jit(solution)/shard_map/ppermute | solution.py:30
  623.2 19.0 %collective-permute-start.26 = (bf16[2,192,1088]{2,1,0:T(8,128)(2,1)S(1)}, bf16[2,192,1088]{2,1,0:T(8,128)(2,1)S(1)}, u32[]{:S(2)}, u32[]{:S(2)}) collective-permute-start(bf16[2,192,1088]{2,1,0:T(8,128)(2,1)S(1)} %collective-permute-done.25), channel_id=1, source_target_pairs={{1,0},{2,1},{3,2},{5,4},{6,5},{7,6},{9,8},{10,9},{11,10},{13,12},{... | collective-permute-start | bytes 2506760 | tf_op jit(solution)/shard_map/ppermute | solution.py:31
  625.1 18.9 %collective-permute-start.28 = (bf16[2,192,1088]{2,1,0:T(8,128)(2,1)S(1)}, bf16[2,192,1088]{2,1,0:T(8,128)(2,1)S(1)}, u32[]{:S(2)}, u32[]{:S(2)}) collective-permute-start(bf16[2,192,1088]{2,1,0:T(8,128)(2,1)S(1)} %collective-permute-done.27), channel_id=1, source_target_pairs={{0,1},{1,2},{2,3},{4,5},{5,6},{6,7},{8,9},{9,10},{10,11},{12,13},{... | collective-permute-start | bytes 2506760 | tf_op jit(solution)/shard_map/ppermute | solution.py:30
  647.9 18.4 %all-to-all-start.5 = ((bf16[8,64,768]{2,1,0:T(8,128)(2,1)}), bf16[8,64,768]{2,1,0:T(8,128)(2,1)}, u32[]{:S(2)}, u32[]{:S(2)}) async-start(bf16[8,64,768]{2,1,0:T(8,128)(2,1)} %bitcast.237), calls=%async_computation.5 | async-start | bytes 1572864 | tf_op jit(solution)/shard_map/all_to_all | solution.py:504
  653.6 162.6 %reduce-scatter.12.cloned.1.call-start = ((), (), s32[]{:S(2)}) async-start(), calls=%async_computation.14 | async-start | bytes 2820096
  663.1 155.0 %reduce-scatter.14.cloned.1.call-start = ((), (), s32[]{:S(2)}) async-start(), calls=%async_computation.15 | async-start | bytes 2820096
  736.0 10.1 collective-permute-start.29
  750.1 41.0 %all-to-all-start.6 = ((bf16[8,192,768]{2,1,0:T(8,128)(2,1)}), bf16[8,192,768]{2,1,0:T(8,128)(2,1)}, u32[]{:S(2)}, u32[]{:S(2)}) async-start(bf16[8,192,768]{2,1,0:T(8,128)(2,1)} %pad_maximum_fusion.1), calls=%async_computation.6 | async-start | bytes 4718592 | tf_op jit(solution)/shard_map/all_to_all | solution.py:523
  791.1 81.5 %all-to-all-start.3 = ((bf16[4,384,1088]{1,2,0:T(8,128)(2,1)}), bf16[4,384,1088]{1,2,0:T(8,128)(2,1)}, u32[]{:S(2)}, u32[]{:S(2)}) async-start(bf16[4,384,1088]{1,2,0:T(8,128)(2,1)} %bitcast.210), calls=%async_computation.3 | async-start | bytes 6684672 | tf_op jit(solution)/shard_map/all_to_all | solution.py:43
  795.9 145.4 %reduce-scatter.10.cloned.1.call-start = ((), (), s32[]{:S(2)}) async-start(), calls=%async_computation.12 | async-start | bytes 3244032 | tf_op jit(solution)/shard_map/reduce_scatter | solution.py:511
  816.2 10.5 copy-start.42
  872.6 196.5 %all-to-all-start.7 = ((bf16[4,384,1088]{1,2,0:T(8,128)(2,1)}), bf16[4,384,1088]{1,2,0:T(8,128)(2,1)}, u32[]{:S(2)}, u32[]{:S(2)}) async-start(bf16[4,384,1088]{1,2,0:T(8,128)(2,1)} %copy.362), calls=%async_computation.7 | async-start | bytes 6684672 | tf_op jit(solution)/shard_map/all_to_all | solution.py:43
  878.1 117.1 %all-reduce.12.cloned.1.call-start = ((), (), s32[]{:S(2)}) async-start(), calls=%async_computation.13 | async-start | bytes 1179648 | tf_op jit(solution)/shard_map/psum | solution.py:555
  879.6 61.8 %copy-start.11 = (bf16[384,1088]{0,1:T(8,128)(2,1)S(1)}, bf16[384,1088]{0,1:T(8,128)(2,1)}, u32[]{:S(2)}) copy-start(bf16[384,1088]{0,1:T(8,128)(2,1)} %copy-done.10) | copy-start | bytes 2506756
  879.6 61.8 %copy-start.41 = (bf16[1,64,384]{2,1,0:T(8,128)(2,1)S(1)}, bf16[1,64,384]{2,1,0:T(8,128)(2,1)}, u32[]{:S(2)}) copy-start(bf16[1,64,384]{2,1,0:T(8,128)(2,1)} %get-tuple-element.40) | copy-start | bytes 147460
  884.6 67.7 %collective-permute-start.31 = (bf16[1,48,1088]{2,1,0:T(8,128)(2,1)}, bf16[1,48,1088]{2,1,0:T(8,128)(2,1)}, u32[]{:S(2)}, u32[]{:S(2)}) collective-permute-start(bf16[1,48,1088]{2,1,0:T(8,128)(2,1)} %slice.168), channel_id=1, source_target_pairs={{1,0},{2,1},{3,2},{5,4},{6,5},{7,6},{9,8},{10,9},{11,10},{13,12},{... | collective-permute-start | bytes 313352 | tf_op jit(solution)/shard_map/ppermute | solution.py:352
  943.6 121.1 %all-reduce.14.cloned.1.call-start = ((), (), s32[]{:S(2)}) async-start(), calls=%async_computation.16 | async-start | bytes 5013504
  949.6 46.8 %copy-start.36 = (bf16[1,256,1088]{2,1,0:T(8,128)(2,1)S(1)}, bf16[1,256,1088]{2,1,0:T(8,128)(2,1)}, u32[]{:S(2)}) copy-start(bf16[1,256,1088]{2,1,0:T(8,128)(2,1)} %copy-done.35) | copy-start | bytes 1671172
  951.0 46.5 %collective-permute-start.30 = (bf16[3,48,1088]{2,1,0:T(8,128)(2,1)S(1)}, bf16[3,48,1088]{2,1,0:T(8,128)(2,1)}, u32[]{:S(2)}, u32[]{:S(2)}) collective-permute-start(bf16[3,48,1088]{2,1,0:T(8,128)(2,1)S(1)} %slice.164), channel_id=1, source_target_pairs={{1,0},{2,1},{3,2},{5,4},{6,5},{7,6},{9,8},{10,9},{11,10},{13,12},{... | collective-permute-start | bytes 940040 | tf_op jit(solution)/shard_map/ppermute | solution.py:352
  (53 other events, 123.7 us)
Sparse Core Ops, SparseCore 0:
  147.8 69.3 all-gather.1
  663.2 44.7 reduce-scatter.11
  746.2 55.6 reduce-scatter.13
  812.2 129.1 reduce-scatter.9
  944.1 51.0 all-reduce.11
  1000.8 63.8 all-reduce.13

commit v2 on v1

v2 whole, which is shorter than its diff:
```python
import functools

import jax
import jax.numpy as jnp
from jax import lax
from jax.experimental import pallas as pl
from jax.experimental.pallas import tpu as pltpu
from jax.sharding import PartitionSpec as P

HEADS = 17
HEAD_DIM = 64
REACH = 11

norm_eps = 1e-05
score_scale = 0.125
masked_score = -1e30
everywhere = ("chip", "core", "tensor")
layer = ("chip", "core")
sharers = ("tensor", "chip")


def line(count, steps):
    first, last = (max(0, -steps), min(count, count - steps))
    return [(source, source + steps) for source in range(first, last)]


def gather_tensor(rows, axis):
    count = lax.axis_size("tensor")
    index = lax.axis_index("tensor")
    up, down = [rows], [rows]
    for _ in range(count - 1):
        up.append(lax.ppermute(up[-1], "tensor", line(count, 1)))
        down.append(lax.ppermute(down[-1], "tensor", line(count, -1)))
    shape = rows.shape[:axis] + (count,) + rows.shape[axis:]
    gathered = lax.dynamic_update_index_in_dim(jnp.zeros(shape, rows.dtype), rows, index, axis)
    for steps in range(1, count):
        block = jnp.where(index >= steps, up[steps], down[count - steps])
        gathered = lax.dynamic_update_index_in_dim(
            gathered, block, lax.rem(index - steps + count, count), axis
        )
    return gathered


def scatter_tensor(partial_sum):
    arrived = lax.all_to_all(partial_sum, "tensor", split_axis=0, concat_axis=0, tiled=True)
    return jnp.sum(arrived.astype(jnp.float32), axis=0)


def after(value, token):
    return lax.optimization_barrier((value, token))[0]


def other_core(value):
    return lax.ppermute(value, "core", [(0, 1), (1, 0)])


def small_sum(value):
    count = lax.axis_size(everywhere)
    copies = jnp.broadcast_to(value[None], (count,) + value.shape)
    arrived = lax.all_to_all(copies, everywhere, split_axis=0, concat_axis=0, tiled=True)
    return jnp.sum(arrived, axis=0)


def pick(value, index, axis):
    return lax.dynamic_index_in_dim(value, index, axis, keepdims=False)


def halve(value, axis, neighbour, index, token):
    sent = lax.ppermute(pick(value, 1 - index, axis), "chip", neighbour)
    if token is not None:
        sent = after(sent, token)
    kept = pick(value, index, axis).astype(jnp.float32) + sent.astype(jnp.float32)
    return kept.astype(jnp.bfloat16)


def flip(bit):
    return [(i, i ^ bit) for i in range(4)]


def chip_bits():
    index = lax.axis_index("chip")
    return lax.rem(index, 2), lax.div(index, 2)


def scatter_ring(both):
    tensor_size, index = lax.axis_size("tensor"), lax.axis_index("tensor")
    total = pick(both, index, 0).astype(jnp.float32)
    for steps in range(1, tensor_size):
        ring = [(i, (i + steps) % tensor_size) for i in range(tensor_size)]
        arrived = lax.ppermute(pick(both, lax.rem(index + steps, tensor_size), 0), "tensor", ring)
        total = total + arrived.astype(jnp.float32)
    return total


def gather_ring(block):
    tensor_size = lax.axis_size("tensor")
    blocks = [block]
    for steps in range(1, tensor_size):
        ring = [(i, (i + steps) % tensor_size) for i in range(tensor_size)]
        blocks.append(lax.ppermute(block, "tensor", ring))
    return blocks


def butterfly(value):
    for axis in ("core", "chip", "tensor"):
        count = lax.axis_size(axis)
        step = 1
        while step < count:
            value = value + lax.ppermute(value, axis, [(i, i ^ step) for i in range(count)])
            step *= 2
    return value


def norm_forward(values, gain_vec, bias_vec):
    mean_row = jnp.mean(values, axis=1, keepdims=True)
    centered = values - mean_row
    variance = jnp.mean(centered * centered, axis=1, keepdims=True)
    inv_std = lax.rsqrt(variance + norm_eps)
    normed = centered * inv_std
    return (normed, inv_std, normed * gain_vec + bias_vec)


def norm_backward(grad_normed, normed, inv_std, gain_vec):
    scaled = grad_normed * gain_vec
    plain_mean = jnp.mean(scaled, axis=1, keepdims=True)
    cross_mean = jnp.mean(scaled * normed, axis=1, keepdims=True)
    grad_values = inv_std * (scaled - plain_mean - normed * cross_mean)
    return (grad_values, jnp.sum(grad_normed * normed, axis=0), jnp.sum(grad_normed, axis=0))


def tile_of(width):
    return 384 if width % 384 == 0 else width


def attention_plan(query_pos, key_base, key_offsets, seq_ends):
    width = query_pos.shape[1]
    key_width = key_offsets.shape[0]
    tile, key_tile = tile_of(width), tile_of(key_width)
    starts = jnp.max(
        jnp.where(seq_ends[None, None, :] <= query_pos[:, :, None], seq_ends[None, None, :], 0),
        axis=2,
    )
    rows = jnp.stack((query_pos, starts), axis=1)
    tiles = query_pos.reshape(-1, tile)
    first, last = tiles[:, 0], tiles[:, tile - 1]
    last_start = starts.reshape(-1, tile)[:, tile - 1]
    offset_tiles = key_offsets.reshape(-1, key_tile)
    key_min = (key_base[:, None] + offset_tiles[None, :, 0]).reshape(-1)
    key_max = (key_base[:, None] + offset_tiles[None, :, key_tile - 1]).reshape(-1)
    key_end = jnp.min(
        jnp.where(seq_ends[None, :] > key_max[:, None], seq_ends[None, :], seq_ends[-1]), axis=1
    )
    low = jnp.sum((last[None, :] < key_min[:, None]).astype(jnp.int32), axis=1)
    high = jnp.sum((first[None, :] < key_end[:, None]).astype(jnp.int32), axis=1)
    bases = jnp.repeat(key_base, key_width // key_tile)
    plan = jnp.concatenate((low, high, bases, key_min, key_max, first, last_start))
    return (plan.astype(jnp.int32), rows.astype(jnp.int32), key_offsets[:, None].astype(jnp.int32))


def key_allowed(column_ref, rows_ref, step, per_key, key_tile, base, group, lanes):
    offset = pl.multiple_of(lax.rem(step, per_key) * key_tile, key_tile)
    key_pos = column_ref[pl.ds(offset, key_tile), :] + base
    query_pos = rows_ref[group, 0:1, lanes]
    query_start = rows_ref[group, 1:2, lanes]
    return (key_pos <= query_pos) & (key_pos >= query_start)


def forward_kernel(dims, ends, plan_ref, query_ref, pair_ref, rows_ref, column_ref, *more):
    first, final = ends
    state, more = ((), more) if first else (more[:3], more[3:])
    outs, (acc, top, tot) = more[:3], more[3:]
    blocks, groups, per_query, per_key, tile, key_tile, part = dims
    count = groups * per_query
    step = pl.program_id(0)

    @pl.when(step == 0)
    def _():
        if first:
            acc[...] = jnp.zeros_like(acc)
            top[...] = jnp.full(top.shape, masked_score, jnp.float32)
            tot[...] = jnp.zeros_like(tot)
        else:
            for held, given in zip((acc, top, tot), state):
                held[...] = given[...]

    keys = jnp.transpose(pair_ref[0, :HEAD_DIM, :].astype(jnp.float32)).astype(jnp.bfloat16)
    values_t = pair_ref[0, HEAD_DIM:, :]
    base, key_min, key_max = (plan_ref[kind * blocks + step] for kind in (2, 3, 4))

    def one_tile(index, _):
        group = lax.div(index, per_query)
        lanes = pl.ds(pl.multiple_of(lax.rem(index, per_query) * tile, tile), tile)
        queries_t = query_ref[group, :HEAD_DIM, lanes] * jnp.bfloat16(score_scale)
        inside = (key_max <= plan_ref[5 * blocks + index]) & (
            key_min >= plan_ref[5 * blocks + count + index]
        )

        def update(masked):
            scores = jnp.dot(keys, queries_t, preferred_element_type=jnp.float32)
            if masked:
                allowed = key_allowed(
                    column_ref, rows_ref, step, per_key, key_tile, base, group, lanes
                )
                scores = jnp.where(allowed, scores, masked_score)
            old_top = top[index]
            new_top = jnp.maximum(old_top, jnp.max(scores, axis=0, keepdims=True))
            weights = jnp.exp(scores - new_top)
            shrink = jnp.exp(old_top - new_top)
            top[index] = new_top
            tot[index] = tot[index] * shrink + jnp.sum(weights, axis=0, keepdims=True)
            acc[index] = acc[index] * shrink + jnp.dot(
                values_t, weights.astype(jnp.bfloat16), preferred_element_type=jnp.float32
            )

        pl.when(inside)(lambda: update(False))
        pl.when(jnp.logical_not(inside))(lambda: update(True))
        return 0

    lax.fori_loop(plan_ref[step], plan_ref[blocks + step], one_tile, 0)

    @pl.when(step == blocks - 1)
    def _():
        if not final:
            for held, given in zip(outs, (acc, top, tot)):
                held[...] = given[...]
            return
        out_ref, low_ref, total_ref = outs

        def finish(index, _):
            group = lax.div(index, per_query)
            lanes = pl.ds(pl.multiple_of(lax.rem(index, per_query) * tile, tile), tile)
            result = acc[index] / tot[index]
            out_ref[group, :, lanes] = result
            for piece in range(tile // part):
                low_ref[index * (tile // part) + piece] = result[
                    :, piece * part : (piece + 1) * part
                ].astype(jnp.bfloat16)
            total_ref[index] = top[index] + jnp.log(tot[index])
            return 0

        lax.fori_loop(0, count, finish, 0)


def backward_kernel(
    dims,
    ends,
    plan_ref,
    query_ref,
    pair_ref,
    rows_ref,
    column_ref,
    grad_ref,
    out_ref,
    total_ref,
    *more,
):
    first, final = ends
    state, more = ((), more) if first else (more[:1], more[1:])
    query_grad_ref, pair_grad_ref, acc, inner, grad_cols, query_rows, grad_rows = more[:7]
    key_acc, value_acc = more[7:]
    blocks, groups, per_query, per_key, tile, key_tile, part = dims
    count = groups * per_query
    step = pl.program_id(0)

    @pl.when(step == 0)
    def _():
        acc[...] = jnp.zeros_like(acc) if first else state[0][...]

        def prepare(index, _):
            group = lax.div(index, per_query)
            lanes = pl.ds(pl.multiple_of(lax.rem(index, per_query) * tile, tile), tile)
            for piece in range(tile // part):
                grad_cols[index, :, piece * part : (piece + 1) * part] = grad_ref[
                    index * (tile // part) + piece
                ]
            grads = grad_cols[index].astype(jnp.float32)
            inner[index] = jnp.sum(grads * out_ref[group, :, lanes], axis=0, keepdims=True)
            grad_rows[index] = jnp.transpose(grads).astype(jnp.bfloat16)
            scaled = query_ref[group, :HEAD_DIM, lanes].astype(jnp.float32) * score_scale
            query_rows[index] = jnp.transpose(scaled).astype(jnp.bfloat16)
            return 0

        lax.fori_loop(0, count, prepare, 0)

    keys_t = pair_ref[0, :HEAD_DIM, :]
    keys = jnp.transpose(keys_t.astype(jnp.float32)).astype(jnp.bfloat16)
    values = jnp.transpose(pair_ref[0, HEAD_DIM:, :].astype(jnp.float32)).astype(jnp.bfloat16)
    base, key_min, key_max = (plan_ref[kind * blocks + step] for kind in (2, 3, 4))
    key_acc[...] = jnp.zeros_like(key_acc)
    value_acc[...] = jnp.zeros_like(value_acc)

    def one_tile(index, _):
        group = lax.div(index, per_query)
        lanes = pl.ds(pl.multiple_of(lax.rem(index, per_query) * tile, tile), tile)
        queries_t = query_ref[group, :HEAD_DIM, lanes] * jnp.bfloat16(score_scale)
        grads_t = grad_cols[index]
        inside = (key_max <= plan_ref[5 * blocks + index]) & (
            key_min >= plan_ref[5 * blocks + count + index]
        )

        def update(masked):
            scores = jnp.dot(keys, queries_t, preferred_element_type=jnp.float32)
            weights = jnp.exp(scores - total_ref[index])
            if masked:
                allowed = key_allowed(
                    column_ref, rows_ref, step, per_key, key_tile, base, group, lanes
                )
                weights = jnp.where(allowed, weights, 0.0)
            grad_weights = jnp.dot(values, grads_t, preferred_element_type=jnp.float32)
            grad_scores = (weights * (grad_weights - inner[index])).astype(jnp.bfloat16)
            value_acc[...] += jnp.dot(
                weights.astype(jnp.bfloat16), grad_rows[index], preferred_element_type=jnp.float32
            )
            key_acc[...] += jnp.dot(
                grad_scores, query_rows[index], preferred_element_type=jnp.float32
            )
            acc[index] += jnp.dot(keys_t, grad_scores, preferred_element_type=jnp.float32)

        pl.when(inside)(lambda: update(False))
        pl.when(jnp.logical_not(inside))(lambda: update(True))
        return 0

    lax.fori_loop(plan_ref[step], plan_ref[blocks + step], one_tile, 0)
    pair_grad_ref[0, :HEAD_DIM, :] = jnp.transpose(key_acc[...]).astype(jnp.bfloat16)
    pair_grad_ref[0, HEAD_DIM:, :] = jnp.transpose(value_acc[...]).astype(jnp.bfloat16)

    @pl.when(step == blocks - 1)
    def _():
        if not final:
            query_grad_ref[...] = acc[...]
            return

        def finish(index, _):
            group = lax.div(index, per_query)
            lanes = pl.ds(pl.multiple_of(lax.rem(index, per_query) * tile, tile), tile)
            query_grad_ref[group, :, lanes] = (acc[index] * score_scale).astype(jnp.bfloat16)
            return 0

        lax.fori_loop(0, count, finish, 0)


def attention_call(kernel, ends, queries, pairs, plan, more, part, outs, scratch, flops):
    numbers, rows, column = plan
    groups, _, width = queries.shape
    key_groups, _, key_width = pairs.shape
    tile, key_tile = tile_of(width), tile_of(key_width)
    per_query, per_key = width // tile, key_width // key_tile
    blocks = key_groups * per_key
    count = groups * per_query

    def whole(array):
        return pl.BlockSpec(array.shape, lambda step, plan_ref: (0,) * array.ndim)

    pair_spec = pl.BlockSpec(
        (1, 2 * HEAD_DIM, key_tile),
        lambda step, plan_ref: (lax.div(step, per_key), 0, lax.rem(step, per_key)),
    )
    out_shapes, out_specs = [], []
    for kind in outs:
        if kind == "pairs":
            out_shapes.append(jax.ShapeDtypeStruct(pairs.shape, jnp.bfloat16))
            out_specs.append(pair_spec)
        else:
            shape = {
                "row": (count, 1, tile),
                "acc": (count, HEAD_DIM, tile),
                "low": (groups * width // part, HEAD_DIM, part),
            }.get(kind, (groups, HEAD_DIM, width))
            dtype = jnp.bfloat16 if kind in ("grads", "low") else jnp.float32
            out_shapes.append(jax.ShapeDtypeStruct(shape, dtype))
            out_specs.append(whole(out_shapes[-1]))
    sizes = {
        "acc": pltpu.VMEM((count, HEAD_DIM, tile), jnp.float32),
        "row": pltpu.VMEM((count, 1, tile), jnp.float32),
        "cols": pltpu.VMEM((count, HEAD_DIM, tile), jnp.bfloat16),
        "rows": pltpu.VMEM((count, tile, HEAD_DIM), jnp.bfloat16),
        "keys": pltpu.VMEM((key_tile, HEAD_DIM), jnp.float32),
    }
    pairs_near = groups * width * min(key_groups * key_width, 2304)
    return pl.pallas_call(
        functools.partial(kernel, (blocks, groups, per_query, per_key, tile, key_tile, part), ends),
        out_shape=out_shapes,
        grid_spec=pltpu.PrefetchScalarGridSpec(
            num_scalar_prefetch=1,
            grid=(blocks,),
            in_specs=[whole(queries), pair_spec, whole(rows), whole(column)]
            + [whole(array) for array in more],
            out_specs=out_specs,
            scratch_shapes=[sizes[name] for name in scratch],
        ),
        compiler_params=pltpu.CompilerParams(
            dimension_semantics=("arbitrary",), vmem_limit_bytes=56 * 2**20
        ),
        cost_estimate=pl.CostEstimate(
            flops=flops * pairs_near * HEAD_DIM,
            bytes_accessed=4 * queries.size + 4 * pairs.size,
            transcendentals=pairs_near,
        ),
    )(numbers, queries, pairs, rows, column, *more)


def attend(queries, pairs, plans, part):
    state = ()
    for index, (keys, plan) in enumerate(zip(pairs, plans)):
        ends = (index == 0, index == len(pairs) - 1)
        if index == 1:
            keys = after(keys, state)
        state = attention_call(
            forward_kernel,
            ends,
            queries,
            keys,
            plan,
            tuple(state),
            part,
            ("out", "low", "row") if ends[1] else ("acc", "row", "row"),
            ("acc", "row", "row"),
            16,
        )
    return state


def attend_back(queries, keys, plan, known, state, final):
    return attention_call(
        backward_kernel,
        (not state, final),
        queries,
        keys,
        plan,
        known + state,
        known[0].shape[2],
        ("grads" if final else "acc", "pairs"),
        ("acc", "row", "cols", "rows", "rows", "keys", "keys"),
        40,
    )


def aligned_weights(stacked, tensor_size, tensor_index, head_rows):
    slab = stacked.shape[1]
    extra = slab - head_rows
    most = (tensor_size - 1) * extra
    before = lax.ppermute(stacked[:, slab - most :], "tensor", line(tensor_size, 1))
    joined = jnp.concatenate((before, stacked), axis=1)
    own = lax.dynamic_slice_in_dim(joined, most - extra * tensor_index, head_rows, 1)
    return own


def last_weights(stacked, tensor_size, tensor_index):
    final = stacked[:, stacked.shape[1] - HEAD_DIM :]
    last = jnp.where(tensor_index == tensor_size - 1, final, jnp.zeros_like(final))
    for target in range(tensor_size - 1):
        last = last + lax.ppermute(final, "tensor", [(tensor_size - 1, target)])
    return last


def slab_rows(own, last, slab, tensor_size, tensor_index):
    extra = slab - own.shape[1]
    most = (tensor_size - 1) * extra
    following = lax.ppermute(own[:, :most], "tensor", line(tensor_size, -1))
    following = jnp.pad(following, ((0, 0), (0, HEAD_DIM - most), (0, 0)))
    following = jnp.where(tensor_index == tensor_size - 1, last, following)
    joined = jnp.concatenate((own, following), axis=1)
    return lax.dynamic_slice_in_dim(joined, extra * tensor_index, slab, 1)


def local(
    tokens_in,
    ln1_gain,
    ln1_bias,
    w_qkv,
    b_qv,
    w_out,
    b_out,
    ln2_gain,
    ln2_bias,
    w_up,
    b_up,
    w_down,
    b_down,
    seq_lengths,
    cotangent,
):
    tensor_size = lax.axis_size("tensor")
    tensor_index = lax.axis_index("tensor")
    chips = lax.axis_size("chip")
    chip_index = lax.axis_index("chip")
    core_index = lax.axis_index("core")
    dp_size = lax.axis_size(layer)
    dp_index = lax.axis_index(layer)
    flat_index = lax.axis_index(everywhere)
    devices = dp_size * tensor_size
    rows, width = tokens_in.shape
    slab = w_qkv.shape[1]
    unit_slab = w_up.shape[1]
    slots = (HEADS - 1) // tensor_size
    members = dp_size // slots
    member = lax.rem(dp_index, members)
    part = rows // members
    lanes = tensor_size * part
    head_rows = slots * HEAD_DIM
    whole_heads = width - HEAD_DIM
    low = jnp.bfloat16
    seq_ends = jnp.cumsum(seq_lengths)
    gain_one = ln1_gain.astype(jnp.float32)
    shift_one = ln1_bias.astype(jnp.float32)
    gain_two = ln2_gain.astype(jnp.float32)
    shift_two = ln2_bias.astype(jnp.float32)
    contract_first = (((0,), (0,)), ((), ()))
    contract_cols = (((1,), (1,)), ((), ()))

    stream = tokens_in.astype(jnp.float32)
    normed_one, inv_one, pre_one = norm_forward(stream, gain_one, shift_one)
    pre_one = pre_one.astype(low)
    wide_one = gather_tensor(pre_one.reshape(members, part, width), 1)
    wide_one = wide_one.reshape(members, lanes, width)
    own_w = aligned_weights(w_qkv, tensor_size, tensor_index, head_rows)
    last_w = last_weights(w_qkv, tensor_size, tensor_index)
    qkv_w = own_w.reshape(3, slots, HEAD_DIM, width).transpose(1, 0, 2, 3)
    qkv_w = qkv_w.reshape(slots, 3 * HEAD_DIM, width)
    last_qkv_w = last_w.reshape(3 * HEAD_DIM, width)
    bias_full = jnp.stack((b_qv[0], jnp.zeros_like(b_qv[0]), b_qv[1])).astype(jnp.float32)
    own_bias = lax.dynamic_slice_in_dim(bias_full, tensor_index * head_rows, head_rows, 1)
    own_bias = own_bias.reshape(3, slots, HEAD_DIM).transpose(1, 0, 2).reshape(slots, -1)
    last_bias = bias_full[:, whole_heads:].reshape(-1)

    half = unit_slab // 2
    quarter = half // chips
    if slab % chips == 0:
        out_rows = slab // chips
        out_piece = after(
            lax.dynamic_slice_in_dim(w_out, chip_index * out_rows, out_rows, 0), wide_one
        )
        full_out = lax.all_gather(out_piece, sharers, axis=0, tiled=True)
    else:
        full_out = lax.all_gather(w_out, "tensor", axis=0, tiled=True)
    unit_start = core_index * half + chip_index * quarter
    up_piece = after(lax.dynamic_slice_in_dim(w_up, unit_start, quarter, 1).T, wide_one)
    down_piece = after(lax.dynamic_slice_in_dim(w_down, unit_start, quarter, 0), wide_one)
    half_up = lax.all_gather(up_piece, sharers, axis=0, tiled=True)
    half_down = lax.all_gather(down_piece, sharers, axis=0, tiled=True)
    up_bias = lax.all_to_all(
        jnp.broadcast_to(b_up[None], (tensor_size, unit_slab)), "tensor", 0, 0, tiled=True
    )
    up_bias = lax.dynamic_slice_in_dim(up_bias, core_index * half, half, 1).reshape(-1)
    wide_grad = jnp.concatenate((cotangent, other_core(cotangent)), axis=0)

    offsets = jnp.arange(tensor_size, dtype=jnp.int32)[:, None] * rows
    offsets = (offsets + jnp.arange(part, dtype=jnp.int32)[None]).reshape(-1)
    dp_starts = jnp.arange(dp_size, dtype=jnp.int32) * (tensor_size * rows)
    query_pos = dp_starts[:, None] + offsets[None] + member * part
    halves = jnp.arange(members, dtype=jnp.int32)
    if members == 2:
        halves = lax.rem(member + halves, 2)
    key_base = halves[:, None] * part + dp_starts[None]
    bases = [key_base[0], key_base[1]] if members == 2 else [key_base.reshape(-1)]
    plans = [attention_plan(query_pos, base, offsets, seq_ends) for base in bases]
    row_range = jnp.arange(rows, dtype=jnp.int32)
    steps_back = min(-(-REACH // tensor_size), dp_size - 1) + 1
    last_base = dp_index - jnp.arange(steps_back, dtype=jnp.int32)
    distance = tensor_index + tensor_size - jnp.arange(tensor_size, dtype=jnp.int32)
    last_base = last_base[None] * tensor_size + lax.rem(distance, tensor_size)[:, None]
    last_base = last_base.reshape(-1) * rows
    last_plan = attention_plan(
        (flat_index * rows + row_range)[None], last_base, row_range, seq_ends
    )

    qkv = jnp.einsum("cfd,gtd->cgft", qkv_w, wide_one, preferred_element_type=jnp.float32)
    qkv = (qkv + own_bias[:, None, :, None]).astype(low).reshape(dp_size, 3 * HEAD_DIM, lanes)
    qkv = lax.all_to_all(qkv, layer, split_axis=0, concat_axis=0, tiled=True)
    last_qkv = jnp.einsum("fd,td->ft", last_qkv_w, pre_one, preferred_element_type=jnp.float32)
    last_qkv = (last_qkv + last_bias[:, None]).astype(low)[None]
    own_pairs = qkv[:, HEAD_DIM:]
    last_pairs = last_qkv[:, HEAD_DIM:]
    last_pairs = [last_pairs] + [
        lax.ppermute(last_pairs, layer, line(dp_size, step)) for step in range(1, steps_back)
    ]
    last_blocks = gather_ring(jnp.concatenate(last_pairs, axis=0))
    sharing = [list(range(i, i + members)) for i in range(0, dp_size, members)]
    if members == 2:
        pairs = [own_pairs, other_core(own_pairs)]
    else:
        pairs = [lax.all_gather(own_pairs, layer, axis_index_groups=sharing, axis=0, tiled=True)]
    mixed, mixed_low, total = attend(qkv, pairs, plans, part)
    attended = lax.all_to_all(mixed_low, everywhere, split_axis=0, concat_axis=0, tiled=True)
    last_pairs = jnp.concatenate(after(last_blocks, total), axis=0)
    last_mixed, last_low, last_total = attend(
        after(last_qkv, total), [last_pairs], [last_plan], rows
    )

    attended = attended.reshape(slots, members, tensor_size, HEAD_DIM, part)
    attended = attended.transpose(1, 2, 0, 3, 4).reshape(members, whole_heads, part)
    branch = jnp.einsum(
        "gkt,kd->gtd", attended, full_out[:whole_heads], preferred_element_type=jnp.float32
    ).reshape(rows, width)
    branch = branch + lax.dot_general(
        last_low[0], full_out[whole_heads:], contract_first, preferred_element_type=jnp.float32
    )
    stream_one = stream + branch + b_out.astype(jnp.float32)
    normed_two, inv_two, pre_two = norm_forward(stream_one, gain_two, shift_two)
    pre_two = pre_two.astype(low)
    wide_two = jnp.concatenate((pre_two, other_core(pre_two)), axis=0)
    hidden_pre = lax.dot_general(
        wide_two, half_up, contract_cols, preferred_element_type=jnp.float32
    ) + up_bias.astype(jnp.float32)
    gelu_out, gelu_pull = jax.vjp(
        lambda hidden_in: jax.nn.gelu(hidden_in, approximate=True), hidden_pre
    )
    activated = gelu_out.astype(low)
    grad_act = lax.dot_general(
        wide_grad, half_down, contract_cols, preferred_element_type=jnp.float32
    )
    grad_hidden = gelu_pull(grad_act)[0].astype(low)
    grad_up_part = jnp.sum(grad_hidden.astype(jnp.float32), axis=0)
    grad_two = cotangent.astype(jnp.float32)
    grad_down_bias = jnp.sum(grad_two, axis=0)
    grad_normed_two = jnp.dot(grad_hidden, half_up, preferred_element_type=jnp.float32)
    grad_normed_two = grad_normed_two[:rows] + other_core(
        grad_normed_two[rows:].astype(low)
    ).astype(jnp.float32)
    down_sum = jnp.dot(activated, half_down, preferred_element_type=jnp.float32)
    down_sum = down_sum[:rows] + other_core(down_sum[rows:].astype(low)).astype(jnp.float32)
    block_out = (stream_one + down_sum + b_down.astype(jnp.float32)).astype(low)
    grad_res_two, grad_gain_two, grad_shift_two = norm_backward(
        grad_normed_two, normed_two, inv_two, gain_two
    )
    grad_stream_one = grad_two + grad_res_two
    grad_branch = grad_stream_one.astype(low)
    grad_out_bias = jnp.sum(grad_branch.astype(jnp.float32), axis=0)

    branch_parts = grad_branch.reshape(members, part, width)
    grads = jnp.einsum(
        "kd,gtd->gkt", full_out[:whole_heads], branch_parts, preferred_element_type=jnp.float32
    )
    grads = grads.astype(low).reshape(members, tensor_size, slots, HEAD_DIM, part)
    grads = grads.transpose(2, 0, 1, 3, 4).reshape(devices, HEAD_DIM, part)
    grads = lax.all_to_all(grads, everywhere, split_axis=0, concat_axis=0, tiled=True)
    last_grads = lax.dot_general(
        full_out[whole_heads:], grad_branch, contract_cols, preferred_element_type=jnp.float32
    )
    last_grads = last_grads.astype(low)[None]
    last_query_grad, last_pair_grad = attend_back(
        last_qkv, last_pairs, last_plan, (last_grads, last_mixed, last_total), (), True
    )
    column = width // dp_size
    grad_down = lax.dot_general(
        wide_grad, activated, contract_first, preferred_element_type=jnp.float32
    ).astype(low)
    grad_up = lax.dot_general(
        wide_two, grad_hidden, contract_first, preferred_element_type=jnp.float32
    ).astype(low)
    grad_out = jnp.einsum(
        "gtd,gkt->dk", branch_parts, attended, preferred_element_type=jnp.float32
    )
    last_out = lax.dot_general(
        grad_branch, last_low[0], (((0,), (1,)), ((), ())), preferred_element_type=jnp.float32
    )
    grad_out = jnp.concatenate((grad_out, last_out), axis=1).astype(low)
    low_bit, high_bit = chip_bits()
    if chips != 4:
        grad_down = lax.psum_scatter(grad_down, "chip", scatter_dimension=0, tiled=True)
        grad_up = lax.psum_scatter(grad_up, "chip", scatter_dimension=0, tiled=True)
        grad_out = lax.psum_scatter(grad_out, "chip", scatter_dimension=0, tiled=True)
    last_pair_grad = last_pair_grad.reshape(tensor_size, steps_back, 2 * HEAD_DIM, rows)
    last_arrived = [last_pair_grad[0]]
    for step in range(1, tensor_size):
        back = [(i, (i - step) % tensor_size) for i in range(tensor_size)]
        last_arrived.append(lax.ppermute(last_pair_grad[step], "tensor", back))
    known = (grads, mixed, total)
    if members == 2:
        query_state, pair_grad = attend_back(qkv, pairs[1], plans[1], known, (), False)
        other_grad = other_core(pair_grad)
        last_arrived = after(last_arrived, query_state)
        last_arrived = sum(block.astype(jnp.float32) for block in last_arrived)
        last_blocks = [
            lax.ppermute(last_arrived[step].astype(low), layer, line(dp_size, -step))
            for step in range(1, steps_back)
        ]
        if chips == 4:
            blocked = (2, 2, 2 * column, -1)
            grad_down = halve(grad_down.reshape(blocked), 0, flip(2), high_bit, query_state)
            grad_up = halve(grad_up.reshape(blocked), 1, flip(1), low_bit, query_state)
            grad_out = halve(grad_out.reshape(blocked), 1, flip(1), low_bit, query_state)
        query_grad, pair_grad = attend_back(
            qkv, pairs[0], plans[0], known, (query_state,), True
        )
        if chips == 4:
            grad_down = halve(grad_down, 0, flip(1), low_bit, query_grad)
            grad_up = halve(grad_up, 0, flip(2), high_bit, query_grad)
            grad_out = halve(grad_out, 0, flip(2), high_bit, query_grad)
        last_sum = last_arrived[0]
        for block in after(last_blocks, query_grad):
            last_sum = last_sum + block.astype(jnp.float32)
        pair_sum = pair_grad.astype(jnp.float32) + other_grad.astype(jnp.float32)
    else:
        last_arrived = sum(block.astype(jnp.float32) for block in last_arrived)
        last_sum = last_arrived[0]
        for step in range(1, steps_back):
            arrived = lax.ppermute(last_arrived[step].astype(low), layer, line(dp_size, -step))
            last_sum = last_sum + arrived.astype(jnp.float32)
        query_grad, pair_grad = attend_back(qkv, pairs[0], plans[0], known, (), True)
        pair_grad = pair_grad.reshape(members, dp_size, 2 * HEAD_DIM, lanes)
        pair_grad = lax.all_to_all(pair_grad, layer, 0, 0, axis_index_groups=sharing, tiled=True)
        pair_sum = jnp.sum(pair_grad.astype(jnp.float32), axis=0)
    last_pair_grad = last_sum.astype(low)
    qkv_grad = jnp.concatenate((query_grad, pair_sum.astype(low)), axis=1)
    qkv_grad = lax.all_to_all(qkv_grad, layer, split_axis=0, concat_axis=0, tiled=True)
    qkv_grad = qkv_grad.reshape(slots, members, 3 * HEAD_DIM, lanes)
    last_qkv_grad = jnp.concatenate((last_query_grad[0], last_pair_grad), axis=0)

    grad_normed_one = []
    for piece in range(members):
        product = jnp.einsum(
            "cfd,cft->dt", qkv_w, qkv_grad[:, piece], preferred_element_type=jnp.float32
        )
        product = product.astype(low).T.reshape(tensor_size, part, width)
        grad_normed_one.append(scatter_tensor(product))
    grad_normed_one = jnp.concatenate(grad_normed_one, axis=0)
    last_normed_one = lax.dot_general(
        last_qkv_grad, last_qkv_w, contract_first, preferred_element_type=jnp.float32
    )
    grad_normed_one = grad_normed_one + last_normed_one
    grad_res_one, grad_gain_one, grad_shift_one = norm_backward(
        grad_normed_one, normed_one, inv_one, gain_one
    )
    grad_input = grad_stream_one + grad_res_one

    units = jnp.stack((grad_up, grad_down)).reshape(2, 2 * column, tensor_size, half)
    units = scatter_ring(units.transpose(2, 0, 1, 3))
    units = units.astype(low).reshape(2, 2, column, half)
    kept = pick(units, core_index, 1)
    arrived = other_core(pick(units, 1 - core_index, 1))
    units = (
        jnp.where(core_index == 0, kept, arrived),
        jnp.where(core_index == 0, arrived, kept),
    )
    units = jnp.concatenate(units, axis=2).astype(jnp.float32)
    grad_out = grad_out.reshape(2 * column, tensor_size, slab).transpose(1, 0, 2)
    grad_out = scatter_ring(grad_out).reshape(2, column, slab)
    sent = other_core(pick(grad_out, 1 - core_index, 0).astype(low))
    grad_out = (pick(grad_out, core_index, 0) + sent.astype(jnp.float32)).T

    own_qkv_grad = jnp.einsum(
        "gtd,cgft->dcf", wide_one, qkv_grad, preferred_element_type=jnp.float32
    )
    last_part = lax.dot_general(
        pre_one, last_qkv_grad, (((0,), (1,)), ((), ())), preferred_element_type=jnp.float32
    )
    grad_qkv = jnp.concatenate((own_qkv_grad.reshape(width, -1), last_part), axis=1).astype(low)
    if chips == 4:
        grad_qkv = grad_qkv.reshape(2, 2, 2, column, -1)
        sent = other_core(pick(grad_qkv, 1 - core_index, 2))
        kept = pick(grad_qkv, core_index, 2).astype(jnp.float32)
        grad_qkv = (kept + sent.astype(jnp.float32)).astype(low)
        grad_qkv = halve(grad_qkv, 1, flip(1), low_bit, None)
        grad_qkv = halve(grad_qkv, 0, flip(2), high_bit, None)
    else:
        grad_qkv = lax.psum_scatter(grad_qkv, layer, scatter_dimension=0, tiled=True)
    own_qkv_grad = grad_qkv[:, : 3 * head_rows].T.reshape(slots, 3, HEAD_DIM, column)
    own_qkv_grad = own_qkv_grad.transpose(1, 0, 2, 3).reshape(3, head_rows, column)
    last_part = grad_qkv[:, 3 * head_rows :].T.reshape(3, HEAD_DIM, column)
    last_sum = last_part.astype(jnp.float32)
    for source in range(tensor_size - 1):
        arrived = lax.ppermute(last_part, "tensor", [(source, tensor_size - 1)])
        last_sum = last_sum + arrived.astype(jnp.float32)
    grad_qkv = slab_rows(own_qkv_grad, last_sum.astype(low), slab, tensor_size, tensor_index)
    grad_qkv = grad_qkv.astype(jnp.float32)

    head = tensor_index * slots + lax.div(dp_index, members)
    own_sums = (jnp.sum(query_grad.astype(jnp.float32), axis=(0, 2)),)
    own_sums += (jnp.sum(pair_sum[:, HEAD_DIM:], axis=(0, 2)),)
    last_sums = jnp.sum(last_qkv_grad.astype(jnp.float32), axis=1).reshape(3, HEAD_DIM)
    qv_sum = jnp.zeros((2, HEADS, HEAD_DIM), jnp.float32).at[:, HEADS - 1].set(last_sums[::2])
    qv_sum = lax.dynamic_update_slice_in_dim(qv_sum, jnp.stack(own_sums)[:, None], head, 1)
    up_full = lax.dynamic_update_slice_in_dim(
        jnp.zeros((tensor_size, unit_slab), jnp.float32),
        grad_up_part.reshape(tensor_size, half),
        core_index * half,
        1,
    ).reshape(-1)
    early = jnp.concatenate(
        (grad_out_bias, grad_gain_two, grad_shift_two, grad_down_bias, up_full, qv_sum.reshape(-1))
    )
    early = butterfly(early)
    qv_sum = early[-2 * width :].reshape(2, width)
    early, up_sum = early[: 4 * width].reshape(4, width), early[4 * width : -2 * width]
    late = small_sum(jnp.stack((grad_gain_one, grad_shift_one)))
    grad_up_bias = lax.dynamic_slice_in_dim(up_sum, tensor_index * unit_slab, unit_slab, 0)
    return (
        block_out,
        grad_input,
        late[0],
        late[1],
        grad_qkv,
        qv_sum,
        grad_out,
        early[0],
        early[1],
        early[2],
        units[0],
        grad_up_bias,
        units[1].T,
        early[3],
    )


def solution(mesh):
    chips, tensor = mesh.shape["dp"] // 2, mesh.shape["tensor"]
    cores = jax.sharding.Mesh(mesh.devices.reshape(chips, 2, tensor), everywhere)
    in_specs = (
        P(everywhere, None),
        P(),
        P(),
        P(None, "tensor", None),
        P(),
        P("tensor", None),
        P(),
        P(),
        P(),
        P(None, "tensor"),
        P("tensor"),
        P("tensor", None),
        P(),
        P(),
        P(everywhere, None),
    )
    out_specs = (
        P(everywhere, None),
        P(everywhere, None),
        P(),
        P(),
        P(None, "tensor", layer),
        P(),
        P("tensor", layer),
        P(),
        P(),
        P(),
        P(layer, "tensor"),
        P("tensor"),
        P("tensor", layer),
        P(),
    )
    return jax.shard_map(local, mesh=cores, in_specs=in_specs, out_specs=out_specs, check_vma=False)
```

time: 1150 us -> 898 us (0.78)
  waiting for transfers between devices: 423 us -> 260 us
  blocking collectives: 131 us -> 0 us
  Pallas kernels: 143 us -> 177 us
    ppermute x7 -> x47, waiting for transfers between devices: 0.02 us -> 147 us  [the longest x3 54.3 us: gather_ring(): blocks.append(lax.ppermute(block, 'tensor', ring))]
    ppermute x12 -> x3, waiting for transfers between devices: 158 us -> 44.3 us  [gather_tensor(): down.append(lax.ppermute(down[-1], 'tensor', line(count, -1)))]
    all_to_all x2 -> x0, blocking collectives: 89 us -> none  [the longest x1 73 us: scatter_tensor(): lax.all_to_all(partial_sum.astype(jnp.bfloat16), 'tensor', split_axis=0,...]
    ppermute x12 -> x3, starting transfers between devices: 76.9 us -> 16.6 us  [gather_tensor(): up.append(lax.ppermute(up[-1], 'tensor', line(count, 1)))]
    ppermute x7 -> x47, starting transfers between devices: 6.81 us -> 66.5 us  [the longest x6 9.81 us: scatter_ring(): lax.ppermute(pick(both, lax.rem(index + steps, tensor_size), 0), 'tensor'...]
    unnamed x9 -> x3, waiting for transfers between devices: 57.3 us -> 0.05 us
    reduce_scatter x1 -> x0, waiting for transfers between devices: 55.5 us -> none  [local(): lax.psum_scatter(last_pair_grad, everywhere, scatter_dimension=0, tiled=T...]
    psum x1 -> x0, waiting for transfers between devices: 42.9 us -> none  [local(): last_parts = lax.psum(last_parts, 'tensor').reshape(4, HEAD_DIM, width)]
  transfers between devices with their start and end apart: 44 -> 65, of which waited for: 22 -> 25; matrix products, arithmetic and copies ran while one was open for 18% -> 26% of each run, Pallas kernels for 13% -> 20%
where the time goes in v2:
time: 898 us; the launch traced here: 883 us
  waiting for transfers between devices  260 us (29%)
  Pallas kernels  177 us (20%)
  starting transfers between devices  155 us (17%)
  local copies, waits for them, and re-layouts  117 us (13%)
  matrix products  84.3 us (9%)
  other arithmetic  74.4 us (8%)
  between operations  15.9 us (2%)
    pallas_call x6, Pallas kernels, attention_call(): pl.pallas_call(functools.partial(kernel, (blocks, groups, per_query, per_...  177 us
    ppermute x3, waiting for transfers between devices, gather_ring(): blocks.append(lax.ppermute(block, 'tensor', ring))  54.3 us
    ppermute x6, waiting for transfers between devices, scatter_ring(): lax.ppermute(pick(both, lax.rem(index + steps, tensor_size), 0), 'tensor'...  44.8 us
    ppermute x3, waiting for transfers between devices, gather_tensor(): down.append(lax.ppermute(down[-1], 'tensor', line(count, -1)))  44.3 us
    ppermute x8, waiting for transfers between devices, halve(): sent = lax.ppermute(pick(value, 1 - index, axis), 'chip', neighbour)  31.9 us
    all_to_all x1, waiting for transfers between devices, local(): qkv = lax.all_to_all(qkv, layer, split_axis=0, concat_axis=0, tiled=True)  30.5 us
    all_to_all x2, starting transfers between devices, scatter_tensor(): lax.all_to_all(partial_sum, 'tensor', split_axis=0, concat_axis=0, tiled=...  25.1 us
    unnamed x192, local copies, waits for them, and re-layouts  23.8 us
  transfers between devices with their start and end apart: 65, of which 25 were waited for; matrix products, arithmetic and copies ran while one was open for 26% of the time, Pallas kernels for 20%

profile of v2, /device:TPU:0, one launch (start us, length us, event | category | flops | bytes accessed | tf_op | source)
XLA Modules:
  0.0 883.1 jit_solution(6060207912821828759)
XLA Ops:
  16.4 6.5 collective-permute-start
  22.9 17.0 %collective-permute-done.1 = bf16[2,192,1088]{2,1,0:T(8,128)(2,1)S(1)} collective-permute-done((bf16[2,192,1088]{2,1,0:T(8,128)(2,1)}, bf16[2,192,1088]{2,1,0:T(8,128)(2,1)S(1)}, u32[]{:S(2)}, u32[]{:S(2)}) %collective-permute-start.1) | collective-permute-done | bytes 835616 | tf_op jit(solution)/shard_map/ppermute | solution.py:33
  42.1 5.5 collective-permute-start.4
  47.6 16.0 %collective-permute-done.2 = bf16[2,192,1088]{2,1,0:T(8,128)(2,1)} collective-permute-done((bf16[2,192,1088]{2,1,0:T(8,128)(2,1)S(1)}, bf16[2,192,1088]{2,1,0:T(8,128)(2,1)}, u32[]{:S(2)}, u32[]{:S(2)}) %collective-permute-start.2) | collective-permute-done | bytes 835616 | tf_op jit(solution)/shard_map/ppermute | solution.py:33
  69.9 4.6 collective-permute-start.5
  74.4 11.3 %collective-permute-done.3 = bf16[2,192,1088]{2,1,0:T(8,128)(2,1)} collective-permute-done((bf16[2,192,1088]{2,1,0:T(8,128)(2,1)}, bf16[2,192,1088]{2,1,0:T(8,128)(2,1)}, u32[]{:S(2)}, u32[]{:S(2)}) %collective-permute-start.3) | collective-permute-done | bytes 835616 | tf_op jit(solution)/shard_map/ppermute | solution.py:33
  103.2 4.3 collective-permute-start.6
  109.0 5.5 collective-permute-done.6
  116.4 6.2 fusion.18
  124.2 4.4 all-to-all-start
  137.0 30.5 %all-to-all-done.query_ref = bf16[8,192,768]{2,1,0:T(8,128)(2,1)} async-done(((bf16[8,192,768]{2,1,0:T(8,128)(2,1)}), bf16[8,192,768]{2,1,0:T(8,128)(2,1)}, u32[]{:S(2)}, u32[]{:S(2)}) %all-to-all-start) | async-done | bytes 2359328 | tf_op jit(solution)/shard_map/all_to_all | solution.py:569
  170.2 31.5 %shard_map.254 = (f32[16,64,384]{2,1,0:T(8,128)}, f32[16,1,384]{2,1,0:T(1,128)}, f32[16,1,384]{2,1,0:T(1,128)}) custom-call(s32[112]{0:T(128)} %concatenate.59.plan_ref, bf16[8,192,768]{2,1,0:T(8,128)(2,1)} %all-to-all-done.query_ref, bf16[8,128,768]{2,1,0:T(8,128)(2,1)} %copy-done.32, s32[8,2,768]{2,1,0:T(2,128)} %pad_add_fusion.rows_ref, ...), custom_call_target="tpu_custom_call" | custom-call | flops 14495514624 | bytes 7864320 | tf_op jit(solution)/shard_map/pallas_call | solution.py:380
  201.7 33.7 %shard_map.255 = (f32[8,64,768]{2,1,0:T(8,128)}, bf16[32,64,192]{2,1,0:T(8,128)(2,1)}, f32[16,1,384]{2,1,0:T(1,128)}) custom-call(s32[112]{0:T(128)} %concatenate.57.plan_ref, bf16[8,192,768]{2,1,0:T(8,128)(2,1)} %all-to-all-done.query_ref, bf16[8,128,768]{2,1,0:T(8,128)(2,1)} %collective-permute-done.7.pair_ref, s32[8,2,768]{2,1,0:T(2,128)} %pad_add_fusion.rows_ref, ...), custom_call_target="tpu_custom_call" | custom-call | flops 14495514624 | bytes 7864320 | tf_op jit(solution)/shard_map/pallas_call | solution.py:380
  235.4 7.6 all-to-all-start.1
  245.0 3.4 collective-permute-start.13
  248.3 3.4 collective-permute-start.12
  255.5 3.5 collective-permute-done.12
  259.1 5.3 collective-permute-start.16
  268.6 15.4 %collective-permute-done.16 = bf16[4,128,384]{2,1,0:T(8,128)(2,1)S(1)} collective-permute-done((bf16[4,128,384]{2,1,0:T(8,128)(2,1)S(1)}, bf16[4,128,384]{2,1,0:T(8,128)(2,1)S(1)}, u32[]{:S(2)}, u32[]{:S(2)}) %collective-permute-start.16) | collective-permute-done | bytes 393248 | tf_op jit(solution)/shard_map/ppermute | solution.py:100
  284.1 38.9 %collective-permute-done.15 = bf16[4,128,384]{2,1,0:T(8,128)(2,1)S(1)} collective-permute-done((bf16[4,128,384]{2,1,0:T(8,128)(2,1)S(1)}, bf16[4,128,384]{2,1,0:T(8,128)(2,1)S(1)}, u32[]{:S(2)}, u32[]{:S(2)}) %collective-permute-start.15) | collective-permute-done | bytes 393248 | tf_op jit(solution)/shard_map/ppermute | solution.py:100
  325.5 14.7 %shard_map.256 = (f32[1,64,384]{2,1,0:T(8,128)}, bf16[1,64,384]{2,1,0:T(8,128)(2,1)}, f32[1,1,384]{2,1,0:T(1,128)}) custom-call(s32[82]{0:T(128)} %concatenate.60.plan_ref, bf16[1,192,384]{2,1,0:T(8,128)(2,1)} %copy-done.38, bf16[16,128,384]{2,1,0:T(8,128)(2,1)} %copy-done.51, s32[1,2,384]{2,1,0:T(2,128)} %pad_add_fusion.1.rows_ref, s32[384,1]{1,0:T(8,128)} %iota.130.column_ref), custom_call_target="tpu_custom_call" | custom-call | flops 905969664 | bytes 3440640 | tf_op jit(solution)/shard_map/pallas_call | solution.py:380
  340.2 4.4 reshape.737
  347.2 3.3 fusion.22
  359.6 4.0 all-to-all-done.2
  366.0 5.7 copy.358
  371.7 7.6 fusion.66
  382.1 6.5 convolution_convert_fusion
  388.6 10.4 %convert_reduce_fusion = (f32[2176]{0:T(1024)S(1)}, bf16[768,2176]{1,0:T(8,128)(2,1)S(1)}) fusion(f32[768,2176]{1,0:T(8,128)} %copy-done.81, f32[2176]{0:T(1024)S(1)} %reshape.724, bf16[768,1088]{0,1:T(8,128)(2,1)} %constant_dynamic-update-slice_fusion.4, bf16[2176,1088]{1,0:T(8,128)(2,1)} %all-gather.7.cloned.1.call-done), kind=kOutput, calls=%fused_computation.11 | convolution fusion | flops 3674896384 | bytes 16450560 | tf_op jit(solution)/shard_map/dot_general | solution.py:609
  399.1 8.2 fusion.104
  409.2 6.7 fusion.94
  421.1 8.6 convolution_convert_fusion.1
  436.4 3.8 fusion.49
  442.7 3.8 all-to-all-start.3
  454.6 4.1 dot_general.99
  466.2 16.8 %shard_map.259 = (bf16[1,64,384]{2,1,0:T(8,128)(2,1)}, bf16[16,128,384]{2,1,0:T(8,128)(2,1)}) custom-call(s32[82]{0:T(128)} %concatenate.60.plan_ref, bf16[1,192,384]{2,1,0:T(8,128)(2,1)} %copy-done.38, bf16[16,128,384]{2,1,0:T(8,128)(2,1)} %copy-done.51, s32[1,2,384]{2,1,0:T(2,128)} %pad_add_fusion.1.rows_ref, s32[384,1]{1,0:T(8,128)} %iota.131.column_ref, ...), custom_call_target="tpu_custom_call" | custom-call | flops 2264924160 | bytes 3440640 | tf_op jit(solution)/shard_map/pallas_call | solution.py:380
  488.2 39.9 %shard_map.257 = (f32[16,64,384]{2,1,0:T(8,128)}, bf16[8,128,768]{2,1,0:T(8,128)(2,1)}) custom-call(s32[112]{0:T(128)} %concatenate.57.plan_ref, bf16[8,192,768]{2,1,0:T(8,128)(2,1)} %all-to-all-done.query_ref, bf16[8,128,768]{2,1,0:T(8,128)(2,1)} %collective-permute-done.7.pair_ref, s32[8,2,768]{2,1,0:T(2,128)} %pad_add_fusion.rows_ref, ...), custom_call_target="tpu_custom_call" | custom-call | flops 36238786560 | bytes 7864320 | tf_op jit(solution)/shard_map/pallas_call | solution.py:380
  528.1 10.0 %collective-permute-done.40 = bf16[2,272,1088]{2,1,0:T(8,128)(2,1)} collective-permute-done((bf16[2,272,1088]{2,1,0:T(8,128)(2,1)}, bf16[2,272,1088]{2,1,0:T(8,128)(2,1)}, u32[]{:S(2)}, u32[]{:S(2)}) %collective-permute-start.40) | collective-permute-done | bytes 1183776 | tf_op jit(solution)/shard_map/ppermute | solution.py:69
  538.2 3.3 collective-permute-start.22
  545.6 4.6 collective-permute-done.22
  555.3 40.6 %shard_map.258 = (bf16[8,64,768]{2,1,0:T(8,128)(2,1)}, bf16[8,128,768]{2,1,0:T(8,128)(2,1)}) custom-call(s32[112]{0:T(128)} %concatenate.59.plan_ref, bf16[8,192,768]{2,1,0:T(8,128)(2,1)} %all-to-all-done.query_ref, bf16[8,128,768]{2,1,0:T(8,128)(2,1)} %copy-done.32, s32[8,2,768]{2,1,0:T(2,128)} %pad_add_fusion.rows_ref, s32[768,1]{1,0:T(8,128)} %add.910.column_ref, ...), custom_call_target="tpu_custom_call" | custom-call | flops 36238786560 | bytes 7864320 | tf_op jit(solution)/shard_map/pallas_call | solution.py:380
  617.1 4.4 all-to-all-start.4
  625.4 4.2 collective-permute-start.44
  631.3 3.9 collective-permute-done.44
  635.2 5.0 collective-permute-done.42
  640.2 6.4 collective-permute-done.43
  653.0 12.5 %all-to-all-done.4 = bf16[8,192,768]{2,1,0:T(8,128)(2,1)} async-done(((bf16[8,192,768]{2,1,0:T(8,128)(2,1)}), bf16[8,192,768]{2,1,0:T(8,128)(2,1)}, u32[]{:S(2)}, u32[]{:S(2)}) %all-to-all-start.4) | async-done | bytes 2359328 | tf_op jit(solution)/shard_map/all_to_all | solution.py:706
  665.5 4.0 fusion.10
  669.4 3.8 copy.354
  673.3 5.6 all-to-all-start.6
  685.1 4.1 stack.57
  691.7 6.3 constant_dynamic-slice_fusion.2
  714.4 4.5 fusion.9
  718.9 3.8 copy.352
  722.7 12.2 %all-to-all-done.6 = bf16[4,192,1088]{2,1,0:T(8,128)(2,1)} async-done(((bf16[4,192,1088]{2,1,0:T(8,128)(2,1)}), bf16[4,192,1088]{2,1,0:T(8,128)(2,1)}, u32[]{:S(2)}, u32[]{:S(2)}) %all-to-all-start.6) | async-done | bytes 1671200 | tf_op jit(solution)/shard_map/all_to_all | solution.py:45
  734.9 19.5 %all-to-all-start.5 = ((bf16[4,192,1088]{2,1,0:T(8,128)(2,1)}), bf16[4,192,1088]{2,1,0:T(8,128)(2,1)}, u32[]{:S(2)}, u32[]{:S(2)}) async-start(bf16[4,192,1088]{2,1,0:T(8,128)(2,1)} %bitcast.297), calls=%async_computation.5 | async-start | bytes 3538944 | tf_op jit(solution)/shard_map/all_to_all | solution.py:45
  754.4 29.4 %collective-permute-done.51 = bf16[2,272,544]{2,1,0:T(8,128)(2,1)} collective-permute-done((bf16[2,272,544]{2,1,0:T(8,128)(2,1)}, bf16[2,272,544]{2,1,0:T(8,128)(2,1)}, u32[]{:S(2)}, u32[]{:S(2)}) %collective-permute-start.51) | collective-permute-done | bytes 591904 | tf_op jit(solution)/shard_map/ppermute | solution.py:90
  788.2 14.7 %collective-permute-done.29 = bf16[2,136,960]{2,1,0:T(8,128)(2,1)S(1)} collective-permute-done((bf16[2,136,960]{2,1,0:T(8,128)(2,1)S(1)}, bf16[2,136,960]{2,1,0:T(8,128)(2,1)S(1)}, u32[]{:S(2)}, u32[]{:S(2)}) %collective-permute-start.29) | collective-permute-done | bytes 522272 | tf_op jit(solution)/shard_map/ppermute | solution.py:69
  804.4 7.2 collective-permute-done.30
  823.4 3.3 fusion.38
  826.9 4.1 fusion.37
  835.5 5.3 collective-permute-start.31
  845.2 14.8 %all-to-all-start.7 = ((f32[32,2,1088]{2,1,0:T(2,128)}), f32[32,2,1088]{2,1,0:T(2,128)S(1)}, u32[]{:S(2)}, u32[]{:S(2)}) async-start(f32[32,2,1088]{2,1,0:T(2,128)} %broadcast_in_dim.83), calls=%async_computation.7 | async-start | bytes 589824 | tf_op jit(solution)/shard_map/all_to_all | solution.py:60
  862.9 4.3 collective-permute-done.38
  867.2 3.8 collective-permute-start.39
  (507 shorter events, 218.5 us)
Async XLA Ops:
  7.2 333.0 %all-gather.9.cloned.1.call-start = ((), (), s32[]{:S(2)}) async-start(), calls=%async_computation.10 | async-start | bytes 2820096 | tf_op jit(solution)/shard_map/all_gather | solution.py:533
  15.1 24.8 %collective-permute-start.1 = (bf16[2,192,1088]{2,1,0:T(8,128)(2,1)}, bf16[2,192,1088]{2,1,0:T(8,128)(2,1)S(1)}, u32[]{:S(2)}, u32[]{:S(2)}) collective-permute-start(bf16[2,192,1088]{2,1,0:T(8,128)(2,1)} %bitcast.313), channel_id=1, source_target_pairs={{1,0},{2,1},{3,2},{5,4},{6,5},{7,6},{9,8},{10,9},{11,10},{13,12},{... | collective-permute-start | bytes 2506760 | tf_op jit(solution)/shard_map/ppermute | solution.py:33
  16.4 25.7 %collective-permute-start = (bf16[2,192,1088]{2,1,0:T(8,128)(2,1)}, bf16[2,192,1088]{2,1,0:T(8,128)(2,1)}, u32[]{:S(2)}, u32[]{:S(2)}) collective-permute-start(bf16[2,192,1088]{2,1,0:T(8,128)(2,1)} %bitcast.314), channel_id=1, source_target_pairs={{0,1},{1,2},{2,3},{4,5},{5,6},{6,7},{8,9},{9,10},{10,11},{12,13},{... | collective-permute-start | bytes 2506760 | tf_op jit(solution)/shard_map/ppermute | solution.py:32
  40.8 22.8 %collective-permute-start.2 = (bf16[2,192,1088]{2,1,0:T(8,128)(2,1)S(1)}, bf16[2,192,1088]{2,1,0:T(8,128)(2,1)}, u32[]{:S(2)}, u32[]{:S(2)}) collective-permute-start(bf16[2,192,1088]{2,1,0:T(8,128)(2,1)S(1)} %collective-permute-done.1), channel_id=1, source_target_pairs={{1,0},{2,1},{3,2},{5,4},{6,5},{7,6},{9,8},{10,9},{11,10},{13,12},{... | collective-permute-start | bytes 2506760 | tf_op jit(solution)/shard_map/ppermute | solution.py:33
  42.1 27.7 %collective-permute-start.4 = (bf16[2,192,1088]{2,1,0:T(8,128)(2,1)}, bf16[2,192,1088]{2,1,0:T(8,128)(2,1)}, u32[]{:S(2)}, u32[]{:S(2)}) collective-permute-start(bf16[2,192,1088]{2,1,0:T(8,128)(2,1)} %collective-permute-done), channel_id=1, source_target_pairs={{0,1},{1,2},{2,3},{4,5},{5,6},{6,7},{8,9},{9,10},{10,11},{12,13},{... | collective-permute-start | bytes 2506760 | tf_op jit(solution)/shard_map/ppermute | solution.py:32
  63.7 22.1 %collective-permute-start.3 = (bf16[2,192,1088]{2,1,0:T(8,128)(2,1)}, bf16[2,192,1088]{2,1,0:T(8,128)(2,1)}, u32[]{:S(2)}, u32[]{:S(2)}) collective-permute-start(bf16[2,192,1088]{2,1,0:T(8,128)(2,1)} %collective-permute-done.2), channel_id=1, source_target_pairs={{1,0},{2,1},{3,2},{5,4},{6,5},{7,6},{9,8},{10,9},{11,10},{13,12},{... | collective-permute-start | bytes 2506760 | tf_op jit(solution)/shard_map/ppermute | solution.py:33
  69.9 22.0 %collective-permute-start.5 = (bf16[2,192,1088]{2,1,0:T(8,128)(2,1)}, bf16[2,192,1088]{2,1,0:T(8,128)(2,1)S(1)}, u32[]{:S(2)}, u32[]{:S(2)}) collective-permute-start(bf16[2,192,1088]{2,1,0:T(8,128)(2,1)} %collective-permute-done.4), channel_id=1, source_target_pairs={{0,1},{1,2},{2,3},{4,5},{5,6},{6,7},{8,9},{9,10},{10,11},{12,13},{... | collective-permute-start | bytes 2506760 | tf_op jit(solution)/shard_map/ppermute | solution.py:32
  93.0 278.7 %all-gather.5.cloned.1.call-start = ((), (), s32[]{:S(2)}) async-start(), calls=%async_computation.8 | async-start | bytes 5326848 | tf_op jit(solution)/shard_map/all_gather | solution.py:539
  98.0 144.9 %collective-permute-start.9 = (bf16[3,64,1088]{2,1,0:T(8,128)(2,1)}, bf16[3,64,1088]{2,1,0:T(8,128)(2,1)}, u32[]{:S(2)}, u32[]{:S(2)}) collective-permute-start(bf16[3,64,1088]{2,1,0:T(8,128)(2,1)} %slice.232), channel_id=1, source_target_pairs={{3,1},{7,5},{11,9},{15,13},{19,17},{23,21},{27,25},{31,29}} | collective-permute-start | bytes 1253384 | tf_op jit(solution)/shard_map/ppermute | solution.py:452
  99.5 143.5 %collective-permute-start.8 = (bf16[3,64,1088]{2,1,0:T(8,128)(2,1)}, bf16[3,64,1088]{2,1,0:T(8,128)(2,1)}, u32[]{:S(2)}, u32[]{:S(2)}) collective-permute-start(bf16[3,64,1088]{2,1,0:T(8,128)(2,1)} %slice.232), channel_id=1, source_target_pairs={{3,0},{7,4},{11,8},{15,12},{19,16},{23,20},{27,24},{31,28}} | collective-permute-start | bytes 1253384 | tf_op jit(solution)/shard_map/ppermute | solution.py:452
  100.8 142.3 %collective-permute-start.10 = (bf16[3,64,1088]{2,1,0:T(8,128)(2,1)}, bf16[3,64,1088]{2,1,0:T(8,128)(2,1)}, u32[]{:S(2)}, u32[]{:S(2)}) collective-permute-start(bf16[3,64,1088]{2,1,0:T(8,128)(2,1)} %slice.232), channel_id=1, source_target_pairs={{3,2},{7,6},{11,10},{15,14},{19,18},{23,22},{27,26},{31,30}} | collective-permute-start | bytes 1253384 | tf_op jit(solution)/shard_map/ppermute | solution.py:452
  103.2 11.4 %collective-permute-start.6 = (bf16[3,48,1088]{2,1,0:T(8,128)(2,1)S(1)}, bf16[3,48,1088]{2,1,0:T(8,128)(2,1)S(1)}, u32[]{:S(2)}, u32[]{:S(2)}) collective-permute-start(bf16[3,48,1088]{2,1,0:T(8,128)(2,1)S(1)} %slice.221), channel_id=1, source_target_pairs={{0,1},{1,2},{2,3},{4,5},{5,6},{6,7},{8,9},{9,10},{10,11},{12,13},{... | collective-permute-start | bytes 940040 | tf_op jit(solution)/shard_map/ppermute | solution.py:442
  107.6 256.3 %collective-permute-start.19 = (bf16[384,1088]{0,1:T(8,128)(2,1)S(1)}, bf16[384,1088]{0,1:T(8,128)(2,1)}, u32[]{:S(2)}, u32[]{:S(2)}) collective-permute-start(bf16[384,1088]{0,1:T(8,128)(2,1)S(1)} %copy-done.12), channel_id=1, source_target_pairs={{0,4},{4,0},{1,5},{5,1},{2,6},{6,2},{3,7},{7,3},{8,12},{12,8},{9,1... | collective-permute-start | bytes 2506760 | tf_op jit(solution)/shard_map/ppermute | solution.py:54
  124.2 43.3 %all-to-all-start = ((bf16[8,192,768]{2,1,0:T(8,128)(2,1)}), bf16[8,192,768]{2,1,0:T(8,128)(2,1)}, u32[]{:S(2)}, u32[]{:S(2)}) async-start(bf16[8,192,768]{2,1,0:T(8,128)(2,1)} %bitcast.22), calls=%async_computation | async-start | bytes 4718592 | tf_op jit(solution)/shard_map/all_to_all | solution.py:569
  128.6 260.0 %all-gather.7.cloned.1.call-start = ((), (), s32[]{:S(2)}) async-start(), calls=%async_computation.9 | async-start | bytes 5326848 | tf_op jit(solution)/shard_map/all_gather | solution.py:540
  169.0 32.6 %collective-permute-start.7 = (bf16[8,128,768]{2,1,0:T(8,128)(2,1)S(1)}, bf16[8,128,768]{2,1,0:T(8,128)(2,1)}, u32[]{:S(2)}, u32[]{:S(2)}) collective-permute-start(bf16[8,128,768]{2,1,0:T(8,128)(2,1)S(1)} %slice.271.pair_ref), channel_id=1, source_target_pairs={{0,4},{4,0},{1,5},{5,1},{2,6},{6,2},{3,7},{7,3},{8,12},{12,8},{9,1... | collective-permute-start | bytes 4718600 | tf_op jit(solution)/shard_map/ppermute | solution.py:54
  235.4 109.2 %all-to-all-start.1 = ((bf16[32,64,192]{2,1,0:T(8,128)(2,1)}), bf16[32,64,192]{2,1,0:T(8,128)(2,1)}, u32[]{:S(2)}, u32[]{:S(2)}) async-start(bf16[32,64,192]{2,1,0:T(8,128)(2,1)} %get-tuple-element.67), calls=%async_computation.1 | async-start | bytes 2097152 | tf_op jit(solution)/shard_map/all_to_all | solution.py:584
  245.0 10.5 %collective-permute-start.13 = (bf16[1,128,384]{2,1,0:T(8,128)(2,1)S(1)}, bf16[1,128,384]{2,1,0:T(8,128)(2,1)S(1)}, u32[]{:S(2)}, u32[]{:S(2)}) collective-permute-start(bf16[1,128,384]{2,1,0:T(8,128)(2,1)S(1)} %slice.277), channel_id=1, source_target_pairs={{0,12},{4,16},{8,20},{12,24},{16,28},{1,13},{5,17},{9,21},{13,25},... | collective-permute-start | bytes 294920 | tf_op jit(solution)/shard_map/ppermute | solution.py:575
  248.3 10.7 %collective-permute-start.12 = (bf16[1,128,384]{2,1,0:T(8,128)(2,1)S(1)}, bf16[1,128,384]{2,1,0:T(8,128)(2,1)S(1)}, u32[]{:S(2)}, u32[]{:S(2)}) collective-permute-start(bf16[1,128,384]{2,1,0:T(8,128)(2,1)S(1)} %slice.277), channel_id=1, source_target_pairs={{0,8},{4,12},{8,16},{12,20},{16,24},{20,28},{1,9},{5,13},{9,17},{1... | collective-permute-start | bytes 294920 | tf_op jit(solution)/shard_map/ppermute | solution.py:575
  251.7 7.3 collective-permute-start.11
  259.1 25.0 %collective-permute-start.16 = (bf16[4,128,384]{2,1,0:T(8,128)(2,1)S(1)}, bf16[4,128,384]{2,1,0:T(8,128)(2,1)S(1)}, u32[]{:S(2)}, u32[]{:S(2)}) collective-permute-start(bf16[4,128,384]{2,1,0:T(8,128)(2,1)S(1)} %pad_maximum_fusion.4), channel_id=1, source_target_pairs={{0,3},{1,0},{2,1},{3,2},{4,7},{5,4},{6,5},{7,6},{8,11},{9,8},{10,9... | collective-permute-start | bytes 1179656 | tf_op jit(solution)/shard_map/ppermute | solution.py:100
  264.4 58.6 %collective-permute-start.15 = (bf16[4,128,384]{2,1,0:T(8,128)(2,1)S(1)}, bf16[4,128,384]{2,1,0:T(8,128)(2,1)S(1)}, u32[]{:S(2)}, u32[]{:S(2)}) collective-permute-start(bf16[4,128,384]{2,1,0:T(8,128)(2,1)S(1)} %pad_maximum_fusion.4), channel_id=1, source_target_pairs={{0,2},{1,3},{2,0},{3,1},{4,6},{5,7},{6,4},{7,5},{8,10},{9,11},{10,... | collective-permute-start | bytes 1179656 | tf_op jit(solution)/shard_map/ppermute | solution.py:100
  264.4 58.6 %collective-permute-start.14 = (bf16[4,128,384]{2,1,0:T(8,128)(2,1)S(1)}, bf16[4,128,384]{2,1,0:T(8,128)(2,1)}, u32[]{:S(2)}, u32[]{:S(2)}) collective-permute-start(bf16[4,128,384]{2,1,0:T(8,128)(2,1)S(1)} %pad_maximum_fusion.4), channel_id=1, source_target_pairs={{0,1},{1,2},{2,3},{3,0},{4,5},{5,6},{6,7},{7,4},{8,9},{9,10},{10,1... | collective-permute-start | bytes 1179656 | tf_op jit(solution)/shard_map/ppermute | solution.py:100
  352.7 19.0 %collective-permute-start.17 = (bf16[384,1088]{0,1:T(8,128)(2,1)S(1)}, bf16[384,1088]{0,1:T(8,128)(2,1)}, u32[]{:S(2)}, u32[]{:S(2)}) collective-permute-start(bf16[384,1088]{0,1:T(8,128)(2,1)S(1)} %add_convert_fusion.1), channel_id=1, source_target_pairs={{0,4},{4,0},{1,5},{5,1},{2,6},{6,2},{3,7},{7,3},{8,12},{12,8},{9,1... | collective-permute-start | bytes 2506760 | tf_op jit(solution)/shard_map/ppermute | solution.py:54
  354.7 8.8 %all-to-all-start.2 = ((bf16[4,2,544]{2,1,0:T(2,128)(2,1)}), bf16[4,2,544]{2,1,0:T(2,128)(2,1)S(1)}, u32[]{:S(2)}, u32[]{:S(2)}) async-start(bf16[4,2,544]{2,1,0:T(2,128)(2,1)} %reshape.758), calls=%async_computation.2 | async-start | bytes 20480 | tf_op jit(solution)/shard_map/all_to_all | solution.py:541
  409.1 20.7 %collective-permute-start.20 = (bf16[384,1088]{0,1:T(8,128)(2,1)S(1)}, bf16[384,1088]{0,1:T(8,128)(2,1)}, u32[]{:S(2)}, u32[]{:S(2)}) collective-permute-start(bf16[384,1088]{0,1:T(8,128)(2,1)S(1)} %slice.357), channel_id=1, source_target_pairs={{0,4},{4,0},{1,5},{5,1},{2,6},{6,2},{3,7},{7,3},{8,12},{12,8},{9,1... | collective-permute-start | bytes 2506760 | tf_op jit(solution)/shard_map/ppermute | solution.py:54
  421.1 176.1 %collective-permute-start.48 = (bf16[2,272,2176]{2,1,0:T(8,128)(2,1)}, bf16[2,272,2176]{2,1,0:T(8,128)(2,1)}, u32[]{:S(2)}, u32[]{:S(2)}) collective-permute-start(bf16[2,272,2176]{2,1,0:T(8,128)(2,1)} %dynamic-slice_bitcast_fusion), channel_id=1, source_target_pairs={{0,16},{8,24},{16,0},{24,8},{1,17},{9,25},{17,1},{25,9},{2,18},{10... | collective-permute-start | bytes 7102472 | tf_op jit(solution)/shard_map/ppermute | solution.py:69
  442.7 45.5 %all-to-all-start.3 = ((bf16[32,64,192]{2,1,0:T(8,128)(2,1)}), bf16[32,64,192]{2,1,0:T(8,128)(2,1)}, u32[]{:S(2)}, u32[]{:S(2)}) async-start(bf16[32,64,192]{2,1,0:T(8,128)(2,1)} %bitcast.312), calls=%async_computation.3 | async-start | bytes 2097152 | tf_op jit(solution)/shard_map/all_to_all | solution.py:636
  449.7 149.2 %collective-permute-start.46 = (bf16[2,272,2176]{2,1,0:T(8,128)(2,1)}, bf16[2,272,2176]{2,1,0:T(8,128)(2,1)}, u32[]{:S(2)}, u32[]{:S(2)}) collective-permute-start(bf16[2,272,2176]{2,1,0:T(8,128)(2,1)} %dynamic-slice_bitcast_fusion.1), channel_id=1, source_target_pairs={{0,8},{8,0},{16,24},{24,16},{1,9},{9,1},{17,25},{25,17},{2,10},{10... | collective-permute-start | bytes 7102472 | tf_op jit(solution)/shard_map/ppermute | solution.py:69
  463.5 74.6 %collective-permute-start.40 = (bf16[2,272,1088]{2,1,0:T(8,128)(2,1)}, bf16[2,272,1088]{2,1,0:T(8,128)(2,1)}, u32[]{:S(2)}, u32[]{:S(2)}) collective-permute-start(bf16[2,272,1088]{2,1,0:T(8,128)(2,1)} %fusion.53), channel_id=1, source_target_pairs={{0,8},{8,0},{16,24},{24,16},{1,9},{9,1},{17,25},{25,17},{2,10},{10... | collective-permute-start | bytes 3551240 | tf_op jit(solution)/shard_map/ppermute | solution.py:69
  485.4 58.7 %collective-permute-start.24 = (bf16[4,128,384]{2,1,0:T(8,128)(2,1)}, bf16[4,128,384]{2,1,0:T(8,128)(2,1)}, u32[]{:S(2)}, u32[]{:S(2)}) collective-permute-start(bf16[4,128,384]{2,1,0:T(8,128)(2,1)} %get-tuple-element.138), channel_id=1, source_target_pairs={{0,1},{1,2},{2,3},{3,0},{4,5},{5,6},{6,7},{7,4},{8,9},{9,10},{10,1... | collective-permute-start | bytes 1179656 | tf_op jit(solution)/shard_map/ppermute | solution.py:667
  487.3 58.3 %collective-permute-start.23 = (bf16[4,128,384]{2,1,0:T(8,128)(2,1)}, bf16[4,128,384]{2,1,0:T(8,128)(2,1)}, u32[]{:S(2)}, u32[]{:S(2)}) collective-permute-start(bf16[4,128,384]{2,1,0:T(8,128)(2,1)} %get-tuple-element.139), channel_id=1, source_target_pairs={{0,2},{1,3},{2,0},{3,1},{4,6},{5,7},{6,4},{7,5},{8,10},{9,11},{10,... | collective-permute-start | bytes 1179656 | tf_op jit(solution)/shard_map/ppermute | solution.py:667
  538.2 12.0 %collective-permute-start.22 = (bf16[4,128,384]{2,1,0:T(8,128)(2,1)}, bf16[4,128,384]{2,1,0:T(8,128)(2,1)S(1)}, u32[]{:S(2)}, u32[]{:S(2)}) collective-permute-start(bf16[4,128,384]{2,1,0:T(8,128)(2,1)} %get-tuple-element.140), channel_id=1, source_target_pairs={{0,3},{1,0},{2,1},{3,2},{4,7},{5,4},{6,5},{7,6},{8,11},{9,8},{10,9... | collective-permute-start | bytes 1179656 | tf_op jit(solution)/shard_map/ppermute | solution.py:667
  544.1 69.4 %collective-permute-start.41 = (bf16[272,1088]{1,0:T(8,128)(2,1)}, bf16[272,1088]{1,0:T(8,128)(2,1)}, u32[]{:S(2)}, u32[]{:S(2)}) collective-permute-start(bf16[272,1088]{1,0:T(8,128)(2,1)} %dynamic-slice_bitcast_fusion.4), channel_id=1, source_target_pairs={{0,16},{8,24},{16,0},{24,8},{1,17},{9,25},{17,1},{25,9},{2,18},{10... | collective-permute-start | bytes 1775624 | tf_op jit(solution)/shard_map/ppermute | solution.py:69
  552.4 56.1 %collective-permute-start.27 = (bf16[128,384]{1,0:T(8,128)(2,1)S(1)}, bf16[128,384]{1,0:T(8,128)(2,1)S(1)}, u32[]{:S(2)}, u32[]{:S(2)}) collective-permute-start(bf16[128,384]{1,0:T(8,128)(2,1)S(1)} %get-tuple-element.151), channel_id=1, source_target_pairs={{12,0},{16,4},{20,8},{24,12},{28,16},{13,1},{17,5},{21,9},{25,13},... | collective-permute-start | bytes 294920 | tf_op jit(solution)/shard_map/ppermute | solution.py:675
  553.7 57.5 %collective-permute-start.26 = (bf16[128,384]{1,0:T(8,128)(2,1)S(1)}, bf16[128,384]{1,0:T(8,128)(2,1)S(1)}, u32[]{:S(2)}, u32[]{:S(2)}) collective-permute-start(bf16[128,384]{1,0:T(8,128)(2,1)S(1)} %get-tuple-element.152), channel_id=1, source_target_pairs={{8,0},{12,4},{16,8},{20,12},{24,16},{28,20},{9,1},{13,5},{17,9},{2... | collective-permute-start | bytes 294920 | tf_op jit(solution)/shard_map/ppermute | solution.py:675
  597.2 16.2 %collective-permute-start.25 = (bf16[128,384]{1,0:T(8,128)(2,1)S(1)}, bf16[128,384]{1,0:T(8,128)(2,1)S(1)}, u32[]{:S(2)}, u32[]{:S(2)}) collective-permute-start(bf16[128,384]{1,0:T(8,128)(2,1)S(1)} %get-tuple-element.153), channel_id=1, source_target_pairs={{4,0},{8,4},{12,8},{16,12},{20,16},{24,20},{28,24},{5,1},{9,5},{13... | collective-permute-start | bytes 294920 | tf_op jit(solution)/shard_map/ppermute | solution.py:675
  599.0 14.5 %collective-permute-start.21 = (bf16[8,128,768]{2,1,0:T(8,128)(2,1)}, bf16[8,128,768]{2,1,0:T(8,128)(2,1)S(1)}, u32[]{:S(2)}, u32[]{:S(2)}) collective-permute-start(bf16[8,128,768]{2,1,0:T(8,128)(2,1)} %get-tuple-element.82), channel_id=1, source_target_pairs={{0,4},{4,0},{1,5},{5,1},{2,6},{6,2},{3,7},{7,3},{8,12},{12,8},{9,1... | collective-permute-start | bytes 4718600 | tf_op jit(solution)/shard_map/ppermute | solution.py:54
  608.5 41.4 %collective-permute-start.49 = (bf16[272,2176]{1,0:T(8,128)(2,1)}, bf16[272,2176]{1,0:T(8,128)(2,1)}, u32[]{:S(2)}, u32[]{:S(2)}) collective-permute-start(bf16[272,2176]{1,0:T(8,128)(2,1)} %dynamic-slice_bitcast_fusion.2), channel_id=1, source_target_pairs={{0,8},{8,0},{16,24},{24,16},{1,9},{9,1},{17,25},{25,17},{2,10},{10... | collective-permute-start | bytes 3551240 | tf_op jit(solution)/shard_map/ppermute | solution.py:69
  611.3 38.7 %collective-permute-start.47 = (bf16[272,2176]{1,0:T(8,128)(2,1)}, bf16[272,2176]{1,0:T(8,128)(2,1)}, u32[]{:S(2)}, u32[]{:S(2)}) collective-permute-start(bf16[272,2176]{1,0:T(8,128)(2,1)} %dynamic-slice_bitcast_fusion.3), channel_id=1, source_target_pairs={{0,16},{8,24},{16,0},{24,8},{1,17},{9,25},{17,1},{25,9},{2,18},{10... | collective-permute-start | bytes 3551240 | tf_op jit(solution)/shard_map/ppermute | solution.py:69
  617.1 48.3 %all-to-all-start.4 = ((bf16[8,192,768]{2,1,0:T(8,128)(2,1)}), bf16[8,192,768]{2,1,0:T(8,128)(2,1)}, u32[]{:S(2)}, u32[]{:S(2)}) async-start(bf16[8,192,768]{2,1,0:T(8,128)(2,1)} %pad_maximum_fusion), calls=%async_computation.4 | async-start | bytes 4718592 | tf_op jit(solution)/shard_map/all_to_all | solution.py:706
  625.4 9.8 %collective-permute-start.44 = (bf16[272,272]{1,0:T(8,128)(2,1)S(1)}, bf16[272,272]{1,0:T(8,128)(2,1)S(1)}, u32[]{:S(2)}, u32[]{:S(2)}) collective-permute-start(bf16[272,272]{1,0:T(8,128)(2,1)S(1)} %bitcast.336), channel_id=1, source_target_pairs={{0,3},{1,0},{2,1},{3,2},{4,7},{5,4},{6,5},{7,6},{8,11},{9,8},{10,9... | collective-permute-start | bytes 443912 | tf_op jit(solution)/shard_map/ppermute | solution.py:90
  629.6 10.6 %collective-permute-start.42 = (bf16[272,272]{1,0:T(8,128)(2,1)S(1)}, bf16[272,272]{1,0:T(8,128)(2,1)S(1)}, u32[]{:S(2)}, u32[]{:S(2)}) collective-permute-start(bf16[272,272]{1,0:T(8,128)(2,1)S(1)} %bitcast.335), channel_id=1, source_target_pairs={{0,1},{1,2},{2,3},{3,0},{4,5},{5,6},{6,7},{7,4},{8,9},{9,10},{10,1... | collective-permute-start | bytes 443912 | tf_op jit(solution)/shard_map/ppermute | solution.py:90
  629.6 17.0 %collective-permute-start.43 = (bf16[272,272]{1,0:T(8,128)(2,1)S(1)}, bf16[272,272]{1,0:T(8,128)(2,1)S(1)}, u32[]{:S(2)}, u32[]{:S(2)}) collective-permute-start(bf16[272,272]{1,0:T(8,128)(2,1)S(1)} %bitcast.334), channel_id=1, source_target_pairs={{0,2},{1,3},{2,0},{3,1},{4,6},{5,7},{6,4},{7,5},{8,10},{9,11},{10,... | collective-permute-start | bytes 443912 | tf_op jit(solution)/shard_map/ppermute | solution.py:90
  635.2 191.5 %collective-permute-start.18 = (bf16[384,1088]{0,1:T(8,128)(2,1)}, bf16[384,1088]{0,1:T(8,128)(2,1)}, u32[]{:S(2)}, u32[]{:S(2)}) collective-permute-start(bf16[384,1088]{0,1:T(8,128)(2,1)} %slice.358), channel_id=1, source_target_pairs={{0,4},{4,0},{1,5},{5,1},{2,6},{6,2},{3,7},{7,3},{8,12},{12,8},{9,1... | collective-permute-start | bytes 2506760 | tf_op jit(solution)/shard_map/ppermute | solution.py:54
  646.8 2.5 collective-permute-start.45
  673.3 61.7 %all-to-all-start.6 = ((bf16[4,192,1088]{2,1,0:T(8,128)(2,1)}), bf16[4,192,1088]{2,1,0:T(8,128)(2,1)}, u32[]{:S(2)}, u32[]{:S(2)}) async-start(bf16[4,192,1088]{2,1,0:T(8,128)(2,1)} %bitcast.52), calls=%async_computation.6 | async-start | bytes 3538944 | tf_op jit(solution)/shard_map/all_to_all | solution.py:45
  700.8 83.0 %collective-permute-start.51 = (bf16[2,272,544]{2,1,0:T(8,128)(2,1)}, bf16[2,272,544]{2,1,0:T(8,128)(2,1)}, u32[]{:S(2)}, u32[]{:S(2)}) collective-permute-start(bf16[2,272,544]{2,1,0:T(8,128)(2,1)} %bitcast.289), channel_id=1, source_target_pairs={{0,2},{1,3},{2,0},{3,1},{4,6},{5,7},{6,4},{7,5},{8,10},{9,11},{10,... | collective-permute-start | bytes 1775624 | tf_op jit(solution)/shard_map/ppermute | solution.py:90
  703.7 80.1 %collective-permute-start.52 = (bf16[2,272,544]{2,1,0:T(8,128)(2,1)}, bf16[2,272,544]{2,1,0:T(8,128)(2,1)}, u32[]{:S(2)}, u32[]{:S(2)}) collective-permute-start(bf16[2,272,544]{2,1,0:T(8,128)(2,1)} %bitcast.288), channel_id=1, source_target_pairs={{0,3},{1,0},{2,1},{3,2},{4,7},{5,4},{6,5},{7,6},{8,11},{9,8},{10,9... | collective-permute-start | bytes 1775624 | tf_op jit(solution)/shard_map/ppermute | solution.py:90
  705.2 78.6 %collective-permute-start.50 = (bf16[2,272,544]{2,1,0:T(8,128)(2,1)}, bf16[2,272,544]{2,1,0:T(8,128)(2,1)}, u32[]{:S(2)}, u32[]{:S(2)}) collective-permute-start(bf16[2,272,544]{2,1,0:T(8,128)(2,1)} %bitcast.290), channel_id=1, source_target_pairs={{0,1},{1,2},{2,3},{3,0},{4,5},{5,6},{6,7},{7,4},{8,9},{9,10},{10,1... | collective-permute-start | bytes 1775624 | tf_op jit(solution)/shard_map/ppermute | solution.py:90
  713.4 72.8 %collective-permute-start.28 = (bf16[2,2,136,960]{3,2,1,0:T(8,128)(2,1)}, bf16[2,2,136,960]{3,2,1,0:T(8,128)(2,1)}, u32[]{:S(2)}, u32[]{:S(2)}) collective-permute-start(bf16[2,2,136,960]{3,2,1,0:T(8,128)(2,1)} %fusion.62), channel_id=1, source_target_pairs={{0,4},{4,0},{1,5},{5,1},{2,6},{6,2},{3,7},{7,3},{8,12},{12,8},{9,1... | collective-permute-start | bytes 3133448 | tf_op jit(solution)/shard_map/ppermute | solution.py:54
  734.9 81.7 %all-to-all-start.5 = ((bf16[4,192,1088]{2,1,0:T(8,128)(2,1)}), bf16[4,192,1088]{2,1,0:T(8,128)(2,1)}, u32[]{:S(2)}, u32[]{:S(2)}) async-start(bf16[4,192,1088]{2,1,0:T(8,128)(2,1)} %bitcast.297), calls=%async_computation.5 | async-start | bytes 3538944 | tf_op jit(solution)/shard_map/all_to_all | solution.py:45
  786.1 1.8 collective-permute-start.53
  787.9 15.1 %collective-permute-start.29 = (bf16[2,136,960]{2,1,0:T(8,128)(2,1)S(1)}, bf16[2,136,960]{2,1,0:T(8,128)(2,1)S(1)}, u32[]{:S(2)}, u32[]{:S(2)}) collective-permute-start(bf16[2,136,960]{2,1,0:T(8,128)(2,1)S(1)} %dynamic-slice_bitcast_fusion.5), channel_id=1, source_target_pairs={{0,8},{8,0},{16,24},{24,16},{1,9},{9,1},{17,25},{25,17},{2,10},{10... | collective-permute-start | bytes 1566728 | tf_op jit(solution)/shard_map/ppermute | solution.py:69
  803.2 8.4 collective-permute-start.30
  832.4 10.5 %collective-permute-start.36 = (f32[10880]{0:T(1024)S(1)}, f32[10880]{0:T(1024)S(1)}, u32[]{:S(2)}, u32[]{:S(2)}) collective-permute-start(f32[10880]{0:T(1024)S(1)} %add.891), channel_id=1, source_target_pairs={{0,8},{8,0},{16,24},{24,16},{1,9},{9,1},{17,25},{25,17},{2,10},{10... | collective-permute-start | bytes 130568 | tf_op jit(solution)/shard_map/ppermute | solution.py:109
  834.2 27.7 %collective-permute-start.33 = (bf16[3,64,136]{1,2,0:T(8,128)(2,1)S(1)}, bf16[3,64,136]{1,2,0:T(8,128)(2,1)S(1)}, u32[]{:S(2)}, u32[]{:S(2)}) collective-permute-start(bf16[3,64,136]{1,2,0:T(8,128)(2,1)S(1)} %copy.364), channel_id=1, source_target_pairs={{2,3},{6,7},{10,11},{14,15},{18,19},{22,23},{26,27},{30,31}} | collective-permute-start | bytes 156680 | tf_op jit(solution)/shard_map/ppermute | solution.py:763
  834.8 27.0 %collective-permute-start.32 = (bf16[3,64,136]{1,2,0:T(8,128)(2,1)S(1)}, bf16[3,64,136]{1,2,0:T(8,128)(2,1)S(1)}, u32[]{:S(2)}, u32[]{:S(2)}) collective-permute-start(bf16[3,64,136]{1,2,0:T(8,128)(2,1)S(1)} %copy.364), channel_id=1, source_target_pairs={{1,3},{5,7},{9,11},{13,15},{17,19},{21,23},{25,27},{29,31}} | collective-permute-start | bytes 156680 | tf_op jit(solution)/shard_map/ppermute | solution.py:763
  835.5 26.4 %collective-permute-start.31 = (bf16[3,64,136]{1,2,0:T(8,128)(2,1)S(1)}, bf16[3,64,136]{1,2,0:T(8,128)(2,1)}, u32[]{:S(2)}, u32[]{:S(2)}) collective-permute-start(bf16[3,64,136]{1,2,0:T(8,128)(2,1)S(1)} %copy.364), channel_id=1, source_target_pairs={{0,3},{4,7},{8,11},{12,15},{16,19},{20,23},{24,27},{28,31}} | collective-permute-start | bytes 156680 | tf_op jit(solution)/shard_map/ppermute | solution.py:763
  841.6 20.3 %collective-permute-start.34 = (bf16[3,48,136]{1,2,0:T(8,128)(2,1)S(1)}, bf16[3,48,136]{1,2,0:T(8,128)(2,1)}, u32[]{:S(2)}, u32[]{:S(2)}) collective-permute-start(bf16[3,48,136]{1,2,0:T(8,128)(2,1)S(1)} %slice.293), channel_id=1, source_target_pairs={{1,0},{2,1},{3,2},{5,4},{6,5},{7,6},{9,8},{10,9},{11,10},{13,12},{... | collective-permute-start | bytes 117512 | tf_op jit(solution)/shard_map/ppermute | solution.py:459
  842.9 17.1 %collective-permute-start.37 = (f32[10880]{0:T(1024)S(1)}, f32[10880]{0:T(1024)S(1)}, u32[]{:S(2)}, u32[]{:S(2)}) collective-permute-start(f32[10880]{0:T(1024)S(1)} %add.892), channel_id=1, source_target_pairs={{0,16},{8,24},{16,0},{24,8},{1,17},{9,25},{17,1},{25,9},{2,18},{10... | collective-permute-start | bytes 130568 | tf_op jit(solution)/shard_map/ppermute | solution.py:109
  845.2 30.4 %all-to-all-start.7 = ((f32[32,2,1088]{2,1,0:T(2,128)}), f32[32,2,1088]{2,1,0:T(2,128)S(1)}, u32[]{:S(2)}, u32[]{:S(2)}) async-start(f32[32,2,1088]{2,1,0:T(2,128)} %broadcast_in_dim.83), calls=%async_computation.7 | async-start | bytes 589824 | tf_op jit(solution)/shard_map/all_to_all | solution.py:60
  860.0 7.2 collective-permute-start.38
  867.2 6.3 collective-permute-start.39
  (89 other events, 1249.6 us)
Sparse Core Ops, SparseCore 0:
  93.1 80.6 all-gather.8
  176.5 102.8 all-gather.4
  282.1 101.0 all-gather.6

commit v3 on v2

--- a/solution.py
+++ b/solution.py
@@ -1,5 +1,3 @@
-import functools
-
 import jax
 import jax.numpy as jnp
 from jax import lax
@@ -59,6 +57,10 @@
     copies = jnp.broadcast_to(value[None], (count,) + value.shape)
     arrived = lax.all_to_all(copies, everywhere, split_axis=0, concat_axis=0, tiled=True)
     return jnp.sum(arrived, axis=0)
+
+
+def nothing(value):
+    return jnp.minimum(jnp.abs(value[(0,) * value.ndim].astype(jnp.float32)), 0.0)
 
 
 def pick(value, index, axis):
@@ -339,7 +341,7 @@
         lax.fori_loop(0, count, finish, 0)
 
 
-def attention_call(kernel, ends, queries, pairs, plan, more, part, outs, scratch, flops):
+def attention_call(kernel, ends, queries, pairs, plan, more, part, outs, scratch, flops, tokens):
     numbers, rows, column = plan
     groups, _, width = queries.shape
     key_groups, _, key_width = pairs.shape
@@ -376,15 +378,22 @@
         "rows": pltpu.VMEM((count, tile, HEAD_DIM), jnp.bfloat16),
         "keys": pltpu.VMEM((key_tile, HEAD_DIM), jnp.float32),
     }
+    position = 5 + len(more)
+
+    def body(*refs):
+        kernel(dims, ends, *refs[:position], *refs[position + len(tokens) :])
+
+    dims = (blocks, groups, per_query, per_key, tile, key_tile, part)
     pairs_near = groups * width * min(key_groups * key_width, 2304)
     return pl.pallas_call(
-        functools.partial(kernel, (blocks, groups, per_query, per_key, tile, key_tile, part), ends),
+        body,
         out_shape=out_shapes,
         grid_spec=pltpu.PrefetchScalarGridSpec(
             num_scalar_prefetch=1,
             grid=(blocks,),
             in_specs=[whole(queries), pair_spec, whole(rows), whole(column)]
-            + [whole(array) for array in more],
+            + [whole(array) for array in more]
+            + [pl.BlockSpec(memory_space=pl.ANY)] * len(tokens),
             out_specs=out_specs,
             scratch_shapes=[sizes[name] for name in scratch],
         ),
@@ -396,10 +405,10 @@
             bytes_accessed=4 * queries.size + 4 * pairs.size,
             transcendentals=pairs_near,
         ),
-    )(numbers, queries, pairs, rows, column, *more)
-
-
-def attend(queries, pairs, plans, part):
+    )(numbers, queries, pairs, rows, column, *more, *tokens)
+
+
+def attend(queries, pairs, plans, part, tokens):
     state = ()
     for index, (keys, plan) in enumerate(zip(pairs, plans)):
         ends = (index == 0, index == len(pairs) - 1)
@@ -416,11 +425,12 @@
             ("out", "low", "row") if ends[1] else ("acc", "row", "row"),
             ("acc", "row", "row"),
             16,
+            tuple(tokens) if ends[1] else (),
         )
     return state
 
 
-def attend_back(queries, keys, plan, known, state, final):
+def attend_back(queries, keys, plan, known, state, final, tokens):
     return attention_call(
         backward_kernel,
         (not state, final),
@@ -432,6 +442,7 @@
         ("grads" if final else "acc", "pairs"),
         ("acc", "row", "cols", "rows", "rows", "keys", "keys"),
         40,
+        tokens,
     )
 
 
@@ -525,23 +536,26 @@
 
     half = unit_slab // 2
     quarter = half // chips
-    if slab % chips == 0:
-        out_rows = slab // chips
-        out_piece = after(
-            lax.dynamic_slice_in_dim(w_out, chip_index * out_rows, out_rows, 0), wide_one
-        )
-        full_out = lax.all_gather(out_piece, sharers, axis=0, tiled=True)
+    unit_start = core_index * half + chip_index * quarter
+    up_piece = lax.dynamic_slice_in_dim(w_up, unit_start, quarter, 1).T
+    down_piece = lax.dynamic_slice_in_dim(w_down, unit_start, quarter, 0)
+    bias_row = lax.dynamic_slice_in_dim(b_up, unit_start, quarter, 0)
+    bias_row = jnp.pad(bias_row, (0, width - quarter))[None]
+    out_rows = slab // chips if slab % chips == 0 else 0
+    padded = -(-(out_rows + 1) // 8) * 8
+    out_piece = lax.dynamic_slice_in_dim(w_out, chip_index * out_rows, out_rows, 0)
+    filler = jnp.zeros((padded - out_rows - 1, width), low)
+    pieces = [out_piece, bias_row, filler, up_piece, down_piece]
+    pieces = jnp.concatenate(pieces, axis=0) + nothing(wide_one).astype(low)
+    gathered = lax.all_gather(pieces, sharers, axis=0, tiled=True)
+    gathered = gathered.reshape(tensor_size * chips, -1, width)
+    up_bias = gathered[:, out_rows, :quarter].reshape(-1)
+    if out_rows:
+        full_out = gathered[:, :out_rows].reshape(width, width)
     else:
         full_out = lax.all_gather(w_out, "tensor", axis=0, tiled=True)
-    unit_start = core_index * half + chip_index * quarter
-    up_piece = after(lax.dynamic_slice_in_dim(w_up, unit_start, quarter, 1).T, wide_one)
-    down_piece = after(lax.dynamic_slice_in_dim(w_down, unit_start, quarter, 0), wide_one)
-    half_up = lax.all_gather(up_piece, sharers, axis=0, tiled=True)
-    half_down = lax.all_gather(down_piece, sharers, axis=0, tiled=True)
-    up_bias = lax.all_to_all(
-        jnp.broadcast_to(b_up[None], (tensor_size, unit_slab)), "tensor", 0, 0, tiled=True
-    )
-    up_bias = lax.dynamic_slice_in_dim(up_bias, core_index * half, half, 1).reshape(-1)
+    half_up = gathered[:, padded : padded + quarter].reshape(-1, width)
+    half_down = gathered[:, padded + quarter :].reshape(-1, width)
     wide_grad = jnp.concatenate((cotangent, other_core(cotangent)), axis=0)
 
     offsets = jnp.arange(tensor_size, dtype=jnp.int32)[:, None] * rows
@@ -580,11 +594,11 @@
         pairs = [own_pairs, other_core(own_pairs)]
     else:
         pairs = [lax.all_gather(own_pairs, layer, axis_index_groups=sharing, axis=0, tiled=True)]
-    mixed, mixed_low, total = attend(qkv, pairs, plans, part)
+    mixed, mixed_low, total = attend(qkv, pairs, plans, part, last_blocks)
     attended = lax.all_to_all(mixed_low, everywhere, split_axis=0, concat_axis=0, tiled=True)
-    last_pairs = jnp.concatenate(after(last_blocks, total), axis=0)
+    last_pairs = jnp.concatenate(last_blocks, axis=0)
     last_mixed, last_low, last_total = attend(
-        after(last_qkv, total), [last_pairs], [last_plan], rows
+        after(last_qkv, total), [last_pairs], [last_plan], rows, ()
     )
 
     attended = attended.reshape(slots, members, tensor_size, HEAD_DIM, part)
@@ -639,7 +653,7 @@
     )
     last_grads = last_grads.astype(low)[None]
     last_query_grad, last_pair_grad = attend_back(
-        last_qkv, last_pairs, last_plan, (last_grads, last_mixed, last_total), (), True
+        last_qkv, last_pairs, last_plan, (last_grads, last_mixed, last_total), (), True, ()
     )
     column = width // dp_size
     grad_down = lax.dot_general(
@@ -667,7 +681,7 @@
         last_arrived.append(lax.ppermute(last_pair_grad[step], "tensor", back))
     known = (grads, mixed, total)
     if members == 2:
-        query_state, pair_grad = attend_back(qkv, pairs[1], plans[1], known, (), False)
+        query_state, pair_grad = attend_back(qkv, pairs[1], plans[1], known, (), False, ())
         other_grad = other_core(pair_grad)
         last_arrived = after(last_arrived, query_state)
         last_arrived = sum(block.astype(jnp.float32) for block in last_arrived)
@@ -681,7 +695,7 @@
             grad_up = halve(grad_up.reshape(blocked), 1, flip(1), low_bit, query_state)
             grad_out = halve(grad_out.reshape(blocked), 1, flip(1), low_bit, query_state)
         query_grad, pair_grad = attend_back(
-            qkv, pairs[0], plans[0], known, (query_state,), True
+            qkv, pairs[0], plans[0], known, (query_state,), True, (grad_down, grad_up, grad_out)
         )
         if chips == 4:
             grad_down = halve(grad_down, 0, flip(1), low_bit, query_grad)
@@ -697,7 +711,7 @@
         for step in range(1, steps_back):
             arrived = lax.ppermute(last_arrived[step].astype(low), layer, line(dp_size, -step))
             last_sum = last_sum + arrived.astype(jnp.float32)
-        query_grad, pair_grad = attend_back(qkv, pairs[0], plans[0], known, (), True)
+        query_grad, pair_grad = attend_back(qkv, pairs[0], plans[0], known, (), True, ())
         pair_grad = pair_grad.reshape(members, dp_size, 2 * HEAD_DIM, lanes)
         pair_grad = lax.all_to_all(pair_grad, layer, 0, 0, axis_index_groups=sharing, tiled=True)
         pair_sum = jnp.sum(pair_grad.astype(jnp.float32), axis=0)
@@ -707,25 +721,45 @@
     qkv_grad = qkv_grad.reshape(slots, members, 3 * HEAD_DIM, lanes)
     last_qkv_grad = jnp.concatenate((last_query_grad[0], last_pair_grad), axis=0)
 
+    units = jnp.stack((grad_up, grad_down)).reshape(2, 2 * column, tensor_size, half)
+    units = units.transpose(2, 0, 1, 3)
+    units = scatter_ring(units)
+    zero = nothing(units)
     grad_normed_one = []
     for piece in range(members):
         product = jnp.einsum(
             "cfd,cft->dt", qkv_w, qkv_grad[:, piece], preferred_element_type=jnp.float32
         )
-        product = product.astype(low).T.reshape(tensor_size, part, width)
+        product = (product + zero).astype(low).T.reshape(tensor_size, part, width)
         grad_normed_one.append(scatter_tensor(product))
     grad_normed_one = jnp.concatenate(grad_normed_one, axis=0)
     last_normed_one = lax.dot_general(
         last_qkv_grad, last_qkv_w, contract_first, preferred_element_type=jnp.float32
     )
-    grad_normed_one = grad_normed_one + last_normed_one
+    head = tensor_index * slots + lax.div(dp_index, members)
+    own_sums = (jnp.sum(query_grad.astype(jnp.float32), axis=(0, 2)),)
+    own_sums += (jnp.sum(pair_sum[:, HEAD_DIM:], axis=(0, 2)),)
+    last_sums = jnp.sum(last_qkv_grad.astype(jnp.float32), axis=1).reshape(3, HEAD_DIM)
+    qv_sum = jnp.zeros((2, HEADS, HEAD_DIM), jnp.float32).at[:, HEADS - 1].set(last_sums[::2])
+    qv_sum = lax.dynamic_update_slice_in_dim(qv_sum, jnp.stack(own_sums)[:, None], head, 1)
+    up_full = lax.dynamic_update_slice_in_dim(
+        jnp.zeros((tensor_size, unit_slab), jnp.float32),
+        grad_up_part.reshape(tensor_size, half),
+        core_index * half,
+        1,
+    ).reshape(-1)
+    early = jnp.concatenate(
+        (grad_out_bias, grad_gain_two, grad_shift_two, grad_down_bias, up_full, qv_sum.reshape(-1))
+    )
+    early = butterfly(early)
+    qv_sum = early[-2 * width :].reshape(2, width)
+    early, up_sum = early[: 4 * width].reshape(4, width), early[4 * width : -2 * width]
+    grad_normed_one = grad_normed_one + last_normed_one + nothing(early)
     grad_res_one, grad_gain_one, grad_shift_one = norm_backward(
         grad_normed_one, normed_one, inv_one, gain_one
     )
     grad_input = grad_stream_one + grad_res_one
 
-    units = jnp.stack((grad_up, grad_down)).reshape(2, 2 * column, tensor_size, half)
-    units = scatter_ring(units.transpose(2, 0, 1, 3))
     units = units.astype(low).reshape(2, 2, column, half)
     kept = pick(units, core_index, 1)
     arrived = other_core(pick(units, 1 - core_index, 1))
@@ -765,24 +799,6 @@
     grad_qkv = slab_rows(own_qkv_grad, last_sum.astype(low), slab, tensor_size, tensor_index)
     grad_qkv = grad_qkv.astype(jnp.float32)
 
-    head = tensor_index * slots + lax.div(dp_index, members)
-    own_sums = (jnp.sum(query_grad.astype(jnp.float32), axis=(0, 2)),)
-    own_sums += (jnp.sum(pair_sum[:, HEAD_DIM:], axis=(0, 2)),)
-    last_sums = jnp.sum(last_qkv_grad.astype(jnp.float32), axis=1).reshape(3, HEAD_DIM)
-    qv_sum = jnp.zeros((2, HEADS, HEAD_DIM), jnp.float32).at[:, HEADS - 1].set(last_sums[::2])
-    qv_sum = lax.dynamic_update_slice_in_dim(qv_sum, jnp.stack(own_sums)[:, None], head, 1)
-    up_full = lax.dynamic_update_slice_in_dim(
-        jnp.zeros((tensor_size, unit_slab), jnp.float32),
-        grad_up_part.reshape(tensor_size, half),
-        core_index * half,
-        1,
-    ).reshape(-1)
-    early = jnp.concatenate(
-        (grad_out_bias, grad_gain_two, grad_shift_two, grad_down_bias, up_full, qv_sum.reshape(-1))
-    )
-    early = butterfly(early)
-    qv_sum = early[-2 * width :].reshape(2, width)
-    early, up_sum = early[: 4 * width].reshape(4, width), early[4 * width : -2 * width]
     late = small_sum(jnp.stack((grad_gain_one, grad_shift_one)))
     grad_up_bias = lax.dynamic_slice_in_dim(up_sum, tensor_index * unit_slab, unit_slab, 0)
     return (

time: 898 us -> 877 us (0.977)
  waiting for transfers between devices: 260 us -> 234 us
  local copies, waits for them, and re-layouts: 117 us -> 130 us
    ppermute x3, waiting for transfers between devices: 54.3 us -> 35 us  [gather_ring(): blocks.append(lax.ppermute(block, 'tensor', ring))]
    all_to_all x2, starting transfers between devices: 25.1 us -> 8.02 us  [scatter_tensor(): lax.all_to_all(partial_sum, 'tensor', split_axis=0, concat_axis=0, tiled=...]
    ppermute x5, waiting for transfers between devices: 6.93 us -> 22.6 us  [butterfly(): lax.ppermute(value, axis, [(i, i ^ step) for i in range(count)])]
    all_to_all x2, waiting for transfers between devices: 14.7 us -> 0.01 us  [scatter_tensor(): lax.all_to_all(partial_sum, 'tensor', split_axis=0, concat_axis=0, tiled=...]
    ppermute x3, starting transfers between devices: 6.36 us -> 20.4 us  [gather_ring(): blocks.append(lax.ppermute(block, 'tensor', ring))]
    slice x1 -> x6, local copies, waits for them, and re-layouts: 0.01 us -> 13.5 us  [the longest x1 8.41 us: local(): half_up = gathered[:, padded:padded + quarter].reshape(-1, width)]
    all_to_all x1, waiting for transfers between devices: 12.5 us -> 0.01 us  [local(): lax.all_to_all(qkv_grad, layer, split_axis=0, concat_axis=0, tiled=True)]
    ppermute x1, waiting for transfers between devices: 0.01 us -> 10.7 us  [slab_rows(): following = lax.ppermute(own[:, :most], 'tensor', line(tensor_size, -1))]
  transfers between devices with their start and end apart: 65 -> 62, of which waited for: 25 -> 23; matrix products, arithmetic and copies ran while one was open for 26% -> 25% of each run, Pallas kernels for 20% -> 20%
where the time goes in v3:
time: 877 us; the launch traced here: 861 us
  waiting for transfers between devices  234 us (27%)
  Pallas kernels  170 us (19%)
  starting transfers between devices  150 us (17%)
  local copies, waits for them, and re-layouts  130 us (15%)
  matrix products  86 us (10%)
  other arithmetic  71.2 us (8%)
  between operations  18.3 us (2%)
    pallas_call x6, Pallas kernels, attention_call(): pl.pallas_call(body, out_shape=out_shapes, grid_spec=pltpu.PrefetchScalar...  170 us
    ppermute x6, waiting for transfers between devices, scatter_ring(): lax.ppermute(pick(both, lax.rem(index + steps, tensor_size), 0), 'tensor'...  46.6 us
    ppermute x3, waiting for transfers between devices, gather_tensor(): down.append(lax.ppermute(down[-1], 'tensor', line(count, -1)))  42.6 us
    ppermute x3, waiting for transfers between devices, gather_ring(): blocks.append(lax.ppermute(block, 'tensor', ring))  35 us
    ppermute x8, waiting for transfers between devices, halve(): sent = lax.ppermute(pick(value, 1 - index, axis), 'chip', neighbour)  28.6 us
    all_to_all x1, waiting for transfers between devices, local(): qkv = lax.all_to_all(qkv, layer, split_axis=0, concat_axis=0, tiled=True)  23.1 us
    ppermute x5, waiting for transfers between devices, butterfly(): lax.ppermute(value, axis, [(i, i ^ step) for i in range(count)])  22.6 us
    ppermute x3, starting transfers between devices, gather_ring(): blocks.append(lax.ppermute(block, 'tensor', ring))  20.4 us
  transfers between devices with their start and end apart: 62, of which 23 were waited for; matrix products, arithmetic and copies ran while one was open for 25% of the time, Pallas kernels for 20%

profile of v3, /device:TPU:0, one launch (start us, length us, event | category | flops | bytes accessed | tf_op | source)
XLA Modules:
  0.0 860.6 jit_solution(2451737671737225866)
XLA Ops:
  16.4 6.5 collective-permute-start
  22.9 17.1 %collective-permute-done.1 = bf16[2,192,1088]{2,1,0:T(8,128)(2,1)} collective-permute-done((bf16[2,192,1088]{2,1,0:T(8,128)(2,1)}, bf16[2,192,1088]{2,1,0:T(8,128)(2,1)}, u32[]{:S(2)}, u32[]{:S(2)}) %collective-permute-start.1) | collective-permute-done | bytes 835616 | tf_op jit(solution)/shard_map/ppermute | solution.py:31
  41.3 5.5 collective-permute-start.4
  46.8 16.2 %collective-permute-done.2 = bf16[2,192,1088]{2,1,0:T(8,128)(2,1)} collective-permute-done((bf16[2,192,1088]{2,1,0:T(8,128)(2,1)}, bf16[2,192,1088]{2,1,0:T(8,128)(2,1)}, u32[]{:S(2)}, u32[]{:S(2)}) %collective-permute-start.2) | collective-permute-done | bytes 835616 | tf_op jit(solution)/shard_map/ppermute | solution.py:31
  71.3 4.6 collective-permute-start.5
  75.9 9.3 %collective-permute-done.3 = bf16[2,192,1088]{2,1,0:T(8,128)(2,1)} collective-permute-done((bf16[2,192,1088]{2,1,0:T(8,128)(2,1)}, bf16[2,192,1088]{2,1,0:T(8,128)(2,1)}, u32[]{:S(2)}, u32[]{:S(2)}) %collective-permute-start.3) | collective-permute-done | bytes 835616 | tf_op jit(solution)/shard_map/ppermute | solution.py:31
  88.0 5.3 collective-permute-done.5
  104.9 5.0 collective-permute-start.6
  116.6 5.2 collective-permute-done.6
  126.2 3.5 fusion.21
  131.2 4.4 all-to-all-start
  144.5 3.5 collective-permute-start.13
  148.0 3.4 collective-permute-start.12
  153.4 23.1 %all-to-all-done.refs_1_ = bf16[8,192,768]{2,1,0:T(8,128)(2,1)} async-done(((bf16[8,192,768]{2,1,0:T(8,128)(2,1)}), bf16[8,192,768]{2,1,0:T(8,128)(2,1)}, u32[]{:S(2)}, u32[]{:S(2)}) %all-to-all-start) | async-done | bytes 2359328 | tf_op jit(solution)/shard_map/all_to_all | solution.py:583
  183.0 19.8 %collective-permute-start.16 = (bf16[4,128,384]{2,1,0:T(8,128)(2,1)S(1)}, bf16[4,128,384]{2,1,0:T(8,128)(2,1)S(1)}, u32[]{:S(2)}, u32[]{:S(2)}) collective-permute-start(bf16[4,128,384]{2,1,0:T(8,128)(2,1)S(1)} %pad_maximum_fusion.4.refs_8_), channel_id=1, source_target_pairs={{0,3},{1,0},{2,1},{3,2},{4,7},{5,4},{6,5},{7,6},{8,11},{9,8},{10,9... | collective-permute-start | bytes 1179656 | tf_op jit(solution)/shard_map/ppermute | solution.py:102
  203.4 29.2 %shard_map.254 = (f32[16,64,384]{2,1,0:T(8,128)}, f32[16,1,384]{2,1,0:T(1,128)}, f32[16,1,384]{2,1,0:T(1,128)}) custom-call(s32[112]{0:T(128)} %concatenate.63.refs_0_, bf16[8,192,768]{2,1,0:T(8,128)(2,1)} %all-to-all-done.refs_1_, bf16[8,128,768]{2,1,0:T(8,128)(2,1)} %copy-done.36, s32[8,2,768]{2,1,0:T(2,128)} %pad_add_fusion.refs_3_, s32[768,1]{1,0:T(8,128)} %add.943.refs_4_), custom_call_target="tpu_custom_call" | custom-call | flops 14495514624 | bytes 7864320 | tf_op jit(solution)/shard_map/pallas_call | solution.py:388
  232.7 35.0 %collective-permute-done.15.refs_10_ = bf16[4,128,384]{2,1,0:T(8,128)(2,1)S(1)} collective-permute-done((bf16[4,128,384]{2,1,0:T(8,128)(2,1)S(1)}, bf16[4,128,384]{2,1,0:T(8,128)(2,1)S(1)}, u32[]{:S(2)}, u32[]{:S(2)}) %collective-permute-start.15) | collective-permute-done | bytes 393248 | tf_op jit(solution)/shard_map/ppermute | solution.py:102
  269.2 33.1 %shard_map.255 = (f32[8,64,768]{2,1,0:T(8,128)}, bf16[32,64,192]{2,1,0:T(8,128)(2,1)}, f32[16,1,384]{2,1,0:T(1,128)}) custom-call(s32[112]{0:T(128)} %concatenate.61.refs_0_, bf16[8,192,768]{2,1,0:T(8,128)(2,1)} %all-to-all-done.refs_1_, bf16[8,128,768]{2,1,0:T(8,128)(2,1)} %copy-done.81, s32[8,2,768]{2,1,0:T(2,128)} %pad_add_fusion.refs_3_, ...), custom_call_target="tpu_custom_call" | custom-call | flops 14495514624 | bytes 7864320 | tf_op jit(solution)/shard_map/pallas_call | solution.py:388
  302.3 6.0 all-to-all-start.1
  316.4 5.7 copy.394
  322.9 14.6 %shard_map.256 = (f32[1,64,384]{2,1,0:T(8,128)}, bf16[1,64,384]{2,1,0:T(8,128)(2,1)}, f32[1,1,384]{2,1,0:T(1,128)}) custom-call(s32[82]{0:T(128)} %concatenate.66.refs_0_, bf16[1,192,384]{2,1,0:T(8,128)(2,1)} %copy-done.42, bf16[16,128,384]{2,1,0:T(8,128)(2,1)} %constant_dynamic-update-slice_fusion.refs_2_, s32[1,2,384]{2,1,0:T(2,128)} %pad_add_fusion.1.refs_3_, ...), custom_call_target="tpu_custom_call" | custom-call | flops 905969664 | bytes 3440640 | tf_op jit(solution)/shard_map/pallas_call | solution.py:388
  341.0 3.4 slice.317
  353.3 8.4 fusion.101
  361.8 7.6 fusion.68
  369.4 8.8 %convolution_convert_fusion.1 = bf16[1088,2176]{1,0:T(8,128)(2,1)S(1)} fusion(bf16[768,1088]{0,1:T(8,128)(2,1)} %constant_dynamic-update-slice_fusion.7, f32[768,2176]{1,0:T(8,128)S(1)} %fusion.68, f32[2176]{0:T(1024)S(1)} %reshape.750), kind=kOutput, calls=%fused_computation.1 | convolution fusion | flops 3655540736 | bytes 13099520 | tf_op jit(solution)/shard_map/dot_general | solution.py:659
  378.3 12.9 %convert_reduce_fusion = (f32[2176]{0:T(1024)S(1)}, bf16[768,2176]{1,0:T(8,128)(2,1)}) fusion(f32[768,2176]{1,0:T(8,128)S(1)} %fusion.68, f32[2176]{0:T(1024)S(1)} %reshape.750, bf16[768,1088]{0,1:T(8,128)(2,1)} %constant_dynamic-update-slice_fusion.7, bf16[2176,1088]{1,0:T(8,128)(2,1)S(1)} %bitcast.312), kind=kOutput, calls=%fused_computation.11 | convolution fusion | flops 3674896384 | bytes 16450560 | tf_op jit(solution)/shard_map/dot_general | solution.py:623
  391.2 6.4 fusion.109
  400.9 8.6 %convolution_convert_fusion = bf16[1088,2176]{1,0:T(8,128)(2,1)} fusion(bf16[768,2176]{1,0:T(8,128)(2,1)} %get-tuple-element.112, bf16[384,1088]{0,1:T(8,128)(2,1)} %copy-done.82, bf16[384,1088]{0,1:T(8,128)(2,1)S(1)} %add_convert_fusion.1), kind=kOutput, calls=%fused_computation | convolution fusion | flops 3642171392 | bytes 9748480 | tf_op jit(solution)/shard_map/dot_general | solution.py:662
  419.6 5.5 all-to-all-start.2
  425.1 3.3 dynamic-slice_bitcast_fusion
  433.1 3.3 bitcast_convert_fusion
  440.3 16.8 %shard_map.259 = (bf16[1,64,384]{2,1,0:T(8,128)(2,1)}, bf16[16,128,384]{2,1,0:T(8,128)(2,1)}) custom-call(s32[82]{0:T(128)} %concatenate.66.refs_0_, bf16[1,192,384]{2,1,0:T(8,128)(2,1)} %copy-done.42, bf16[16,128,384]{2,1,0:T(8,128)(2,1)} %constant_dynamic-update-slice_fusion.refs_2_, s32[1,2,384]{2,1,0:T(2,128)} %pad_add_fusion.1.refs_3_, ...), custom_call_target="tpu_custom_call" | custom-call | flops 2264924160 | bytes 3440640 | tf_op jit(solution)/shard_map/pallas_call | solution.py:388
  465.8 39.0 %shard_map.257 = (f32[16,64,384]{2,1,0:T(8,128)}, bf16[8,128,768]{2,1,0:T(8,128)(2,1)}) custom-call(s32[112]{0:T(128)} %concatenate.61.refs_0_, bf16[8,192,768]{2,1,0:T(8,128)(2,1)} %all-to-all-done.refs_1_, bf16[8,128,768]{2,1,0:T(8,128)(2,1)} %copy-done.81, s32[8,2,768]{2,1,0:T(2,128)} %pad_add_fusion.refs_3_, s32[768,1]{1,0:T(8,128)} %add.943.refs_4_, ...), custom_call_target="tpu_custom_call" | custom-call | flops 36238786560 | bytes 7864320 | tf_op jit(solution)/shard_map/pallas_call | solution.py:388
  504.8 12.0 %collective-permute-done.23 = bf16[2,272,1088]{2,1,0:T(8,128)(2,1)} collective-permute-done((bf16[2,272,1088]{2,1,0:T(8,128)(2,1)}, bf16[2,272,1088]{2,1,0:T(8,128)(2,1)}, u32[]{:S(2)}, u32[]{:S(2)}) %collective-permute-start.23) | collective-permute-done | bytes 1183776 | tf_op jit(solution)/shard_map/ppermute | solution.py:71
  516.8 3.3 collective-permute-start.30
  524.3 4.2 collective-permute-done.30
  537.6 3.3 collective-permute-start.26
  540.9 3.7 fusion.7.refs_10_
  544.5 37.5 %shard_map.258 = (bf16[8,64,768]{2,1,0:T(8,128)(2,1)}, bf16[8,128,768]{2,1,0:T(8,128)(2,1)}) custom-call(s32[112]{0:T(128)} %concatenate.63.refs_0_, bf16[8,192,768]{2,1,0:T(8,128)(2,1)} %all-to-all-done.refs_1_, bf16[8,128,768]{2,1,0:T(8,128)(2,1)} %copy-done.36, s32[8,2,768]{2,1,0:T(2,128)} %pad_add_fusion.refs_3_, s32[768,1]{1,0:T(8,128)} %add.943.refs_4_, ...), custom_call_target="tpu_custom_call" | custom-call | flops 36238786560 | bytes 7864320 | tf_op jit(solution)/shard_map/pallas_call | solution.py:388
  583.2 3.5 collective-permute-start.25
  599.8 4.3 collective-permute-start.51
  604.6 8.8 %collective-permute-done.25 = bf16[272,2176]{1,0:T(8,128)(2,1)} collective-permute-done((bf16[272,2176]{1,0:T(8,128)(2,1)}, bf16[272,2176]{1,0:T(8,128)(2,1)}, u32[]{:S(2)}, u32[]{:S(2)}) %collective-permute-start.25) | collective-permute-done | bytes 1183776 | tf_op jit(solution)/shard_map/ppermute | solution.py:71
  616.0 3.6 convert_add_fusion.2
  621.2 4.4 all-to-all-start.3
  631.4 3.2 stack.51
  638.2 3.9 collective-permute-start.29
  647.5 7.5 collective-permute-done.37
  658.7 12.5 %collective-permute-done.29 = bf16[2,272,544]{2,1,0:T(8,128)(2,1)} collective-permute-done((bf16[2,272,544]{2,1,0:T(8,128)(2,1)}, bf16[2,272,544]{2,1,0:T(8,128)(2,1)}, u32[]{:S(2)}, u32[]{:S(2)}) %collective-permute-start.29) | collective-permute-done | bytes 591904 | tf_op jit(solution)/shard_map/ppermute | solution.py:92
  671.3 31.9 %collective-permute-done.28 = bf16[2,272,544]{2,1,0:T(8,128)(2,1)} collective-permute-done((bf16[2,272,544]{2,1,0:T(8,128)(2,1)}, bf16[2,272,544]{2,1,0:T(8,128)(2,1)}, u32[]{:S(2)}, u32[]{:S(2)}) %collective-permute-start.28) | collective-permute-done | bytes 591904 | tf_op jit(solution)/shard_map/ppermute | solution.py:92
  707.3 4.0 fusion.12
  711.3 3.8 copy.389
  715.1 4.4 all-to-all-start.5
  727.3 10.2 %fusion.95 = f32[768,1088]{0,1:T(8,128)S(1)} fusion(bf16[2176,1088]{1,0:T(8,128)(2,1)} %bitcast.309, f32[768,2176]{1,0:T(8,128)} %copy-done.84, f32[2176]{0:T(1024)S(1)} %reshape.750), kind=kOutput, calls=%fused_computation.267 | convolution fusion | flops 3653173248 | bytes 14770688 | tf_op jit(solution)/shard_map/dot_general | solution.py:634
  742.6 7.0 collective-permute-done.39
  749.6 4.7 collective-permute-start.40
  755.0 8.1 collective-permute-done.40
  775.7 3.6 all-to-all-start.4
  786.4 5.2 collective-permute-done.43
  796.0 4.2 collective-permute-start.44
  808.6 10.7 %collective-permute-done.47 = bf16[3,48,136]{1,2,0:T(8,128)(2,1)S(1)} collective-permute-done((bf16[3,48,136]{1,2,0:T(8,128)(2,1)S(1)}, bf16[3,48,136]{1,2,0:T(8,128)(2,1)S(1)}, u32[]{:S(2)}, u32[]{:S(2)}) %collective-permute-start.47) | collective-permute-done | bytes 39200 | tf_op jit(solution)/shard_map/ppermute | solution.py:470
  828.6 3.6 fusion.41
  833.0 8.0 all-to-all-start.6
  841.2 5.3 fusion.40
  846.5 5.2 all-to-all-done.6
  (517 shorter events, 226.5 us)
Async XLA Ops:
  7.2 332.9 %all-gather.2.cloned.1.call-start = ((), (), s32[]{:S(2)}) async-start(), calls=%async_computation.7 | async-start | bytes 13473792 | tf_op jit(solution)/shard_map/all_gather | solution.py:550
  15.1 24.9 %collective-permute-start.1 = (bf16[2,192,1088]{2,1,0:T(8,128)(2,1)}, bf16[2,192,1088]{2,1,0:T(8,128)(2,1)}, u32[]{:S(2)}, u32[]{:S(2)}) collective-permute-start(bf16[2,192,1088]{2,1,0:T(8,128)(2,1)} %bitcast.328), channel_id=1, source_target_pairs={{1,0},{2,1},{3,2},{5,4},{6,5},{7,6},{9,8},{10,9},{11,10},{13,12},{... | collective-permute-start | bytes 2506760 | tf_op jit(solution)/shard_map/ppermute | solution.py:31
  16.4 24.9 %collective-permute-start = (bf16[2,192,1088]{2,1,0:T(8,128)(2,1)}, bf16[2,192,1088]{2,1,0:T(8,128)(2,1)}, u32[]{:S(2)}, u32[]{:S(2)}) collective-permute-start(bf16[2,192,1088]{2,1,0:T(8,128)(2,1)} %bitcast.329), channel_id=1, source_target_pairs={{0,1},{1,2},{2,3},{4,5},{5,6},{6,7},{8,9},{9,10},{10,11},{12,13},{... | collective-permute-start | bytes 2506760 | tf_op jit(solution)/shard_map/ppermute | solution.py:30
  40.0 23.0 %collective-permute-start.2 = (bf16[2,192,1088]{2,1,0:T(8,128)(2,1)}, bf16[2,192,1088]{2,1,0:T(8,128)(2,1)}, u32[]{:S(2)}, u32[]{:S(2)}) collective-permute-start(bf16[2,192,1088]{2,1,0:T(8,128)(2,1)} %collective-permute-done.1), channel_id=1, source_target_pairs={{1,0},{2,1},{3,2},{5,4},{6,5},{7,6},{9,8},{10,9},{11,10},{13,12},{... | collective-permute-start | bytes 2506760 | tf_op jit(solution)/shard_map/ppermute | solution.py:31
  41.3 29.9 %collective-permute-start.4 = (bf16[2,192,1088]{2,1,0:T(8,128)(2,1)}, bf16[2,192,1088]{2,1,0:T(8,128)(2,1)}, u32[]{:S(2)}, u32[]{:S(2)}) collective-permute-start(bf16[2,192,1088]{2,1,0:T(8,128)(2,1)} %collective-permute-done), channel_id=1, source_target_pairs={{0,1},{1,2},{2,3},{4,5},{5,6},{6,7},{8,9},{9,10},{10,11},{12,13},{... | collective-permute-start | bytes 2506760 | tf_op jit(solution)/shard_map/ppermute | solution.py:30
  63.0 22.1 %collective-permute-start.3 = (bf16[2,192,1088]{2,1,0:T(8,128)(2,1)}, bf16[2,192,1088]{2,1,0:T(8,128)(2,1)}, u32[]{:S(2)}, u32[]{:S(2)}) collective-permute-start(bf16[2,192,1088]{2,1,0:T(8,128)(2,1)} %collective-permute-done.2), channel_id=1, source_target_pairs={{1,0},{2,1},{3,2},{5,4},{6,5},{7,6},{9,8},{10,9},{11,10},{13,12},{... | collective-permute-start | bytes 2506760 | tf_op jit(solution)/shard_map/ppermute | solution.py:31
  71.3 22.0 %collective-permute-start.5 = (bf16[2,192,1088]{2,1,0:T(8,128)(2,1)}, bf16[2,192,1088]{2,1,0:T(8,128)(2,1)S(1)}, u32[]{:S(2)}, u32[]{:S(2)}) collective-permute-start(bf16[2,192,1088]{2,1,0:T(8,128)(2,1)} %collective-permute-done.4), channel_id=1, source_target_pairs={{0,1},{1,2},{2,3},{4,5},{5,6},{6,7},{8,9},{9,10},{10,11},{12,13},{... | collective-permute-start | bytes 2506760 | tf_op jit(solution)/shard_map/ppermute | solution.py:30
  100.4 40.6 %collective-permute-start.9 = (bf16[3,64,1088]{2,1,0:T(8,128)(2,1)}, bf16[3,64,1088]{2,1,0:T(8,128)(2,1)S(1)}, u32[]{:S(2)}, u32[]{:S(2)}) collective-permute-start(bf16[3,64,1088]{2,1,0:T(8,128)(2,1)} %slice.259), channel_id=1, source_target_pairs={{3,1},{7,5},{11,9},{15,13},{19,17},{23,21},{27,25},{31,29}} | collective-permute-start | bytes 1253384 | tf_op jit(solution)/shard_map/ppermute | solution.py:463
  101.1 40.7 %collective-permute-start.8 = (bf16[3,64,1088]{2,1,0:T(8,128)(2,1)}, bf16[3,64,1088]{2,1,0:T(8,128)(2,1)}, u32[]{:S(2)}, u32[]{:S(2)}) collective-permute-start(bf16[3,64,1088]{2,1,0:T(8,128)(2,1)} %slice.259), channel_id=1, source_target_pairs={{3,0},{7,4},{11,8},{15,12},{19,16},{23,20},{27,24},{31,28}} | collective-permute-start | bytes 1253384 | tf_op jit(solution)/shard_map/ppermute | solution.py:463
  102.4 39.4 %collective-permute-start.10 = (bf16[3,64,1088]{2,1,0:T(8,128)(2,1)}, bf16[3,64,1088]{2,1,0:T(8,128)(2,1)}, u32[]{:S(2)}, u32[]{:S(2)}) collective-permute-start(bf16[3,64,1088]{2,1,0:T(8,128)(2,1)} %slice.259), channel_id=1, source_target_pairs={{3,2},{7,6},{11,10},{15,14},{19,18},{23,22},{27,26},{31,30}} | collective-permute-start | bytes 1253384 | tf_op jit(solution)/shard_map/ppermute | solution.py:463
  104.9 16.9 %collective-permute-start.6 = (bf16[3,48,1088]{2,1,0:T(8,128)(2,1)S(1)}, bf16[3,48,1088]{2,1,0:T(8,128)(2,1)S(1)}, u32[]{:S(2)}, u32[]{:S(2)}) collective-permute-start(bf16[3,48,1088]{2,1,0:T(8,128)(2,1)S(1)} %slice.254), channel_id=1, source_target_pairs={{0,1},{1,2},{2,3},{4,5},{5,6},{6,7},{8,9},{9,10},{10,11},{12,13},{... | collective-permute-start | bytes 940040 | tf_op jit(solution)/shard_map/ppermute | solution.py:453
  109.9 202.0 %collective-permute-start.19 = (bf16[384,1088]{0,1:T(8,128)(2,1)S(1)}, bf16[384,1088]{0,1:T(8,128)(2,1)}, u32[]{:S(2)}, u32[]{:S(2)}) collective-permute-start(bf16[384,1088]{0,1:T(8,128)(2,1)S(1)} %copy-done.14), channel_id=1, source_target_pairs={{0,4},{4,0},{1,5},{5,1},{2,6},{6,2},{3,7},{7,3},{8,12},{12,8},{9,1... | collective-permute-start | bytes 2506760 | tf_op jit(solution)/shard_map/ppermute | solution.py:52
  114.4 297.4 %copy-start.56 = (f32[1088]{0:T(1024)}, f32[1088]{0:T(1024)S(1)}, u32[]{:S(2)}) copy-start(f32[1088]{0:T(1024)S(1)} %convert_element_type.389) | copy-start | bytes 13060
  131.2 45.3 %all-to-all-start = ((bf16[8,192,768]{2,1,0:T(8,128)(2,1)}), bf16[8,192,768]{2,1,0:T(8,128)(2,1)}, u32[]{:S(2)}, u32[]{:S(2)}) async-start(bf16[8,192,768]{2,1,0:T(8,128)(2,1)} %bitcast.22), calls=%async_computation | async-start | bytes 4718592 | tf_op jit(solution)/shard_map/all_to_all | solution.py:583
  144.5 34.5 %collective-permute-start.13 = (bf16[1,128,384]{2,1,0:T(8,128)(2,1)S(1)}, bf16[1,128,384]{2,1,0:T(8,128)(2,1)S(1)}, u32[]{:S(2)}, u32[]{:S(2)}) collective-permute-start(bf16[1,128,384]{2,1,0:T(8,128)(2,1)S(1)} %get-tuple-element.144), channel_id=1, source_target_pairs={{0,12},{4,16},{8,20},{12,24},{16,28},{1,13},{5,17},{9,21},{13,25},... | collective-permute-start | bytes 294920 | tf_op jit(solution)/shard_map/ppermute | solution.py:589
  148.0 33.6 %collective-permute-start.12 = (bf16[1,128,384]{2,1,0:T(8,128)(2,1)S(1)}, bf16[1,128,384]{2,1,0:T(8,128)(2,1)S(1)}, u32[]{:S(2)}, u32[]{:S(2)}) collective-permute-start(bf16[1,128,384]{2,1,0:T(8,128)(2,1)S(1)} %get-tuple-element.144), channel_id=1, source_target_pairs={{0,8},{4,12},{8,16},{12,20},{16,24},{20,28},{1,9},{5,13},{9,17},{1... | collective-permute-start | bytes 294920 | tf_op jit(solution)/shard_map/ppermute | solution.py:589
  151.4 30.2 %collective-permute-start.11 = (bf16[1,128,384]{2,1,0:T(8,128)(2,1)S(1)}, bf16[1,128,384]{2,1,0:T(8,128)(2,1)S(1)}, u32[]{:S(2)}, u32[]{:S(2)}) collective-permute-start(bf16[1,128,384]{2,1,0:T(8,128)(2,1)S(1)} %get-tuple-element.144), channel_id=1, source_target_pairs={{0,4},{4,8},{8,12},{12,16},{16,20},{20,24},{24,28},{1,5},{5,9},{9,... | collective-permute-start | bytes 294920 | tf_op jit(solution)/shard_map/ppermute | solution.py:589
  178.1 54.6 %collective-permute-start.7 = (bf16[8,128,768]{2,1,0:T(8,128)(2,1)S(1)}, bf16[8,128,768]{2,1,0:T(8,128)(2,1)S(1)}, u32[]{:S(2)}, u32[]{:S(2)}) collective-permute-start(bf16[8,128,768]{2,1,0:T(8,128)(2,1)S(1)} %slice.313.refs_2_), channel_id=1, source_target_pairs={{0,4},{4,0},{1,5},{5,1},{2,6},{6,2},{3,7},{7,3},{8,12},{12,8},{9,1... | collective-permute-start | bytes 4718600 | tf_op jit(solution)/shard_map/ppermute | solution.py:52
  183.0 49.7 %collective-permute-start.16 = (bf16[4,128,384]{2,1,0:T(8,128)(2,1)S(1)}, bf16[4,128,384]{2,1,0:T(8,128)(2,1)S(1)}, u32[]{:S(2)}, u32[]{:S(2)}) collective-permute-start(bf16[4,128,384]{2,1,0:T(8,128)(2,1)S(1)} %pad_maximum_fusion.4.refs_8_), channel_id=1, source_target_pairs={{0,3},{1,0},{2,1},{3,2},{4,7},{5,4},{6,5},{7,6},{8,11},{9,8},{10,9... | collective-permute-start | bytes 1179656 | tf_op jit(solution)/shard_map/ppermute | solution.py:102
  202.7 64.9 %collective-permute-start.15 = (bf16[4,128,384]{2,1,0:T(8,128)(2,1)S(1)}, bf16[4,128,384]{2,1,0:T(8,128)(2,1)S(1)}, u32[]{:S(2)}, u32[]{:S(2)}) collective-permute-start(bf16[4,128,384]{2,1,0:T(8,128)(2,1)S(1)} %pad_maximum_fusion.4.refs_8_), channel_id=1, source_target_pairs={{0,2},{1,3},{2,0},{3,1},{4,6},{5,7},{6,4},{7,5},{8,10},{9,11},{10,... | collective-permute-start | bytes 1179656 | tf_op jit(solution)/shard_map/ppermute | solution.py:102
  202.8 64.9 %collective-permute-start.14 = (bf16[4,128,384]{2,1,0:T(8,128)(2,1)S(1)}, bf16[4,128,384]{2,1,0:T(8,128)(2,1)S(1)}, u32[]{:S(2)}, u32[]{:S(2)}) collective-permute-start(bf16[4,128,384]{2,1,0:T(8,128)(2,1)S(1)} %pad_maximum_fusion.4.refs_8_), channel_id=1, source_target_pairs={{0,1},{1,2},{2,3},{3,0},{4,5},{5,6},{6,7},{7,4},{8,9},{9,10},{10,1... | collective-permute-start | bytes 1179656 | tf_op jit(solution)/shard_map/ppermute | solution.py:102
  302.3 35.2 %all-to-all-start.1 = ((bf16[32,64,192]{2,1,0:T(8,128)(2,1)}), bf16[32,64,192]{2,1,0:T(8,128)(2,1)}, u32[]{:S(2)}, u32[]{:S(2)}) async-start(bf16[32,64,192]{2,1,0:T(8,128)(2,1)} %get-tuple-element.60), calls=%async_computation.1 | async-start | bytes 2097152 | tf_op jit(solution)/shard_map/all_to_all | solution.py:598
  352.3 59.5 %copy-start.2 = (f32[384,1088]{0,1:T(8,128)}, f32[384,1088]{0,1:T(8,128)S(1)}, u32[]{:S(2)}) copy-start(f32[384,1088]{0,1:T(8,128)S(1)} %get-tuple-element.164) | copy-start | bytes 5013508
  352.9 8.8 %collective-permute-start.17 = (bf16[384,1088]{0,1:T(8,128)(2,1)S(1)}, bf16[384,1088]{0,1:T(8,128)(2,1)S(1)}, u32[]{:S(2)}, u32[]{:S(2)}) collective-permute-start(bf16[384,1088]{0,1:T(8,128)(2,1)S(1)} %add_convert_fusion.1), channel_id=1, source_target_pairs={{0,4},{4,0},{1,5},{5,1},{2,6},{6,2},{3,7},{7,3},{8,12},{12,8},{9,1... | collective-permute-start | bytes 2506760 | tf_op jit(solution)/shard_map/ppermute | solution.py:52
  397.7 11.8 %collective-permute-start.20 = (bf16[384,1088]{0,1:T(8,128)(2,1)S(1)}, bf16[384,1088]{0,1:T(8,128)(2,1)}, u32[]{:S(2)}, u32[]{:S(2)}) collective-permute-start(bf16[384,1088]{0,1:T(8,128)(2,1)S(1)} %slice.411), channel_id=1, source_target_pairs={{0,4},{4,0},{1,5},{5,1},{2,6},{6,2},{3,7},{7,3},{8,12},{12,8},{9,1... | collective-permute-start | bytes 2506760 | tf_op jit(solution)/shard_map/ppermute | solution.py:52
  400.7 131.9 %collective-permute-start.21 = (bf16[2,272,2176]{2,1,0:T(8,128)(2,1)}, bf16[2,272,2176]{2,1,0:T(8,128)(2,1)}, u32[]{:S(2)}, u32[]{:S(2)}) collective-permute-start(bf16[2,272,2176]{2,1,0:T(8,128)(2,1)} %dynamic-slice_bitcast_fusion.1), channel_id=1, source_target_pairs={{0,16},{8,24},{16,0},{24,8},{1,17},{9,25},{17,1},{25,9},{2,18},{10... | collective-permute-start | bytes 7102472 | tf_op jit(solution)/shard_map/ppermute | solution.py:71
  419.6 46.3 %all-to-all-start.2 = ((bf16[32,64,192]{2,1,0:T(8,128)(2,1)}), bf16[32,64,192]{2,1,0:T(8,128)(2,1)}, u32[]{:S(2)}, u32[]{:S(2)}) async-start(bf16[32,64,192]{2,1,0:T(8,128)(2,1)} %bitcast.48), calls=%async_computation.2 | async-start | bytes 2097152 | tf_op jit(solution)/shard_map/all_to_all | solution.py:650
  428.4 109.1 %collective-permute-start.22 = (bf16[2,272,2176]{2,1,0:T(8,128)(2,1)}, bf16[2,272,2176]{2,1,0:T(8,128)(2,1)}, u32[]{:S(2)}, u32[]{:S(2)}) collective-permute-start(bf16[2,272,2176]{2,1,0:T(8,128)(2,1)} %dynamic-slice_bitcast_fusion), channel_id=1, source_target_pairs={{0,8},{8,0},{16,24},{24,16},{1,9},{9,1},{17,25},{25,17},{2,10},{10... | collective-permute-start | bytes 7102472 | tf_op jit(solution)/shard_map/ppermute | solution.py:71
  437.7 79.1 %collective-permute-start.23 = (bf16[2,272,1088]{2,1,0:T(8,128)(2,1)}, bf16[2,272,1088]{2,1,0:T(8,128)(2,1)}, u32[]{:S(2)}, u32[]{:S(2)}) collective-permute-start(bf16[2,272,1088]{2,1,0:T(8,128)(2,1)} %fusion.55), channel_id=1, source_target_pairs={{0,8},{8,0},{16,24},{24,16},{1,9},{9,1},{17,25},{25,17},{2,10},{10... | collective-permute-start | bytes 3551240 | tf_op jit(solution)/shard_map/ppermute | solution.py:71
  459.6 63.2 %collective-permute-start.32 = (bf16[4,128,384]{2,1,0:T(8,128)(2,1)}, bf16[4,128,384]{2,1,0:T(8,128)(2,1)}, u32[]{:S(2)}, u32[]{:S(2)}) collective-permute-start(bf16[4,128,384]{2,1,0:T(8,128)(2,1)} %get-tuple-element.127), channel_id=1, source_target_pairs={{0,1},{1,2},{2,3},{3,0},{4,5},{5,6},{6,7},{7,4},{8,9},{9,10},{10,1... | collective-permute-start | bytes 1179656 | tf_op jit(solution)/shard_map/ppermute | solution.py:681
  461.5 62.8 %collective-permute-start.31 = (bf16[4,128,384]{2,1,0:T(8,128)(2,1)}, bf16[4,128,384]{2,1,0:T(8,128)(2,1)}, u32[]{:S(2)}, u32[]{:S(2)}) collective-permute-start(bf16[4,128,384]{2,1,0:T(8,128)(2,1)} %get-tuple-element.128), channel_id=1, source_target_pairs={{0,2},{1,3},{2,0},{3,1},{4,6},{5,7},{6,4},{7,5},{8,10},{9,11},{10,... | collective-permute-start | bytes 1179656 | tf_op jit(solution)/shard_map/ppermute | solution.py:681
  516.8 11.7 %collective-permute-start.30 = (bf16[4,128,384]{2,1,0:T(8,128)(2,1)S(1)}, bf16[4,128,384]{2,1,0:T(8,128)(2,1)S(1)}, u32[]{:S(2)}, u32[]{:S(2)}) collective-permute-start(bf16[4,128,384]{2,1,0:T(8,128)(2,1)S(1)} %get-tuple-element.129), channel_id=1, source_target_pairs={{0,3},{1,0},{2,1},{3,2},{4,7},{5,4},{6,5},{7,6},{8,11},{9,8},{10,9... | collective-permute-start | bytes 1179656 | tf_op jit(solution)/shard_map/ppermute | solution.py:681
  522.8 67.9 %collective-permute-start.48 = (bf16[272,1088]{1,0:T(8,128)(2,1)}, bf16[272,1088]{1,0:T(8,128)(2,1)}, u32[]{:S(2)}, u32[]{:S(2)}) collective-permute-start(bf16[272,1088]{1,0:T(8,128)(2,1)} %dynamic-slice_bitcast_fusion.7), channel_id=1, source_target_pairs={{0,16},{8,24},{16,0},{24,8},{1,17},{9,25},{17,1},{25,9},{2,18},{10... | collective-permute-start | bytes 1775624 | tf_op jit(solution)/shard_map/ppermute | solution.py:71
  530.0 53.2 %collective-permute-start.35 = (bf16[128,384]{1,0:T(8,128)(2,1)S(1)}, bf16[128,384]{1,0:T(8,128)(2,1)S(1)}, u32[]{:S(2)}, u32[]{:S(2)}) collective-permute-start(bf16[128,384]{1,0:T(8,128)(2,1)S(1)} %get-tuple-element.140), channel_id=1, source_target_pairs={{12,0},{16,4},{20,8},{24,12},{28,16},{13,1},{17,5},{21,9},{25,13},... | collective-permute-start | bytes 294920 | tf_op jit(solution)/shard_map/ppermute | solution.py:689
  531.3 55.7 %collective-permute-start.34 = (bf16[128,384]{1,0:T(8,128)(2,1)S(1)}, bf16[128,384]{1,0:T(8,128)(2,1)S(1)}, u32[]{:S(2)}, u32[]{:S(2)}) collective-permute-start(bf16[128,384]{1,0:T(8,128)(2,1)S(1)} %get-tuple-element.141), channel_id=1, source_target_pairs={{8,0},{12,4},{16,8},{20,12},{24,16},{28,20},{9,1},{13,5},{17,9},{2... | collective-permute-start | bytes 294920 | tf_op jit(solution)/shard_map/ppermute | solution.py:689
  532.6 54.4 %collective-permute-start.33 = (bf16[128,384]{1,0:T(8,128)(2,1)S(1)}, bf16[128,384]{1,0:T(8,128)(2,1)S(1)}, u32[]{:S(2)}, u32[]{:S(2)}) collective-permute-start(bf16[128,384]{1,0:T(8,128)(2,1)S(1)} %get-tuple-element.142), channel_id=1, source_target_pairs={{4,0},{8,4},{12,8},{16,12},{20,16},{24,20},{28,24},{5,1},{9,5},{13... | collective-permute-start | bytes 294920 | tf_op jit(solution)/shard_map/ppermute | solution.py:689
  537.6 66.5 %collective-permute-start.26 = (bf16[272,2176]{1,0:T(8,128)(2,1)}, bf16[272,2176]{1,0:T(8,128)(2,1)}, u32[]{:S(2)}, u32[]{:S(2)}) collective-permute-start(bf16[272,2176]{1,0:T(8,128)(2,1)} %dynamic-slice_bitcast_fusion.2), channel_id=1, source_target_pairs={{0,8},{8,0},{16,24},{24,16},{1,9},{9,1},{17,25},{25,17},{2,10},{10... | collective-permute-start | bytes 3551240 | tf_op jit(solution)/shard_map/ppermute | solution.py:71
  583.2 30.2 %collective-permute-start.25 = (bf16[272,2176]{1,0:T(8,128)(2,1)}, bf16[272,2176]{1,0:T(8,128)(2,1)}, u32[]{:S(2)}, u32[]{:S(2)}) collective-permute-start(bf16[272,2176]{1,0:T(8,128)(2,1)} %dynamic-slice_bitcast_fusion.3), channel_id=1, source_target_pairs={{0,16},{8,24},{16,0},{24,8},{1,17},{9,25},{17,1},{25,9},{2,18},{10... | collective-permute-start | bytes 3551240 | tf_op jit(solution)/shard_map/ppermute | solution.py:71
  587.0 29.0 %collective-permute-start.24 = (bf16[8,128,768]{2,1,0:T(8,128)(2,1)}, bf16[8,128,768]{2,1,0:T(8,128)(2,1)}, u32[]{:S(2)}, u32[]{:S(2)}) collective-permute-start(bf16[8,128,768]{2,1,0:T(8,128)(2,1)} %get-tuple-element.71), channel_id=1, source_target_pairs={{0,4},{4,0},{1,5},{5,1},{2,6},{6,2},{3,7},{7,3},{8,12},{12,8},{9,1... | collective-permute-start | bytes 4718600 | tf_op jit(solution)/shard_map/ppermute | solution.py:52
  599.8 42.3 %collective-permute-start.51 = (bf16[272,272]{1,0:T(8,128)(2,1)}, bf16[272,272]{1,0:T(8,128)(2,1)}, u32[]{:S(2)}, u32[]{:S(2)}) collective-permute-start(bf16[272,272]{1,0:T(8,128)(2,1)} %bitcast.294), channel_id=1, source_target_pairs={{0,3},{1,0},{2,1},{3,2},{4,7},{5,4},{6,5},{7,6},{8,11},{9,8},{10,9... | collective-permute-start | bytes 443912 | tf_op jit(solution)/shard_map/ppermute | solution.py:92
  604.1 39.1 %collective-permute-start.49 = (bf16[272,272]{1,0:T(8,128)(2,1)}, bf16[272,272]{1,0:T(8,128)(2,1)}, u32[]{:S(2)}, u32[]{:S(2)}) collective-permute-start(bf16[272,272]{1,0:T(8,128)(2,1)} %bitcast.296), channel_id=1, source_target_pairs={{0,1},{1,2},{2,3},{3,0},{4,5},{5,6},{6,7},{7,4},{8,9},{9,10},{10,1... | collective-permute-start | bytes 443912 | tf_op jit(solution)/shard_map/ppermute | solution.py:92
  604.1 39.2 %collective-permute-start.50 = (bf16[272,272]{1,0:T(8,128)(2,1)}, bf16[272,272]{1,0:T(8,128)(2,1)}, u32[]{:S(2)}, u32[]{:S(2)}) collective-permute-start(bf16[272,272]{1,0:T(8,128)(2,1)} %bitcast.295), channel_id=1, source_target_pairs={{0,2},{1,3},{2,0},{3,1},{4,6},{5,7},{6,4},{7,5},{8,10},{9,11},{10,... | collective-permute-start | bytes 443912 | tf_op jit(solution)/shard_map/ppermute | solution.py:92
  621.2 86.1 %all-to-all-start.3 = ((bf16[8,192,768]{2,1,0:T(8,128)(2,1)}), bf16[8,192,768]{2,1,0:T(8,128)(2,1)}, u32[]{:S(2)}, u32[]{:S(2)}) async-start(bf16[8,192,768]{2,1,0:T(8,128)(2,1)} %pad_maximum_fusion), calls=%async_computation.3 | async-start | bytes 4718592 | tf_op jit(solution)/shard_map/all_to_all | solution.py:720
  637.6 21.1 %collective-permute-start.27 = (bf16[2,272,544]{2,1,0:T(8,128)(2,1)}, bf16[2,272,544]{2,1,0:T(8,128)(2,1)}, u32[]{:S(2)}, u32[]{:S(2)}) collective-permute-start(bf16[2,272,544]{2,1,0:T(8,128)(2,1)} %get-tuple-element.122), channel_id=1, source_target_pairs={{0,1},{1,2},{2,3},{3,0},{4,5},{5,6},{6,7},{7,4},{8,9},{9,10},{10,1... | collective-permute-start | bytes 1775624 | tf_op jit(solution)/shard_map/ppermute | solution.py:92
  638.2 33.0 %collective-permute-start.29 = (bf16[2,272,544]{2,1,0:T(8,128)(2,1)}, bf16[2,272,544]{2,1,0:T(8,128)(2,1)}, u32[]{:S(2)}, u32[]{:S(2)}) collective-permute-start(bf16[2,272,544]{2,1,0:T(8,128)(2,1)} %get-tuple-element.123), channel_id=1, source_target_pairs={{0,3},{1,0},{2,1},{3,2},{4,7},{5,4},{6,5},{7,6},{8,11},{9,8},{10,9... | collective-permute-start | bytes 1775624 | tf_op jit(solution)/shard_map/ppermute | solution.py:92
  642.1 61.0 %collective-permute-start.28 = (bf16[2,272,544]{2,1,0:T(8,128)(2,1)}, bf16[2,272,544]{2,1,0:T(8,128)(2,1)}, u32[]{:S(2)}, u32[]{:S(2)}) collective-permute-start(bf16[2,272,544]{2,1,0:T(8,128)(2,1)} %get-tuple-element.124), channel_id=1, source_target_pairs={{0,2},{1,3},{2,0},{3,1},{4,6},{5,7},{6,4},{7,5},{8,10},{9,11},{10,... | collective-permute-start | bytes 1775624 | tf_op jit(solution)/shard_map/ppermute | solution.py:92
  643.2 1.5 collective-permute-start.36
  644.7 10.3 %collective-permute-start.37 = (f32[10880]{0:T(1024)S(1)}, f32[10880]{0:T(1024)S(1)}, u32[]{:S(2)}, u32[]{:S(2)}) collective-permute-start(f32[10880]{0:T(1024)S(1)} %add.920), channel_id=1, source_target_pairs={{0,8},{8,0},{16,24},{24,16},{1,9},{9,1},{17,25},{25,17},{2,10},{10... | collective-permute-start | bytes 130568 | tf_op jit(solution)/shard_map/ppermute | solution.py:111
  647.3 93.7 %collective-permute-start.52 = (bf16[136,272]{1,0:T(8,128)(2,1)}, bf16[136,272]{1,0:T(8,128)(2,1)}, u32[]{:S(2)}, u32[]{:S(2)}) collective-permute-start(bf16[136,272]{1,0:T(8,128)(2,1)} %fusion.81), channel_id=1, source_target_pairs={{0,4},{4,0},{1,5},{5,1},{2,6},{6,2},{3,7},{7,3},{8,12},{12,8},{9,1... | collective-permute-start | bytes 221960 | tf_op jit(solution)/shard_map/ppermute | solution.py:52
  655.0 83.9 %collective-permute-start.38 = (f32[10880]{0:T(1024)S(1)}, f32[10880]{0:T(1024)S(1)}, u32[]{:S(2)}, u32[]{:S(2)}) collective-permute-start(f32[10880]{0:T(1024)S(1)} %add.921), channel_id=1, source_target_pairs={{0,16},{8,24},{16,0},{24,8},{1,17},{9,25},{17,1},{25,9},{2,18},{10... | collective-permute-start | bytes 130568 | tf_op jit(solution)/shard_map/ppermute | solution.py:111
  715.1 60.6 %all-to-all-start.5 = ((bf16[4,192,1088]{2,1,0:T(8,128)(2,1)}), bf16[4,192,1088]{2,1,0:T(8,128)(2,1)}, u32[]{:S(2)}, u32[]{:S(2)}) async-start(bf16[4,192,1088]{2,1,0:T(8,128)(2,1)} %bitcast.80), calls=%async_computation.5 | async-start | bytes 3538944 | tf_op jit(solution)/shard_map/all_to_all | solution.py:43
  727.3 39.2 %collective-permute-start.41 = (bf16[2,2,136,960]{3,2,1,0:T(8,128)(2,1)}, bf16[2,2,136,960]{3,2,1,0:T(8,128)(2,1)}, u32[]{:S(2)}, u32[]{:S(2)}) collective-permute-start(bf16[2,2,136,960]{3,2,1,0:T(8,128)(2,1)} %fusion.64), channel_id=1, source_target_pairs={{0,4},{4,0},{1,5},{5,1},{2,6},{6,2},{3,7},{7,3},{8,12},{12,8},{9,1... | collective-permute-start | bytes 3133448 | tf_op jit(solution)/shard_map/ppermute | solution.py:52
  738.5 102.6 %collective-permute-start.18 = (bf16[384,1088]{0,1:T(8,128)(2,1)}, bf16[384,1088]{0,1:T(8,128)(2,1)}, u32[]{:S(2)}, u32[]{:S(2)}) collective-permute-start(bf16[384,1088]{0,1:T(8,128)(2,1)} %slice.412), channel_id=1, source_target_pairs={{0,4},{4,0},{1,5},{5,1},{2,6},{6,2},{3,7},{7,3},{8,12},{12,8},{9,1... | collective-permute-start | bytes 2506760 | tf_op jit(solution)/shard_map/ppermute | solution.py:52
  739.0 10.6 %collective-permute-start.39 = (f32[10880]{0:T(1024)S(1)}, f32[10880]{0:T(1024)S(1)}, u32[]{:S(2)}, u32[]{:S(2)}) collective-permute-start(f32[10880]{0:T(1024)S(1)} %add.922), channel_id=1, source_target_pairs={{0,1},{1,0},{2,3},{3,2},{4,5},{5,4},{6,7},{7,6},{8,9},{9,8},{10,11... | collective-permute-start | bytes 130568 | tf_op jit(solution)/shard_map/ppermute | solution.py:111
  749.6 13.5 %collective-permute-start.40 = (f32[10880]{0:T(1024)S(1)}, f32[10880]{0:T(1024)S(1)}, u32[]{:S(2)}, u32[]{:S(2)}) collective-permute-start(f32[10880]{0:T(1024)S(1)} %add.923), channel_id=1, source_target_pairs={{0,2},{1,3},{2,0},{3,1},{4,6},{5,7},{6,4},{7,5},{8,10},{9,11},{10,... | collective-permute-start | bytes 130568 | tf_op jit(solution)/shard_map/ppermute | solution.py:111
  755.0 24.3 %collective-permute-start.53 = (bf16[2,136,544]{2,1,0:T(8,128)(2,1)}, bf16[2,136,544]{2,1,0:T(8,128)(2,1)}, u32[]{:S(2)}, u32[]{:S(2)}) collective-permute-start(bf16[2,136,544]{2,1,0:T(8,128)(2,1)} %dynamic-slice_bitcast_fusion.9), channel_id=1, source_target_pairs={{0,4},{4,0},{1,5},{5,1},{2,6},{6,2},{3,7},{7,3},{8,12},{12,8},{9,1... | collective-permute-start | bytes 887816 | tf_op jit(solution)/shard_map/ppermute | solution.py:52
  769.0 14.2 %collective-permute-start.42 = (bf16[2,136,960]{2,1,0:T(8,128)(2,1)}, bf16[2,136,960]{2,1,0:T(8,128)(2,1)}, u32[]{:S(2)}, u32[]{:S(2)}) collective-permute-start(bf16[2,136,960]{2,1,0:T(8,128)(2,1)} %dynamic-slice_bitcast_fusion.8), channel_id=1, source_target_pairs={{0,8},{8,0},{16,24},{24,16},{1,9},{9,1},{17,25},{25,17},{2,10},{10... | collective-permute-start | bytes 1566728 | tf_op jit(solution)/shard_map/ppermute | solution.py:71
  775.7 49.0 %all-to-all-start.4 = ((bf16[4,192,1088]{2,1,0:T(8,128)(2,1)}), bf16[4,192,1088]{2,1,0:T(8,128)(2,1)S(1)}, u32[]{:S(2)}, u32[]{:S(2)}) async-start(bf16[4,192,1088]{2,1,0:T(8,128)(2,1)} %bitcast.77), calls=%async_computation.4 | async-start | bytes 3538944 | tf_op jit(solution)/shard_map/all_to_all | solution.py:43
  784.5 7.1 collective-permute-start.43
  793.4 25.9 %collective-permute-start.46 = (bf16[3,64,136]{1,2,0:T(8,128)(2,1)S(1)}, bf16[3,64,136]{1,2,0:T(8,128)(2,1)}, u32[]{:S(2)}, u32[]{:S(2)}) collective-permute-start(bf16[3,64,136]{1,2,0:T(8,128)(2,1)S(1)} %copy.400), channel_id=1, source_target_pairs={{2,3},{6,7},{10,11},{14,15},{18,19},{22,23},{26,27},{30,31}} | collective-permute-start | bytes 156680 | tf_op jit(solution)/shard_map/ppermute | solution.py:797
  794.8 24.6 %collective-permute-start.45 = (bf16[3,64,136]{1,2,0:T(8,128)(2,1)S(1)}, bf16[3,64,136]{1,2,0:T(8,128)(2,1)}, u32[]{:S(2)}, u32[]{:S(2)}) collective-permute-start(bf16[3,64,136]{1,2,0:T(8,128)(2,1)S(1)} %copy.400), channel_id=1, source_target_pairs={{1,3},{5,7},{9,11},{13,15},{17,19},{21,23},{25,27},{29,31}} | collective-permute-start | bytes 156680 | tf_op jit(solution)/shard_map/ppermute | solution.py:797
  796.0 23.3 %collective-permute-start.44 = (bf16[3,64,136]{1,2,0:T(8,128)(2,1)S(1)}, bf16[3,64,136]{1,2,0:T(8,128)(2,1)}, u32[]{:S(2)}, u32[]{:S(2)}) collective-permute-start(bf16[3,64,136]{1,2,0:T(8,128)(2,1)S(1)} %copy.400), channel_id=1, source_target_pairs={{0,3},{4,7},{8,11},{12,15},{16,19},{20,23},{24,27},{28,31}} | collective-permute-start | bytes 156680 | tf_op jit(solution)/shard_map/ppermute | solution.py:797
  806.2 13.1 %collective-permute-start.47 = (bf16[3,48,136]{1,2,0:T(8,128)(2,1)S(1)}, bf16[3,48,136]{1,2,0:T(8,128)(2,1)S(1)}, u32[]{:S(2)}, u32[]{:S(2)}) collective-permute-start(bf16[3,48,136]{1,2,0:T(8,128)(2,1)S(1)} %slice.344), channel_id=1, source_target_pairs={{1,0},{2,1},{3,2},{5,4},{6,5},{7,6},{9,8},{10,9},{11,10},{13,12},{... | collective-permute-start | bytes 117512 | tf_op jit(solution)/shard_map/ppermute | solution.py:470
  833.0 18.6 %all-to-all-start.6 = ((f32[32,2,1088]{2,1,0:T(2,128)}), f32[32,2,1088]{2,1,0:T(2,128)}, u32[]{:S(2)}, u32[]{:S(2)}) async-start(f32[32,2,1088]{2,1,0:T(2,128)} %broadcast_in_dim.148), calls=%async_computation.6 | async-start | bytes 589824 | tf_op jit(solution)/shard_map/all_to_all | solution.py:58
  (91 other events, 1084.6 us)
Sparse Core Ops, SparseCore 0:
  98.7 225.3 all-gather.1

commit v4 on v3

--- a/solution.py
+++ b/solution.py
@@ -94,12 +94,25 @@
     return total
 
 
+def sum_offsets(blocks):
+    tensor_size, index = lax.axis_size("tensor"), lax.axis_index("tensor")
+    total = 0.0
+    for steps, block in enumerate(blocks):
+        block = block.astype(jnp.float32)
+        near, far = (jnp.pad(block, (ends, (0, 0), (0, 0))) for ends in ((0, 1), (1, 0)))
+        total = total + jnp.where(index + steps >= tensor_size, far, near)
+    return total
+
+
 def gather_ring(block):
     tensor_size = lax.axis_size("tensor")
-    blocks = [block]
+    index, needed = lax.axis_index("tensor"), block.shape[0] - 1
+    blocks = [block[:needed]]
     for steps in range(1, tensor_size):
         ring = [(i, (i + steps) % tensor_size) for i in range(tensor_size)]
-        blocks.append(lax.ppermute(block, "tensor", ring))
+        first = (index + steps >= tensor_size).astype(jnp.int32)
+        sent = lax.dynamic_slice_in_dim(block, first, needed, 0)
+        blocks.append(lax.ppermute(sent, "tensor", ring))
     return blocks
 
 
@@ -570,10 +583,11 @@
     plans = [attention_plan(query_pos, base, offsets, seq_ends) for base in bases]
     row_range = jnp.arange(rows, dtype=jnp.int32)
     steps_back = min(-(-REACH // tensor_size), dp_size - 1) + 1
-    last_base = dp_index - jnp.arange(steps_back, dtype=jnp.int32)
-    distance = tensor_index + tensor_size - jnp.arange(tensor_size, dtype=jnp.int32)
-    last_base = last_base[None] * tensor_size + lax.rem(distance, tensor_size)[:, None]
-    last_base = last_base.reshape(-1) * rows
+    distance = jnp.arange(tensor_size, dtype=jnp.int32)
+    wrapped = (distance > tensor_index).astype(jnp.int32)
+    source = tensor_index - distance + wrapped * tensor_size
+    last_base = dp_index - wrapped[:, None] - jnp.arange(steps_back - 1, dtype=jnp.int32)[None]
+    last_base = (last_base * tensor_size + source[:, None]).reshape(-1) * rows
     last_plan = attention_plan(
         (flat_index * rows + row_range)[None], last_base, row_range, seq_ends
     )
@@ -674,7 +688,7 @@
         grad_down = lax.psum_scatter(grad_down, "chip", scatter_dimension=0, tiled=True)
         grad_up = lax.psum_scatter(grad_up, "chip", scatter_dimension=0, tiled=True)
         grad_out = lax.psum_scatter(grad_out, "chip", scatter_dimension=0, tiled=True)
-    last_pair_grad = last_pair_grad.reshape(tensor_size, steps_back, 2 * HEAD_DIM, rows)
+    last_pair_grad = last_pair_grad.reshape(tensor_size, steps_back - 1, 2 * HEAD_DIM, rows)
     last_arrived = [last_pair_grad[0]]
     for step in range(1, tensor_size):
         back = [(i, (i - step) % tensor_size) for i in range(tensor_size)]
@@ -684,7 +698,7 @@
         query_state, pair_grad = attend_back(qkv, pairs[1], plans[1], known, (), False, ())
         other_grad = other_core(pair_grad)
         last_arrived = after(last_arrived, query_state)
-        last_arrived = sum(block.astype(jnp.float32) for block in last_arrived)
+        last_arrived = sum_offsets(last_arrived)
         last_blocks = [
             lax.ppermute(last_arrived[step].astype(low), layer, line(dp_size, -step))
             for step in range(1, steps_back)
@@ -706,7 +720,7 @@
             last_sum = last_sum + block.astype(jnp.float32)
         pair_sum = pair_grad.astype(jnp.float32) + other_grad.astype(jnp.float32)
     else:
-        last_arrived = sum(block.astype(jnp.float32) for block in last_arrived)
+        last_arrived = sum_offsets(last_arrived)
         last_sum = last_arrived[0]
         for step in range(1, steps_back):
             arrived = lax.ppermute(last_arrived[step].astype(low), layer, line(dp_size, -step))

time: 877 us -> 882 us (level)
  starting transfers between devices: 150 us -> 139 us
    ppermute x3, waiting for transfers between devices: 2.65 us -> 29.4 us  [local(): lax.ppermute(last_pairs, layer, line(dp_size, step))]
    all_to_all x1, waiting for transfers between devices: 23.1 us -> 0.01 us  [local(): qkv = lax.all_to_all(qkv, layer, split_axis=0, concat_axis=0, tiled=True)]
    ppermute x3, waiting for transfers between devices: 35 us -> 17.7 us  [gather_ring(): blocks.append(lax.ppermute(sent, 'tensor', ring))]
    ppermute x8, waiting for transfers between devices: 28.6 us -> 41.9 us  [halve(): sent = lax.ppermute(pick(value, 1 - index, axis), 'chip', neighbour)]
    unnamed x199 -> x200, local copies, waits for them, and re-layouts: 19.9 us -> 17.5 us
  transfers between devices with their start and end apart: 62 -> 62, of which waited for: 23 -> 22; matrix products, arithmetic and copies ran while one was open for 25% -> 25% of each run, Pallas kernels for 20% -> 21%
where the time goes in v4:
time: 882 us; the launch traced here: 865 us
  waiting for transfers between devices  241 us (27%)
  Pallas kernels  178 us (20%)
  starting transfers between devices  139 us (16%)
  local copies, waits for them, and re-layouts  130 us (15%)
  matrix products  85 us (10%)
  other arithmetic  74.1 us (8%)
  between operations  18.2 us (2%)
    pallas_call x6, Pallas kernels, attention_call(): pl.pallas_call(body, out_shape=out_shapes, grid_spec=pltpu.PrefetchScalar...  178 us
    ppermute x6, waiting for transfers between devices, scatter_ring(): lax.ppermute(pick(both, lax.rem(index + steps, tensor_size), 0), 'tensor'...  45.8 us
    ppermute x3, waiting for transfers between devices, gather_tensor(): down.append(lax.ppermute(down[-1], 'tensor', line(count, -1)))  42.6 us
    ppermute x8, waiting for transfers between devices, halve(): sent = lax.ppermute(pick(value, 1 - index, axis), 'chip', neighbour)  41.9 us
    ppermute x3, waiting for transfers between devices, local(): lax.ppermute(last_pairs, layer, line(dp_size, step))  29.4 us
    ppermute x5, waiting for transfers between devices, butterfly(): lax.ppermute(value, axis, [(i, i ^ step) for i in range(count)])  23.1 us
    ppermute x3, starting transfers between devices, gather_ring(): blocks.append(lax.ppermute(sent, 'tensor', ring))  20.5 us
    ppermute x3, waiting for transfers between devices, gather_ring(): blocks.append(lax.ppermute(sent, 'tensor', ring))  17.7 us
  transfers between devices with their start and end apart: 62, of which 22 were waited for; matrix products, arithmetic and copies ran while one was open for 25% of the time, Pallas kernels for 21%

profile of v4, /device:TPU:0, one launch (start us, length us, event | category | flops | bytes accessed | tf_op | source)
XLA Modules:
  0.0 865.1 jit_solution(5734878493106488938)
XLA Ops:
  16.4 6.5 collective-permute-start
  22.9 17.1 %collective-permute-done.1 = bf16[2,192,1088]{2,1,0:T(8,128)(2,1)} collective-permute-done((bf16[2,192,1088]{2,1,0:T(8,128)(2,1)}, bf16[2,192,1088]{2,1,0:T(8,128)(2,1)}, u32[]{:S(2)}, u32[]{:S(2)}) %collective-permute-start.1) | collective-permute-done | bytes 835616 | tf_op jit(solution)/shard_map/ppermute | solution.py:31
  41.3 5.5 collective-permute-start.4
  46.8 16.2 %collective-permute-done.2 = bf16[2,192,1088]{2,1,0:T(8,128)(2,1)} collective-permute-done((bf16[2,192,1088]{2,1,0:T(8,128)(2,1)}, bf16[2,192,1088]{2,1,0:T(8,128)(2,1)}, u32[]{:S(2)}, u32[]{:S(2)}) %collective-permute-start.2) | collective-permute-done | bytes 835616 | tf_op jit(solution)/shard_map/ppermute | solution.py:31
  71.3 4.6 collective-permute-start.5
  75.9 9.3 %collective-permute-done.3 = bf16[2,192,1088]{2,1,0:T(8,128)(2,1)} collective-permute-done((bf16[2,192,1088]{2,1,0:T(8,128)(2,1)}, bf16[2,192,1088]{2,1,0:T(8,128)(2,1)}, u32[]{:S(2)}, u32[]{:S(2)}) %collective-permute-start.3) | collective-permute-done | bytes 835616 | tf_op jit(solution)/shard_map/ppermute | solution.py:31
  88.0 5.3 collective-permute-done.5
  104.8 5.0 collective-permute-start.6
  117.5 4.2 collective-permute-done.6
  126.0 3.5 fusion.21
  131.1 4.4 all-to-all-start
  138.1 3.6 collective-permute-done.8
  148.5 3.6 collective-permute-start.11
  152.1 25.4 %collective-permute-done.13 = bf16[1,128,384]{2,1,0:T(8,128)(2,1)S(1)} collective-permute-done((bf16[1,128,384]{2,1,0:T(8,128)(2,1)S(1)}, bf16[1,128,384]{2,1,0:T(8,128)(2,1)S(1)}, u32[]{:S(2)}, u32[]{:S(2)}) %collective-permute-start.13) | collective-permute-done | bytes 98336 | tf_op jit(solution)/shard_map/ppermute | solution.py:603
  177.5 4.0 collective-permute-done.12
  183.3 19.9 %collective-permute-start.16 = (bf16[3,128,384]{2,1,0:T(8,128)(2,1)S(1)}, bf16[3,128,384]{2,1,0:T(8,128)(2,1)S(1)}, u32[]{:S(2)}, u32[]{:S(2)}) collective-permute-start(bf16[3,128,384]{2,1,0:T(8,128)(2,1)S(1)} %get-tuple-element.142), channel_id=1, source_target_pairs={{0,3},{1,0},{2,1},{3,2},{4,7},{5,4},{6,5},{7,6},{8,11},{9,8},{10,9... | collective-permute-start | bytes 884744 | tf_op jit(solution)/shard_map/ppermute | solution.py:115
  204.6 33.3 %shard_map.254 = (f32[16,64,384]{2,1,0:T(8,128)}, f32[16,1,384]{2,1,0:T(1,128)}, f32[16,1,384]{2,1,0:T(1,128)}) custom-call(s32[112]{0:T(128)} %concatenate.66.refs_0_, bf16[8,192,768]{2,1,0:T(8,128)(2,1)} %all-to-all-done.refs_1_, bf16[8,128,768]{2,1,0:T(8,128)(2,1)} %copy-done.39, s32[8,2,768]{2,1,0:T(2,128)} %pad_add_fusion.refs_3_, s32[768,1]{1,0:T(8,128)} %add.978.refs_4_), custom_call_target="tpu_custom_call" | custom-call | flops 14495514624 | bytes 7864320 | tf_op jit(solution)/shard_map/pallas_call | solution.py:401
  237.9 17.7 %collective-permute-done.15.refs_10_ = bf16[3,128,384]{2,1,0:T(8,128)(2,1)S(1)} collective-permute-done((bf16[3,128,384]{2,1,0:T(8,128)(2,1)S(1)}, bf16[3,128,384]{2,1,0:T(8,128)(2,1)S(1)}, u32[]{:S(2)}, u32[]{:S(2)}) %collective-permute-start.15) | collective-permute-done | bytes 294944 | tf_op jit(solution)/shard_map/ppermute | solution.py:115
  257.0 35.8 %shard_map.255 = (f32[8,64,768]{2,1,0:T(8,128)}, bf16[32,64,192]{2,1,0:T(8,128)(2,1)}, f32[16,1,384]{2,1,0:T(1,128)}) custom-call(s32[112]{0:T(128)} %concatenate.64.refs_0_, bf16[8,192,768]{2,1,0:T(8,128)(2,1)} %all-to-all-done.refs_1_, bf16[8,128,768]{2,1,0:T(8,128)(2,1)} %copy-done.84, s32[8,2,768]{2,1,0:T(2,128)} %pad_add_fusion.refs_3_, ...), custom_call_target="tpu_custom_call" | custom-call | flops 14495514624 | bytes 7864320 | tf_op jit(solution)/shard_map/pallas_call | solution.py:401
  292.8 3.7 all-to-all-start.1
  307.1 5.7 copy.394
  313.5 11.6 %shard_map.256 = (f32[1,64,384]{2,1,0:T(8,128)}, bf16[1,64,384]{2,1,0:T(8,128)(2,1)}, f32[1,1,384]{2,1,0:T(1,128)}) custom-call(s32[62]{0:T(128)} %concatenate.70.refs_0_, bf16[1,192,384]{2,1,0:T(8,128)(2,1)} %copy-done.47, bf16[12,128,384]{2,1,0:T(8,128)(2,1)} %constant_dynamic-update-slice_fusion.refs_2_, s32[1,2,384]{2,1,0:T(2,128)} %pad_add_fusion.1.refs_3_, ...), custom_call_target="tpu_custom_call" | custom-call | flops 905969664 | bytes 2654208 | tf_op jit(solution)/shard_map/pallas_call | solution.py:401
  325.1 4.0 all-to-all-done.1
  332.5 3.4 slice.319
  336.1 3.0 reshape.741
  339.1 3.1 fusion.25
  344.5 8.4 fusion.102
  352.9 7.6 fusion.68
  360.5 9.6 %convolution_convert_fusion.1 = bf16[1088,2176]{1,0:T(8,128)(2,1)S(1)} fusion(bf16[768,1088]{0,1:T(8,128)(2,1)} %constant_dynamic-update-slice_fusion.6, f32[768,2176]{1,0:T(8,128)S(1)} %fusion.68, f32[2176]{0:T(1024)S(1)} %reshape.763), kind=kOutput, calls=%fused_computation.1 | convolution fusion | flops 3655540736 | bytes 13099520 | tf_op jit(solution)/shard_map/dot_general | solution.py:673
  370.2 12.9 %convert_reduce_fusion = (f32[2176]{0:T(1024)S(1)}, bf16[768,2176]{1,0:T(8,128)(2,1)}) fusion(f32[768,2176]{1,0:T(8,128)S(1)} %fusion.68, f32[2176]{0:T(1024)S(1)} %reshape.763, bf16[768,1088]{0,1:T(8,128)(2,1)} %constant_dynamic-update-slice_fusion.6, bf16[2176,1088]{1,0:T(8,128)(2,1)S(1)} %bitcast.312), kind=kOutput, calls=%fused_computation.11 | convolution fusion | flops 3674896384 | bytes 16450560 | tf_op jit(solution)/shard_map/dot_general | solution.py:637
  383.1 6.4 fusion.110
  394.4 8.5 convolution_convert_fusion
  413.6 3.4 all-to-all-start.2
  417.0 3.4 dynamic-slice_bitcast_fusion
  426.4 13.3 %shard_map.259 = (bf16[1,64,384]{2,1,0:T(8,128)(2,1)}, bf16[12,128,384]{2,1,0:T(8,128)(2,1)}) custom-call(s32[62]{0:T(128)} %concatenate.70.refs_0_, bf16[1,192,384]{2,1,0:T(8,128)(2,1)} %copy-done.47, bf16[12,128,384]{2,1,0:T(8,128)(2,1)} %constant_dynamic-update-slice_fusion.refs_2_, s32[1,2,384]{2,1,0:T(2,128)} %pad_add_fusion.1.refs_3_, ...), custom_call_target="tpu_custom_call" | custom-call | flops 2264924160 | bytes 2654208 | tf_op jit(solution)/shard_map/pallas_call | solution.py:401
  451.2 7.4 all-to-all-done.2.refs_5_
  458.6 42.0 %shard_map.257 = (f32[16,64,384]{2,1,0:T(8,128)}, bf16[8,128,768]{2,1,0:T(8,128)(2,1)}) custom-call(s32[112]{0:T(128)} %concatenate.64.refs_0_, bf16[8,192,768]{2,1,0:T(8,128)(2,1)} %all-to-all-done.refs_1_, bf16[8,128,768]{2,1,0:T(8,128)(2,1)} %copy-done.84, s32[8,2,768]{2,1,0:T(2,128)} %pad_add_fusion.refs_3_, s32[768,1]{1,0:T(8,128)} %add.978.refs_4_, ...), custom_call_target="tpu_custom_call" | custom-call | flops 36238786560 | bytes 7864320 | tf_op jit(solution)/shard_map/pallas_call | solution.py:401
  511.8 5.1 collective-permute-start.48
  516.9 2.9 fusion.8.refs_9_
  521.1 34.1 %collective-permute-done.22 = bf16[2,272,2176]{2,1,0:T(8,128)(2,1)S(1)} collective-permute-done((bf16[2,272,2176]{2,1,0:T(8,128)(2,1)}, bf16[2,272,2176]{2,1,0:T(8,128)(2,1)S(1)}, u32[]{:S(2)}, u32[]{:S(2)}) %collective-permute-start.22) | collective-permute-done | bytes 2367520 | tf_op jit(solution)/shard_map/ppermute | solution.py:71
  557.2 42.2 %shard_map.258 = (bf16[8,64,768]{2,1,0:T(8,128)(2,1)}, bf16[8,128,768]{2,1,0:T(8,128)(2,1)}) custom-call(s32[112]{0:T(128)} %concatenate.66.refs_0_, bf16[8,192,768]{2,1,0:T(8,128)(2,1)} %all-to-all-done.refs_1_, bf16[8,128,768]{2,1,0:T(8,128)(2,1)} %copy-done.39, s32[8,2,768]{2,1,0:T(2,128)} %pad_add_fusion.refs_3_, s32[768,1]{1,0:T(8,128)} %add.978.refs_4_, ...), custom_call_target="tpu_custom_call" | custom-call | flops 36238786560 | bytes 7864320 | tf_op jit(solution)/shard_map/pallas_call | solution.py:401
  621.3 3.6 convert_add_fusion.2
  626.5 4.4 all-to-all-start.3
  633.5 3.2 stack.52
  636.7 3.2 stack.51
  652.2 8.1 collective-permute-done.37
  663.5 14.1 %collective-permute-done.29 = bf16[2,272,544]{2,1,0:T(8,128)(2,1)} collective-permute-done((bf16[2,272,544]{2,1,0:T(8,128)(2,1)}, bf16[2,272,544]{2,1,0:T(8,128)(2,1)}, u32[]{:S(2)}, u32[]{:S(2)}) %collective-permute-start.29) | collective-permute-done | bytes 591904 | tf_op jit(solution)/shard_map/ppermute | solution.py:92
  677.7 30.0 %collective-permute-done.28 = bf16[2,272,544]{2,1,0:T(8,128)(2,1)} collective-permute-done((bf16[2,272,544]{2,1,0:T(8,128)(2,1)}, bf16[2,272,544]{2,1,0:T(8,128)(2,1)}, u32[]{:S(2)}, u32[]{:S(2)}) %collective-permute-start.28) | collective-permute-done | bytes 591904 | tf_op jit(solution)/shard_map/ppermute | solution.py:92
  707.7 2.9 fusion.97
  711.8 4.0 fusion.12
  715.8 3.8 copy.389
  719.6 4.6 all-to-all-start.5
  732.0 10.2 %fusion.96 = f32[768,1088]{0,1:T(8,128)S(1)} fusion(bf16[2176,1088]{1,0:T(8,128)(2,1)} %bitcast.309, f32[768,2176]{1,0:T(8,128)} %copy-done.87, f32[2176]{0:T(1024)S(1)} %copy-done.79), kind=kOutput, calls=%fused_computation.270 | convolution fusion | flops 3653173248 | bytes 14770688 | tf_op jit(solution)/shard_map/dot_general | solution.py:648
  747.3 6.9 collective-permute-done.39
  754.3 4.6 collective-permute-start.40
  759.7 8.1 collective-permute-done.40
  780.4 3.6 all-to-all-start.4
  791.0 5.1 collective-permute-done.43
  800.6 4.0 collective-permute-start.44
  813.2 10.5 %collective-permute-done.47 = bf16[3,48,136]{1,2,0:T(8,128)(2,1)S(1)} collective-permute-done((bf16[3,48,136]{1,2,0:T(8,128)(2,1)S(1)}, bf16[3,48,136]{1,2,0:T(8,128)(2,1)S(1)}, u32[]{:S(2)}, u32[]{:S(2)}) %collective-permute-start.47) | collective-permute-done | bytes 39200 | tf_op jit(solution)/shard_map/ppermute | solution.py:483
  833.0 3.6 fusion.41
  837.4 8.3 all-to-all-start.6
  845.8 5.3 fusion.40
  851.1 5.2 all-to-all-done.6
  (523 shorter events, 223.1 us)
Async XLA Ops:
  7.2 324.4 %all-gather.2.cloned.1.call-start = ((), (), s32[]{:S(2)}) async-start(), calls=%async_computation.7 | async-start | bytes 13473792 | tf_op jit(solution)/shard_map/all_gather | solution.py:563
  15.1 24.9 %collective-permute-start.1 = (bf16[2,192,1088]{2,1,0:T(8,128)(2,1)}, bf16[2,192,1088]{2,1,0:T(8,128)(2,1)}, u32[]{:S(2)}, u32[]{:S(2)}) collective-permute-start(bf16[2,192,1088]{2,1,0:T(8,128)(2,1)} %bitcast.326), channel_id=1, source_target_pairs={{1,0},{2,1},{3,2},{5,4},{6,5},{7,6},{9,8},{10,9},{11,10},{13,12},{... | collective-permute-start | bytes 2506760 | tf_op jit(solution)/shard_map/ppermute | solution.py:31
  16.4 24.9 %collective-permute-start = (bf16[2,192,1088]{2,1,0:T(8,128)(2,1)}, bf16[2,192,1088]{2,1,0:T(8,128)(2,1)}, u32[]{:S(2)}, u32[]{:S(2)}) collective-permute-start(bf16[2,192,1088]{2,1,0:T(8,128)(2,1)} %bitcast.327), channel_id=1, source_target_pairs={{0,1},{1,2},{2,3},{4,5},{5,6},{6,7},{8,9},{9,10},{10,11},{12,13},{... | collective-permute-start | bytes 2506760 | tf_op jit(solution)/shard_map/ppermute | solution.py:30
  40.0 23.0 %collective-permute-start.2 = (bf16[2,192,1088]{2,1,0:T(8,128)(2,1)}, bf16[2,192,1088]{2,1,0:T(8,128)(2,1)}, u32[]{:S(2)}, u32[]{:S(2)}) collective-permute-start(bf16[2,192,1088]{2,1,0:T(8,128)(2,1)} %collective-permute-done.1), channel_id=1, source_target_pairs={{1,0},{2,1},{3,2},{5,4},{6,5},{7,6},{9,8},{10,9},{11,10},{13,12},{... | collective-permute-start | bytes 2506760 | tf_op jit(solution)/shard_map/ppermute | solution.py:31
  41.3 29.9 %collective-permute-start.4 = (bf16[2,192,1088]{2,1,0:T(8,128)(2,1)}, bf16[2,192,1088]{2,1,0:T(8,128)(2,1)}, u32[]{:S(2)}, u32[]{:S(2)}) collective-permute-start(bf16[2,192,1088]{2,1,0:T(8,128)(2,1)} %collective-permute-done), channel_id=1, source_target_pairs={{0,1},{1,2},{2,3},{4,5},{5,6},{6,7},{8,9},{9,10},{10,11},{12,13},{... | collective-permute-start | bytes 2506760 | tf_op jit(solution)/shard_map/ppermute | solution.py:30
  63.0 22.1 %collective-permute-start.3 = (bf16[2,192,1088]{2,1,0:T(8,128)(2,1)}, bf16[2,192,1088]{2,1,0:T(8,128)(2,1)}, u32[]{:S(2)}, u32[]{:S(2)}) collective-permute-start(bf16[2,192,1088]{2,1,0:T(8,128)(2,1)} %collective-permute-done.2), channel_id=1, source_target_pairs={{1,0},{2,1},{3,2},{5,4},{6,5},{7,6},{9,8},{10,9},{11,10},{13,12},{... | collective-permute-start | bytes 2506760 | tf_op jit(solution)/shard_map/ppermute | solution.py:31
  71.3 22.0 %collective-permute-start.5 = (bf16[2,192,1088]{2,1,0:T(8,128)(2,1)}, bf16[2,192,1088]{2,1,0:T(8,128)(2,1)S(1)}, u32[]{:S(2)}, u32[]{:S(2)}) collective-permute-start(bf16[2,192,1088]{2,1,0:T(8,128)(2,1)} %collective-permute-done.4), channel_id=1, source_target_pairs={{0,1},{1,2},{2,3},{4,5},{5,6},{6,7},{8,9},{9,10},{10,11},{12,13},{... | collective-permute-start | bytes 2506760 | tf_op jit(solution)/shard_map/ppermute | solution.py:30
  100.4 37.7 %collective-permute-start.9 = (bf16[3,64,1088]{2,1,0:T(8,128)(2,1)}, bf16[3,64,1088]{2,1,0:T(8,128)(2,1)S(1)}, u32[]{:S(2)}, u32[]{:S(2)}) collective-permute-start(bf16[3,64,1088]{2,1,0:T(8,128)(2,1)} %slice.261), channel_id=1, source_target_pairs={{3,1},{7,5},{11,9},{15,13},{19,17},{23,21},{27,25},{31,29}} | collective-permute-start | bytes 1253384 | tf_op jit(solution)/shard_map/ppermute | solution.py:476
  101.1 40.7 %collective-permute-start.8 = (bf16[3,64,1088]{2,1,0:T(8,128)(2,1)}, bf16[3,64,1088]{2,1,0:T(8,128)(2,1)}, u32[]{:S(2)}, u32[]{:S(2)}) collective-permute-start(bf16[3,64,1088]{2,1,0:T(8,128)(2,1)} %slice.261), channel_id=1, source_target_pairs={{3,0},{7,4},{11,8},{15,12},{19,16},{23,20},{27,24},{31,28}} | collective-permute-start | bytes 1253384 | tf_op jit(solution)/shard_map/ppermute | solution.py:476
  102.4 39.4 %collective-permute-start.10 = (bf16[3,64,1088]{2,1,0:T(8,128)(2,1)}, bf16[3,64,1088]{2,1,0:T(8,128)(2,1)}, u32[]{:S(2)}, u32[]{:S(2)}) collective-permute-start(bf16[3,64,1088]{2,1,0:T(8,128)(2,1)} %slice.261), channel_id=1, source_target_pairs={{3,2},{7,6},{11,10},{15,14},{19,18},{23,22},{27,26},{31,30}} | collective-permute-start | bytes 1253384 | tf_op jit(solution)/shard_map/ppermute | solution.py:476
  104.8 16.9 %collective-permute-start.6 = (bf16[3,48,1088]{2,1,0:T(8,128)(2,1)S(1)}, bf16[3,48,1088]{2,1,0:T(8,128)(2,1)S(1)}, u32[]{:S(2)}, u32[]{:S(2)}) collective-permute-start(bf16[3,48,1088]{2,1,0:T(8,128)(2,1)S(1)} %slice.256), channel_id=1, source_target_pairs={{0,1},{1,2},{2,3},{4,5},{5,6},{6,7},{8,9},{9,10},{10,11},{12,13},{... | collective-permute-start | bytes 940040 | tf_op jit(solution)/shard_map/ppermute | solution.py:466
  109.9 195.1 %collective-permute-start.19 = (bf16[384,1088]{0,1:T(8,128)(2,1)S(1)}, bf16[384,1088]{0,1:T(8,128)(2,1)}, u32[]{:S(2)}, u32[]{:S(2)}) collective-permute-start(bf16[384,1088]{0,1:T(8,128)(2,1)S(1)} %copy-done.14), channel_id=1, source_target_pairs={{0,4},{4,0},{1,5},{5,1},{2,6},{6,2},{3,7},{7,3},{8,12},{12,8},{9,1... | collective-permute-start | bytes 2506760 | tf_op jit(solution)/shard_map/ppermute | solution.py:52
  131.1 50.5 %all-to-all-start = ((bf16[8,192,768]{2,1,0:T(8,128)(2,1)}), bf16[8,192,768]{2,1,0:T(8,128)(2,1)}, u32[]{:S(2)}, u32[]{:S(2)}) async-start(bf16[8,192,768]{2,1,0:T(8,128)(2,1)} %bitcast.22), calls=%async_computation | async-start | bytes 4718592 | tf_op jit(solution)/shard_map/all_to_all | solution.py:597
  144.4 33.1 %collective-permute-start.13 = (bf16[1,128,384]{2,1,0:T(8,128)(2,1)S(1)}, bf16[1,128,384]{2,1,0:T(8,128)(2,1)S(1)}, u32[]{:S(2)}, u32[]{:S(2)}) collective-permute-start(bf16[1,128,384]{2,1,0:T(8,128)(2,1)S(1)} %get-tuple-element.146), channel_id=1, source_target_pairs={{0,12},{4,16},{8,20},{12,24},{16,28},{1,13},{5,17},{9,21},{13,25},... | collective-permute-start | bytes 294920 | tf_op jit(solution)/shard_map/ppermute | solution.py:603
  145.7 35.8 %collective-permute-start.12 = (bf16[1,128,384]{2,1,0:T(8,128)(2,1)S(1)}, bf16[1,128,384]{2,1,0:T(8,128)(2,1)S(1)}, u32[]{:S(2)}, u32[]{:S(2)}) collective-permute-start(bf16[1,128,384]{2,1,0:T(8,128)(2,1)S(1)} %get-tuple-element.146), channel_id=1, source_target_pairs={{0,8},{4,12},{8,16},{12,20},{16,24},{20,28},{1,9},{5,13},{9,17},{1... | collective-permute-start | bytes 294920 | tf_op jit(solution)/shard_map/ppermute | solution.py:603
  148.5 33.0 %collective-permute-start.11 = (bf16[1,128,384]{2,1,0:T(8,128)(2,1)S(1)}, bf16[1,128,384]{2,1,0:T(8,128)(2,1)S(1)}, u32[]{:S(2)}, u32[]{:S(2)}) collective-permute-start(bf16[1,128,384]{2,1,0:T(8,128)(2,1)S(1)} %get-tuple-element.146), channel_id=1, source_target_pairs={{0,4},{4,8},{8,12},{12,16},{16,20},{20,24},{24,28},{1,5},{5,9},{9,... | collective-permute-start | bytes 294920 | tf_op jit(solution)/shard_map/ppermute | solution.py:603
  183.1 54.7 %collective-permute-start.7 = (bf16[8,128,768]{2,1,0:T(8,128)(2,1)S(1)}, bf16[8,128,768]{2,1,0:T(8,128)(2,1)S(1)}, u32[]{:S(2)}, u32[]{:S(2)}) collective-permute-start(bf16[8,128,768]{2,1,0:T(8,128)(2,1)S(1)} %slice.315.refs_2_), channel_id=1, source_target_pairs={{0,4},{4,0},{1,5},{5,1},{2,6},{6,2},{3,7},{7,3},{8,12},{12,8},{9,1... | collective-permute-start | bytes 4718600 | tf_op jit(solution)/shard_map/ppermute | solution.py:52
  183.3 54.6 %collective-permute-start.16 = (bf16[3,128,384]{2,1,0:T(8,128)(2,1)S(1)}, bf16[3,128,384]{2,1,0:T(8,128)(2,1)S(1)}, u32[]{:S(2)}, u32[]{:S(2)}) collective-permute-start(bf16[3,128,384]{2,1,0:T(8,128)(2,1)S(1)} %get-tuple-element.142), channel_id=1, source_target_pairs={{0,3},{1,0},{2,1},{3,2},{4,7},{5,4},{6,5},{7,6},{8,11},{9,8},{10,9... | collective-permute-start | bytes 884744 | tf_op jit(solution)/shard_map/ppermute | solution.py:115
  203.2 52.4 %collective-permute-start.15 = (bf16[3,128,384]{2,1,0:T(8,128)(2,1)S(1)}, bf16[3,128,384]{2,1,0:T(8,128)(2,1)S(1)}, u32[]{:S(2)}, u32[]{:S(2)}) collective-permute-start(bf16[3,128,384]{2,1,0:T(8,128)(2,1)S(1)} %get-tuple-element.143), channel_id=1, source_target_pairs={{0,2},{1,3},{2,0},{3,1},{4,6},{5,7},{6,4},{7,5},{8,10},{9,11},{10,... | collective-permute-start | bytes 884744 | tf_op jit(solution)/shard_map/ppermute | solution.py:115
  203.2 52.4 %collective-permute-start.14 = (bf16[3,128,384]{2,1,0:T(8,128)(2,1)S(1)}, bf16[3,128,384]{2,1,0:T(8,128)(2,1)S(1)}, u32[]{:S(2)}, u32[]{:S(2)}) collective-permute-start(bf16[3,128,384]{2,1,0:T(8,128)(2,1)S(1)} %get-tuple-element.144), channel_id=1, source_target_pairs={{0,1},{1,2},{2,3},{3,0},{4,5},{5,6},{6,7},{7,4},{8,9},{9,10},{10,1... | collective-permute-start | bytes 884744 | tf_op jit(solution)/shard_map/ppermute | solution.py:115
  292.8 36.2 %all-to-all-start.1 = ((bf16[32,64,192]{2,1,0:T(8,128)(2,1)}), bf16[32,64,192]{2,1,0:T(8,128)(2,1)}, u32[]{:S(2)}, u32[]{:S(2)}) async-start(bf16[32,64,192]{2,1,0:T(8,128)(2,1)} %get-tuple-element.60), calls=%async_computation.1 | async-start | bytes 2097152 | tf_op jit(solution)/shard_map/all_to_all | solution.py:612
  297.3 107.9 %copy-start.54 = (f32[1088]{0:T(1024)}, f32[1088]{0:T(1024)S(1)}, u32[]{:S(2)}) copy-start(f32[1088]{0:T(1024)S(1)} %convert_element_type.419) | copy-start | bytes 13060
  343.8 61.4 %copy-start.2 = (f32[384,1088]{0,1:T(8,128)}, f32[384,1088]{0,1:T(8,128)S(1)}, u32[]{:S(2)}) copy-start(f32[384,1088]{0,1:T(8,128)S(1)} %get-tuple-element.166) | copy-start | bytes 5013508
  344.4 8.5 collective-permute-start.17
  389.5 13.4 %collective-permute-start.20 = (bf16[384,1088]{0,1:T(8,128)(2,1)S(1)}, bf16[384,1088]{0,1:T(8,128)(2,1)}, u32[]{:S(2)}, u32[]{:S(2)}) collective-permute-start(bf16[384,1088]{0,1:T(8,128)(2,1)S(1)} %slice.413), channel_id=1, source_target_pairs={{0,4},{4,0},{1,5},{5,1},{2,6},{6,2},{3,7},{7,3},{8,12},{12,8},{9,1... | collective-permute-start | bytes 2506760 | tf_op jit(solution)/shard_map/ppermute | solution.py:52
  393.1 118.8 %collective-permute-start.21 = (bf16[2,272,2176]{2,1,0:T(8,128)(2,1)}, bf16[2,272,2176]{2,1,0:T(8,128)(2,1)}, u32[]{:S(2)}, u32[]{:S(2)}) collective-permute-start(bf16[2,272,2176]{2,1,0:T(8,128)(2,1)} %dynamic-slice_bitcast_fusion.1), channel_id=1, source_target_pairs={{0,16},{8,24},{16,0},{24,8},{1,17},{9,25},{17,1},{25,9},{2,18},{10... | collective-permute-start | bytes 7102472 | tf_op jit(solution)/shard_map/ppermute | solution.py:71
  413.6 45.0 %all-to-all-start.2 = ((bf16[32,64,192]{2,1,0:T(8,128)(2,1)}), bf16[32,64,192]{2,1,0:T(8,128)(2,1)}, u32[]{:S(2)}, u32[]{:S(2)}) async-start(bf16[32,64,192]{2,1,0:T(8,128)(2,1)} %bitcast.48), calls=%async_computation.2 | async-start | bytes 2097152 | tf_op jit(solution)/shard_map/all_to_all | solution.py:664
  442.1 58.4 %collective-permute-start.32 = (bf16[3,128,384]{2,1,0:T(8,128)(2,1)}, bf16[3,128,384]{2,1,0:T(8,128)(2,1)}, u32[]{:S(2)}, u32[]{:S(2)}) collective-permute-start(bf16[3,128,384]{2,1,0:T(8,128)(2,1)} %get-tuple-element.128), channel_id=1, source_target_pairs={{0,1},{1,2},{2,3},{3,0},{4,5},{5,6},{6,7},{7,4},{8,9},{9,10},{10,1... | collective-permute-start | bytes 884744 | tf_op jit(solution)/shard_map/ppermute | solution.py:695
  443.7 57.4 %collective-permute-start.31 = (bf16[3,128,384]{2,1,0:T(8,128)(2,1)}, bf16[3,128,384]{2,1,0:T(8,128)(2,1)}, u32[]{:S(2)}, u32[]{:S(2)}) collective-permute-start(bf16[3,128,384]{2,1,0:T(8,128)(2,1)} %get-tuple-element.129), channel_id=1, source_target_pairs={{0,2},{1,3},{2,0},{3,1},{4,6},{5,7},{6,4},{7,5},{8,10},{9,11},{10,... | collective-permute-start | bytes 884744 | tf_op jit(solution)/shard_map/ppermute | solution.py:695
  446.2 54.9 %collective-permute-start.30 = (bf16[3,128,384]{2,1,0:T(8,128)(2,1)}, bf16[3,128,384]{2,1,0:T(8,128)(2,1)}, u32[]{:S(2)}, u32[]{:S(2)}) collective-permute-start(bf16[3,128,384]{2,1,0:T(8,128)(2,1)} %get-tuple-element.130), channel_id=1, source_target_pairs={{0,3},{1,0},{2,1},{3,2},{4,7},{5,4},{6,5},{7,6},{8,11},{9,8},{10,9... | collective-permute-start | bytes 884744 | tf_op jit(solution)/shard_map/ppermute | solution.py:695
  450.8 50.4 %collective-permute-start.23 = (bf16[2,272,1088]{2,1,0:T(8,128)(2,1)}, bf16[2,272,1088]{2,1,0:T(8,128)(2,1)}, u32[]{:S(2)}, u32[]{:S(2)}) collective-permute-start(bf16[2,272,1088]{2,1,0:T(8,128)(2,1)} %fusion.55), channel_id=1, source_target_pairs={{0,8},{8,0},{16,24},{24,16},{1,9},{9,1},{17,25},{25,17},{2,10},{10... | collective-permute-start | bytes 3551240 | tf_op jit(solution)/shard_map/ppermute | solution.py:71
  500.5 54.6 %collective-permute-start.22 = (bf16[2,272,2176]{2,1,0:T(8,128)(2,1)}, bf16[2,272,2176]{2,1,0:T(8,128)(2,1)S(1)}, u32[]{:S(2)}, u32[]{:S(2)}) collective-permute-start(bf16[2,272,2176]{2,1,0:T(8,128)(2,1)} %dynamic-slice_bitcast_fusion), channel_id=1, source_target_pairs={{0,8},{8,0},{16,24},{24,16},{1,9},{9,1},{17,25},{25,17},{2,10},{10... | collective-permute-start | bytes 7102472 | tf_op jit(solution)/shard_map/ppermute | solution.py:71
  505.1 95.4 %collective-permute-start.35 = (bf16[128,384]{1,0:T(8,128)(2,1)}, bf16[128,384]{1,0:T(8,128)(2,1)S(1)}, u32[]{:S(2)}, u32[]{:S(2)}) collective-permute-start(bf16[128,384]{1,0:T(8,128)(2,1)} %get-tuple-element.139), channel_id=1, source_target_pairs={{12,0},{16,4},{20,8},{24,12},{28,16},{13,1},{17,5},{21,9},{25,13},... | collective-permute-start | bytes 294920 | tf_op jit(solution)/shard_map/ppermute | solution.py:703
  506.4 96.5 %collective-permute-start.34 = (bf16[128,384]{1,0:T(8,128)(2,1)S(1)}, bf16[128,384]{1,0:T(8,128)(2,1)S(1)}, u32[]{:S(2)}, u32[]{:S(2)}) collective-permute-start(bf16[128,384]{1,0:T(8,128)(2,1)S(1)} %get-tuple-element.140), channel_id=1, source_target_pairs={{8,0},{12,4},{16,8},{20,12},{24,16},{28,20},{9,1},{13,5},{17,9},{2... | collective-permute-start | bytes 294920 | tf_op jit(solution)/shard_map/ppermute | solution.py:703
  507.7 95.3 %collective-permute-start.33 = (bf16[128,384]{1,0:T(8,128)(2,1)S(1)}, bf16[128,384]{1,0:T(8,128)(2,1)S(1)}, u32[]{:S(2)}, u32[]{:S(2)}) collective-permute-start(bf16[128,384]{1,0:T(8,128)(2,1)S(1)} %get-tuple-element.141), channel_id=1, source_target_pairs={{4,0},{8,4},{12,8},{16,12},{20,16},{24,20},{28,24},{5,1},{9,5},{13... | collective-permute-start | bytes 294920 | tf_op jit(solution)/shard_map/ppermute | solution.py:703
  511.8 94.8 %collective-permute-start.48 = (bf16[272,1088]{1,0:T(8,128)(2,1)}, bf16[272,1088]{1,0:T(8,128)(2,1)}, u32[]{:S(2)}, u32[]{:S(2)}) collective-permute-start(bf16[272,1088]{1,0:T(8,128)(2,1)} %dynamic-slice_bitcast_fusion.7), channel_id=1, source_target_pairs={{0,16},{8,24},{16,0},{24,8},{1,17},{9,25},{17,1},{25,9},{2,18},{10... | collective-permute-start | bytes 1775624 | tf_op jit(solution)/shard_map/ppermute | solution.py:71
  555.2 63.0 %collective-permute-start.26 = (bf16[272,2176]{1,0:T(8,128)(2,1)}, bf16[272,2176]{1,0:T(8,128)(2,1)}, u32[]{:S(2)}, u32[]{:S(2)}) collective-permute-start(bf16[272,2176]{1,0:T(8,128)(2,1)} %dynamic-slice_bitcast_fusion.2), channel_id=1, source_target_pairs={{0,8},{8,0},{16,24},{24,16},{1,9},{9,1},{17,25},{25,17},{2,10},{10... | collective-permute-start | bytes 3551240 | tf_op jit(solution)/shard_map/ppermute | solution.py:71
  600.5 18.0 %collective-permute-start.25 = (bf16[272,2176]{1,0:T(8,128)(2,1)}, bf16[272,2176]{1,0:T(8,128)(2,1)}, u32[]{:S(2)}, u32[]{:S(2)}) collective-permute-start(bf16[272,2176]{1,0:T(8,128)(2,1)} %dynamic-slice_bitcast_fusion.3), channel_id=1, source_target_pairs={{0,16},{8,24},{16,0},{24,8},{1,17},{9,25},{17,1},{25,9},{2,18},{10... | collective-permute-start | bytes 3551240 | tf_op jit(solution)/shard_map/ppermute | solution.py:71
  602.9 18.3 %collective-permute-start.24 = (bf16[8,128,768]{2,1,0:T(8,128)(2,1)}, bf16[8,128,768]{2,1,0:T(8,128)(2,1)}, u32[]{:S(2)}, u32[]{:S(2)}) collective-permute-start(bf16[8,128,768]{2,1,0:T(8,128)(2,1)} %get-tuple-element.71), channel_id=1, source_target_pairs={{0,4},{4,0},{1,5},{5,1},{2,6},{6,2},{3,7},{7,3},{8,12},{12,8},{9,1... | collective-permute-start | bytes 4718600 | tf_op jit(solution)/shard_map/ppermute | solution.py:52
  615.8 31.0 %collective-permute-start.51 = (bf16[272,272]{1,0:T(8,128)(2,1)}, bf16[272,272]{1,0:T(8,128)(2,1)}, u32[]{:S(2)}, u32[]{:S(2)}) collective-permute-start(bf16[272,272]{1,0:T(8,128)(2,1)} %bitcast.294), channel_id=1, source_target_pairs={{0,3},{1,0},{2,1},{3,2},{4,7},{5,4},{6,5},{7,6},{8,11},{9,8},{10,9... | collective-permute-start | bytes 443912 | tf_op jit(solution)/shard_map/ppermute | solution.py:92
  615.8 32.0 %collective-permute-start.49 = (bf16[272,272]{1,0:T(8,128)(2,1)}, bf16[272,272]{1,0:T(8,128)(2,1)}, u32[]{:S(2)}, u32[]{:S(2)}) collective-permute-start(bf16[272,272]{1,0:T(8,128)(2,1)} %bitcast.296), channel_id=1, source_target_pairs={{0,1},{1,2},{2,3},{3,0},{4,5},{5,6},{6,7},{7,4},{8,9},{9,10},{10,1... | collective-permute-start | bytes 443912 | tf_op jit(solution)/shard_map/ppermute | solution.py:92
  618.2 29.7 %collective-permute-start.50 = (bf16[272,272]{1,0:T(8,128)(2,1)}, bf16[272,272]{1,0:T(8,128)(2,1)}, u32[]{:S(2)}, u32[]{:S(2)}) collective-permute-start(bf16[272,272]{1,0:T(8,128)(2,1)} %bitcast.295), channel_id=1, source_target_pairs={{0,2},{1,3},{2,0},{3,1},{4,6},{5,7},{6,4},{7,5},{8,10},{9,11},{10,... | collective-permute-start | bytes 443912 | tf_op jit(solution)/shard_map/ppermute | solution.py:92
  626.5 85.3 %all-to-all-start.3 = ((bf16[8,192,768]{2,1,0:T(8,128)(2,1)}), bf16[8,192,768]{2,1,0:T(8,128)(2,1)}, u32[]{:S(2)}, u32[]{:S(2)}) async-start(bf16[8,192,768]{2,1,0:T(8,128)(2,1)} %pad_maximum_fusion), calls=%async_computation.3 | async-start | bytes 4718592 | tf_op jit(solution)/shard_map/all_to_all | solution.py:734
  642.9 20.6 %collective-permute-start.27 = (bf16[2,272,544]{2,1,0:T(8,128)(2,1)}, bf16[2,272,544]{2,1,0:T(8,128)(2,1)}, u32[]{:S(2)}, u32[]{:S(2)}) collective-permute-start(bf16[2,272,544]{2,1,0:T(8,128)(2,1)} %get-tuple-element.121), channel_id=1, source_target_pairs={{0,1},{1,2},{2,3},{3,0},{4,5},{5,6},{6,7},{7,4},{8,9},{9,10},{10,1... | collective-permute-start | bytes 1775624 | tf_op jit(solution)/shard_map/ppermute | solution.py:92
  644.8 32.8 %collective-permute-start.29 = (bf16[2,272,544]{2,1,0:T(8,128)(2,1)}, bf16[2,272,544]{2,1,0:T(8,128)(2,1)}, u32[]{:S(2)}, u32[]{:S(2)}) collective-permute-start(bf16[2,272,544]{2,1,0:T(8,128)(2,1)} %get-tuple-element.122), channel_id=1, source_target_pairs={{0,3},{1,0},{2,1},{3,2},{4,7},{5,4},{6,5},{7,6},{8,11},{9,8},{10,9... | collective-permute-start | bytes 1775624 | tf_op jit(solution)/shard_map/ppermute | solution.py:92
  646.8 60.9 %collective-permute-start.28 = (bf16[2,272,544]{2,1,0:T(8,128)(2,1)}, bf16[2,272,544]{2,1,0:T(8,128)(2,1)}, u32[]{:S(2)}, u32[]{:S(2)}) collective-permute-start(bf16[2,272,544]{2,1,0:T(8,128)(2,1)} %get-tuple-element.123), channel_id=1, source_target_pairs={{0,2},{1,3},{2,0},{3,1},{4,6},{5,7},{6,4},{7,5},{8,10},{9,11},{10,... | collective-permute-start | bytes 1775624 | tf_op jit(solution)/shard_map/ppermute | solution.py:92
  647.8 1.5 collective-permute-start.36
  649.4 10.9 %collective-permute-start.37 = (f32[10880]{0:T(1024)S(1)}, f32[10880]{0:T(1024)S(1)}, u32[]{:S(2)}, u32[]{:S(2)}) collective-permute-start(f32[10880]{0:T(1024)S(1)} %add.955), channel_id=1, source_target_pairs={{0,8},{8,0},{16,24},{24,16},{1,9},{9,1},{17,25},{25,17},{2,10},{10... | collective-permute-start | bytes 130568 | tf_op jit(solution)/shard_map/ppermute | solution.py:124
  652.0 93.8 %collective-permute-start.52 = (bf16[136,272]{1,0:T(8,128)(2,1)}, bf16[136,272]{1,0:T(8,128)(2,1)}, u32[]{:S(2)}, u32[]{:S(2)}) collective-permute-start(bf16[136,272]{1,0:T(8,128)(2,1)} %fusion.81), channel_id=1, source_target_pairs={{0,4},{4,0},{1,5},{5,1},{2,6},{6,2},{3,7},{7,3},{8,12},{12,8},{9,1... | collective-permute-start | bytes 221960 | tf_op jit(solution)/shard_map/ppermute | solution.py:52
  660.3 83.3 %collective-permute-start.38 = (f32[10880]{0:T(1024)S(1)}, f32[10880]{0:T(1024)S(1)}, u32[]{:S(2)}, u32[]{:S(2)}) collective-permute-start(f32[10880]{0:T(1024)S(1)} %add.956), channel_id=1, source_target_pairs={{0,16},{8,24},{16,0},{24,8},{1,17},{9,25},{17,1},{25,9},{2,18},{10... | collective-permute-start | bytes 130568 | tf_op jit(solution)/shard_map/ppermute | solution.py:124
  719.6 60.8 %all-to-all-start.5 = ((bf16[4,192,1088]{2,1,0:T(8,128)(2,1)}), bf16[4,192,1088]{2,1,0:T(8,128)(2,1)}, u32[]{:S(2)}, u32[]{:S(2)}) async-start(bf16[4,192,1088]{2,1,0:T(8,128)(2,1)} %bitcast.80), calls=%async_computation.5 | async-start | bytes 3538944 | tf_op jit(solution)/shard_map/all_to_all | solution.py:43
  731.9 39.1 %collective-permute-start.41 = (bf16[2,2,136,960]{3,2,1,0:T(8,128)(2,1)}, bf16[2,2,136,960]{3,2,1,0:T(8,128)(2,1)}, u32[]{:S(2)}, u32[]{:S(2)}) collective-permute-start(bf16[2,2,136,960]{3,2,1,0:T(8,128)(2,1)} %fusion.64), channel_id=1, source_target_pairs={{0,4},{4,0},{1,5},{5,1},{2,6},{6,2},{3,7},{7,3},{8,12},{12,8},{9,1... | collective-permute-start | bytes 3133448 | tf_op jit(solution)/shard_map/ppermute | solution.py:52
  743.2 102.6 %collective-permute-start.18 = (bf16[384,1088]{0,1:T(8,128)(2,1)}, bf16[384,1088]{0,1:T(8,128)(2,1)}, u32[]{:S(2)}, u32[]{:S(2)}) collective-permute-start(bf16[384,1088]{0,1:T(8,128)(2,1)} %slice.414), channel_id=1, source_target_pairs={{0,4},{4,0},{1,5},{5,1},{2,6},{6,2},{3,7},{7,3},{8,12},{12,8},{9,1... | collective-permute-start | bytes 2506760 | tf_op jit(solution)/shard_map/ppermute | solution.py:52
  743.7 10.6 %collective-permute-start.39 = (f32[10880]{0:T(1024)S(1)}, f32[10880]{0:T(1024)S(1)}, u32[]{:S(2)}, u32[]{:S(2)}) collective-permute-start(f32[10880]{0:T(1024)S(1)} %add.957), channel_id=1, source_target_pairs={{0,1},{1,0},{2,3},{3,2},{4,5},{5,4},{6,7},{7,6},{8,9},{9,8},{10,11... | collective-permute-start | bytes 130568 | tf_op jit(solution)/shard_map/ppermute | solution.py:124
  754.3 13.5 %collective-permute-start.40 = (f32[10880]{0:T(1024)S(1)}, f32[10880]{0:T(1024)S(1)}, u32[]{:S(2)}, u32[]{:S(2)}) collective-permute-start(f32[10880]{0:T(1024)S(1)} %add.958), channel_id=1, source_target_pairs={{0,2},{1,3},{2,0},{3,1},{4,6},{5,7},{6,4},{7,5},{8,10},{9,11},{10,... | collective-permute-start | bytes 130568 | tf_op jit(solution)/shard_map/ppermute | solution.py:124
  759.7 24.3 %collective-permute-start.53 = (bf16[2,136,544]{2,1,0:T(8,128)(2,1)}, bf16[2,136,544]{2,1,0:T(8,128)(2,1)}, u32[]{:S(2)}, u32[]{:S(2)}) collective-permute-start(bf16[2,136,544]{2,1,0:T(8,128)(2,1)} %dynamic-slice_bitcast_fusion.9), channel_id=1, source_target_pairs={{0,4},{4,0},{1,5},{5,1},{2,6},{6,2},{3,7},{7,3},{8,12},{12,8},{9,1... | collective-permute-start | bytes 887816 | tf_op jit(solution)/shard_map/ppermute | solution.py:52
  773.6 14.2 %collective-permute-start.42 = (bf16[2,136,960]{2,1,0:T(8,128)(2,1)}, bf16[2,136,960]{2,1,0:T(8,128)(2,1)}, u32[]{:S(2)}, u32[]{:S(2)}) collective-permute-start(bf16[2,136,960]{2,1,0:T(8,128)(2,1)} %dynamic-slice_bitcast_fusion.8), channel_id=1, source_target_pairs={{0,8},{8,0},{16,24},{24,16},{1,9},{9,1},{17,25},{25,17},{2,10},{10... | collective-permute-start | bytes 1566728 | tf_op jit(solution)/shard_map/ppermute | solution.py:71
  780.4 48.7 %all-to-all-start.4 = ((bf16[4,192,1088]{2,1,0:T(8,128)(2,1)}), bf16[4,192,1088]{2,1,0:T(8,128)(2,1)S(1)}, u32[]{:S(2)}, u32[]{:S(2)}) async-start(bf16[4,192,1088]{2,1,0:T(8,128)(2,1)} %bitcast.77), calls=%async_computation.4 | async-start | bytes 3538944 | tf_op jit(solution)/shard_map/all_to_all | solution.py:43
  789.1 7.0 collective-permute-start.43
  798.0 25.7 %collective-permute-start.46 = (bf16[3,64,136]{1,2,0:T(8,128)(2,1)S(1)}, bf16[3,64,136]{1,2,0:T(8,128)(2,1)}, u32[]{:S(2)}, u32[]{:S(2)}) collective-permute-start(bf16[3,64,136]{1,2,0:T(8,128)(2,1)S(1)} %copy.400), channel_id=1, source_target_pairs={{2,3},{6,7},{10,11},{14,15},{18,19},{22,23},{26,27},{30,31}} | collective-permute-start | bytes 156680 | tf_op jit(solution)/shard_map/ppermute | solution.py:811
  799.3 24.4 %collective-permute-start.45 = (bf16[3,64,136]{1,2,0:T(8,128)(2,1)S(1)}, bf16[3,64,136]{1,2,0:T(8,128)(2,1)}, u32[]{:S(2)}, u32[]{:S(2)}) collective-permute-start(bf16[3,64,136]{1,2,0:T(8,128)(2,1)S(1)} %copy.400), channel_id=1, source_target_pairs={{1,3},{5,7},{9,11},{13,15},{17,19},{21,23},{25,27},{29,31}} | collective-permute-start | bytes 156680 | tf_op jit(solution)/shard_map/ppermute | solution.py:811
  800.6 23.1 %collective-permute-start.44 = (bf16[3,64,136]{1,2,0:T(8,128)(2,1)S(1)}, bf16[3,64,136]{1,2,0:T(8,128)(2,1)}, u32[]{:S(2)}, u32[]{:S(2)}) collective-permute-start(bf16[3,64,136]{1,2,0:T(8,128)(2,1)S(1)} %copy.400), channel_id=1, source_target_pairs={{0,3},{4,7},{8,11},{12,15},{16,19},{20,23},{24,27},{28,31}} | collective-permute-start | bytes 156680 | tf_op jit(solution)/shard_map/ppermute | solution.py:811
  810.6 13.1 %collective-permute-start.47 = (bf16[3,48,136]{1,2,0:T(8,128)(2,1)S(1)}, bf16[3,48,136]{1,2,0:T(8,128)(2,1)S(1)}, u32[]{:S(2)}, u32[]{:S(2)}) collective-permute-start(bf16[3,48,136]{1,2,0:T(8,128)(2,1)S(1)} %slice.346), channel_id=1, source_target_pairs={{1,0},{2,1},{3,2},{5,4},{6,5},{7,6},{9,8},{10,9},{11,10},{13,12},{... | collective-permute-start | bytes 117512 | tf_op jit(solution)/shard_map/ppermute | solution.py:483
  837.4 18.9 %all-to-all-start.6 = ((f32[32,2,1088]{2,1,0:T(2,128)}), f32[32,2,1088]{2,1,0:T(2,128)}, u32[]{:S(2)}, u32[]{:S(2)}) async-start(f32[32,2,1088]{2,1,0:T(2,128)} %broadcast_in_dim.156), calls=%async_computation.6 | async-start | bytes 589824 | tf_op jit(solution)/shard_map/all_to_all | solution.py:58
  (92 other events, 1127.4 us)
Sparse Core Ops, SparseCore 0:
  98.7 225.4 all-gather.1
